TPU v7x, 32 devices: a whole 2x2x4 slice. The times are simulated.
32 devices in a mesh: groups: 2 (over x), dp: 16 (over z, y, core).
Axes of the slice: x: 2, y: 2, z: 4, core: 2. Of those that a mesh axis runs over, the one named last changes fastest.
Arguments:
- tiles: bfloat16 [1024, 64, 3072], P(('groups', 'dp')), parts along dimension 0, may hold values from -6 to 6
- conv_weight: bfloat16 [3072, 768], P('dp'), may hold values from -0.109375 to 0.109375
- tile_slide: int32 [1024], P(('groups', 'dp')), parts along dimension 0, may hold values from 0 to 31, as said below
- slide_owner: int32 [64], P('groups'), parts along dimension 0, may hold values from 0 to 15, as said below
- labels: int32 [64], P('groups'), parts along dimension 0, may hold values from 0 to 1
- attn_v: bfloat16 [768, 384], replicated, may hold values from -0.21875 to 0.21875
- attn_u: bfloat16 [768, 384], replicated, may hold values from -0.21875 to 0.21875
- attn_w: float32 [384], replicated, may hold values from -0.5 to 0.5
- class_w: float32 [768, 2], replicated, may hold values from -0.6 to 0.6
Outputs:
- conv_grad: float32 [6144, 768], P(('groups', 'dp')), parts along dimension 0
- attn_v_grad: float32 [1536, 384], P(('groups', 'dp')), parts along dimension 0
- attn_u_grad: float32 [1536, 384], P(('groups', 'dp')), parts along dimension 0
- attn_w_grad: float32 [768], P('groups'), parts along dimension 0
- class_grad: float32 [1536, 2], P('groups'), parts along dimension 0
- slide_logits: float32 [64, 2], P(('groups', 'dp')), parts along dimension 0
- loss: float32 [2], P('groups'), parts along dimension 0
There are 2 independent parts, one for each index of `groups`. A program takes and returns all parts, laid end to end along the dimension named above; an argument that names none is the same for every part. Nothing has to cross between parts.
Inputs may be any that keep to these rules, and one draw needn't show every extreme that they name: `tile_slide`: the 32 tiles of one index of dp include at most 4 tiles of the slides of any one owner; some owner gets exactly 4 from every index of dp; every slide has at least one tile. `slide_owner`: every owner holds exactly 2 slides.
All inputs are finite; a program needn't handle non-finite values.
Results may differ from a plain program's by a relative error of at most 0.0094.
Values may be sent and summed in bfloat16 or wider, within the bound.
No kernel may reach another device: no remote copies, remote signals or barrier semaphores. Data moves between devices by JAX's collectives and lax.ppermute only.
A program may use at most 128 MiB of HBM per device.

v0:
```python
import jax
import jax.numpy as jnp
from jax import lax
from jax.sharding import PartitionSpec as P

CAP = 4
SLIDES_DEV = 2


norm_eps = 1e-05


def encode(pre_act):
    pooled = jnp.mean(jnp.maximum(pre_act, 0.0), axis=1)
    centred = pooled - jnp.mean(pooled, axis=-1, keepdims=True)
    spread = jnp.mean(centred * centred, axis=-1, keepdims=True)
    return centred * lax.rsqrt(spread + norm_eps)


def head(embedded, member, picked, attn_v, attn_u, attn_w, class_w, slide_count):
    highest = lax.Precision.HIGHEST
    contract = (((0,), (0,)), ((), ()))
    act_a = jnp.tanh(jnp.dot(embedded, attn_v, preferred_element_type=jnp.float32))
    act_g = jax.nn.sigmoid(jnp.dot(embedded, attn_u, preferred_element_type=jnp.float32))
    gated_act = act_a * act_g
    tile_score = jnp.dot(gated_act, attn_w, precision=highest)
    live_rows = jnp.sum(member, axis=1)
    exp_score = jnp.exp(tile_score) * live_rows
    slide_total = jnp.dot(exp_score, member, precision=highest)
    weight = exp_score * jnp.dot(member, 1.0 / slide_total, precision=highest)
    pool_weight = (member * weight[:, None]).astype(jnp.bfloat16)
    slide_emb = lax.dot_general(pool_weight, embedded, contract, preferred_element_type=jnp.float32)
    logits = jnp.dot(slide_emb, class_w, precision=highest)
    exp_logits = jnp.exp(logits)
    class_sum = jnp.sum(exp_logits, axis=1)
    onehot = (picked[:, None] == jnp.arange(class_w.shape[1])[None, :]).astype(jnp.float32)
    loss_sum = jnp.sum(jnp.log(class_sum) - jnp.sum(logits * onehot, axis=1)) / slide_count
    d_logits = (exp_logits / class_sum[:, None] - onehot) / slide_count
    d_class = lax.dot_general(slide_emb, d_logits, contract, precision=highest)
    d_slide = jnp.dot(d_logits, class_w.T, precision=highest)
    d_rows = jnp.dot(member, d_slide, precision=highest)
    d_weight = jnp.sum(embedded.astype(jnp.float32) * d_rows, axis=1)
    centre = jnp.dot(
        member, jnp.dot(weight * d_weight, member, precision=highest), precision=highest
    )
    d_score = weight * (d_weight - centre)
    attn_w_grad = jnp.dot(d_score, gated_act, precision=highest)
    d_gated = d_score[:, None] * attn_w[None, :]
    d_pre_a = (d_gated * act_g * (1.0 - act_a * act_a)).astype(jnp.bfloat16)
    d_pre_g = (d_gated * act_a * act_g * (1.0 - act_g)).astype(jnp.bfloat16)
    attn_v_grad = lax.dot_general(embedded, d_pre_a, contract, preferred_element_type=jnp.float32)
    attn_u_grad = lax.dot_general(embedded, d_pre_g, contract, preferred_element_type=jnp.float32)
    kept_weight = jnp.sum(pool_weight.astype(jnp.float32), axis=1)
    d_embedded = kept_weight[:, None] * d_rows
    d_embedded = d_embedded + jnp.dot(d_pre_a, attn_v.T, preferred_element_type=jnp.float32)
    d_embedded = d_embedded + jnp.dot(d_pre_g, attn_u.T, preferred_element_type=jnp.float32)
    return (logits, loss_sum, d_embedded, attn_v_grad, attn_u_grad, attn_w_grad, d_class)


def per_device(
    tiles, conv_weight, tile_slide, slide_owner, labels, attn_v, attn_u, attn_w, class_w
):
    tile_count, positions, inputs = tiles.shape
    channels = conv_weight.shape[1]
    slide_total_count = slide_owner.shape[0]
    devices = lax.axis_size("dp")
    my_index = lax.axis_index("dp")
    tile_rows = tiles.reshape(tile_count * positions, inputs)
    pre_act = jnp.dot(
        tile_rows,
        lax.all_gather(conv_weight, "dp", axis=0, tiled=True),
        preferred_element_type=jnp.float32,
    )
    embedded, back_fn = jax.vjp(encode, pre_act.reshape(tile_count, positions, channels))
    embedded = embedded.astype(jnp.bfloat16)
    slide_ids = jnp.arange(slide_total_count)
    my_slides = jnp.argsort(
        jnp.where(slide_owner == my_index, 0, 1) * slide_total_count + slide_ids, stable=True
    )[:SLIDES_DEV]
    picked = jnp.sum(labels[None, :] * (my_slides[:, None] == slide_ids[None, :]), axis=1)
    slide_match = (tile_slide[:, None] == slide_ids[None, :]).astype(jnp.int32)
    owner_tile = jnp.sum(slide_match * slide_owner[None, :], axis=1)
    dest = (owner_tile[:, None] == jnp.arange(devices)[None, :]).astype(jnp.int32)
    before = jnp.cumsum(dest, axis=0) - dest
    rank_tile = jnp.sum(before * dest, axis=1)
    slot_of = owner_tile * CAP + rank_tile
    send_emb = jnp.zeros((devices * CAP, channels), jnp.bfloat16).at[slot_of].set(embedded)
    send_ids = jnp.full((devices * CAP,), -1, jnp.int32).at[slot_of].set(tile_slide)
    recv_emb, recv_ids = (
        lax.all_to_all(
            send_emb.reshape(devices, CAP, channels), "dp", split_axis=0, concat_axis=0, tiled=True
        ),
        lax.all_to_all(
            send_ids.reshape(devices, CAP), "dp", split_axis=0, concat_axis=0, tiled=True
        ),
    )
    recv_emb = recv_emb.reshape(devices * CAP, channels)
    recv_ids = recv_ids.reshape(devices * CAP)
    member = (recv_ids[:, None] == my_slides[None, :]).astype(jnp.float32)
    logits, loss_sum, d_embedded, v_grad, u_grad, w_grad, c_grad = head(
        recv_emb, member, picked, attn_v, attn_u, attn_w, class_w, slide_total_count
    )
    send_back = d_embedded.astype(jnp.bfloat16).reshape(devices, CAP, channels)
    returned = lax.all_to_all(send_back, "dp", split_axis=0, concat_axis=0, tiled=True).reshape(
        devices * CAP, channels
    )
    tile_grad = returned[slot_of].astype(jnp.float32)
    d_pre = back_fn(tile_grad)[0].astype(jnp.bfloat16).reshape(tile_count * positions, channels)
    contract = (((0,), (0,)), ((), ()))
    full_term = lax.dot_general(tile_rows, d_pre, contract, preferred_element_type=jnp.float32)
    conv_grad = lax.psum_scatter(full_term, "dp", scatter_dimension=0, tiled=True)
    v_share, u_share = (
        lax.psum_scatter(v_grad, "dp", scatter_dimension=0, tiled=True),
        lax.psum_scatter(u_grad, "dp", scatter_dimension=0, tiled=True),
    )
    w_total, c_total, loss_total = lax.psum((w_grad, c_grad, loss_sum.reshape(1)), "dp")
    return (conv_grad, v_share, u_share, w_total, c_total, logits, loss_total)


def solution(mesh):
    in_specs = (
        P(("groups", "dp"), None, None),
        P("dp", None),
        P(("groups", "dp")),
        P("groups"),
        P("groups"),
        P(),
        P(),
        P(),
        P(),
    )
    out_specs = (
        P(("groups", "dp"), None),
        P(("groups", "dp"), None),
        P(("groups", "dp"), None),
        P("groups"),
        P("groups", None),
        P(("groups", "dp"), None),
        P("groups"),
    )
    return jax.shard_map(
        per_device, mesh=mesh, in_specs=in_specs, out_specs=out_specs, check_vma=False
    )
```

profile of v0, /device:TPU:0, one launch (start us, length us, event | category | flops | bytes accessed | tf_op | source)
XLA Modules:
  0.0 337.3 jit_solution(16990421243675920430)
XLA Ops:
  7.2 0.7 all-gather.2.cloned.1.call-update
  7.9 0.9 select_reduce_fusion.1
  9.1 0.8 scatter_custom_fusion
  9.9 0.7 all_to_all.12
  10.6 7.4 %all-to-all-start = ((s32[16,1,4]{2,1,0:T(1,128)}), s32[16,1,4]{2,1,0:T(1,128)S(1)}, u32[]{:S(2)}, u32[]{:S(2)}) async-start(s32[16,1,4]{2,1,0:T(1,128)} %bitcast.2), calls=%async_computation | async-start | bytes 16384 | tf_op jit(solution)/shard_map/all_to_all | solution.py:93
  18.0 0.7 reshape.132
  19.3 1.6 sort.17
  21.0 45.5 %all-gather.2.cloned.1.call-done = bf16[3072,768]{1,0:T(8,128)(2,1)} async-done(((bf16[192,768]{1,0:T(8,128)(2,1)}), bf16[3072,768]{1,0:T(8,128)(2,1)}) %all-gather.2.cloned.1.call-update) | async-done | bytes 4718608 | tf_op jit(solution)/shard_map/all_gather | solution.py:71
  66.4 14.9 %convert_reduce_fusion.1 = (u32[64,768]{1,0:T(8,128)S(1)}, u32[64,768]{1,0:T(8,128)S(1)}, f32[32,64,768]{2,1,0:T(8,128)S(1)}) fusion(bf16[32,64,3072]{2,1,0:T(8,128)(2,1)} %param.9, bf16[3072,768]{1,0:T(8,128)(2,1)} %all-gather.2.cloned.1.call-done), kind=kOutput, calls=%fused_computation.7 | convolution fusion | flops 9676161024 | bytes 23986176 | tf_op jit(solution)/shard_map/dot_general | solution.py:69
  81.4 0.7 maximum_reduce_fusion
  82.4 0.8 scatter_custom_fusion.1
  83.9 3.5 %all-to-all-start.1 = ((bf16[16,4,768]{2,1,0:T(4,128)(2,1)}), bf16[16,4,768]{2,1,0:T(4,128)(2,1)S(1)}, u32[]{:S(2)}, u32[]{:S(2)}) async-start(bf16[16,4,768]{2,1,0:T(4,128)(2,1)} %reshape.102), calls=%async_computation.1 | async-start | bytes 196608 | tf_op jit(solution)/shard_map/all_to_all | solution.py:90
  88.2 0.7 reduce.9
  89.0 5.8 %all-to-all-done.1 = bf16[16,4,768]{2,1,0:T(4,128)(2,1)S(1)} async-done(((bf16[16,4,768]{2,1,0:T(4,128)(2,1)}), bf16[16,4,768]{2,1,0:T(4,128)(2,1)S(1)}, u32[]{:S(2)}, u32[]{:S(2)}) %all-to-all-start.1) | async-done | bytes 98336 | tf_op jit(solution)/shard_map/all_to_all | solution.py:90
  97.6 1.4 fusion.70
  99.6 0.7 reshape.104
  100.3 3.5 %all-to-all-start.2 = ((bf16[16,4,768]{2,1,0:T(4,128)(2,1)}), bf16[16,4,768]{2,1,0:T(4,128)(2,1)S(1)}, u32[]{:S(2)}, u32[]{:S(2)}) async-start(bf16[16,4,768]{2,1,0:T(4,128)(2,1)} %reshape.104), calls=%async_computation.2 | async-start | bytes 196608 | tf_op jit(solution)/shard_map/all_to_all | solution.py:104
  103.9 1.4 fusion.69
  105.5 5.7 %all-to-all-done.2 = bf16[16,4,768]{2,1,0:T(4,128)(2,1)S(1)} async-done(((bf16[16,4,768]{2,1,0:T(4,128)(2,1)}), bf16[16,4,768]{2,1,0:T(4,128)(2,1)S(1)}, u32[]{:S(2)}, u32[]{:S(2)}) %all-to-all-start.2) | async-done | bytes 98336 | tf_op jit(solution)/shard_map/all_to_all | solution.py:104
  112.4 15.5 %convolution_bitcast_fusion = f32[3072,768]{0,1:T(8,128)} fusion(bf16[32,64,3072]{2,1,0:T(8,128)(2,1)} %param.9, u32[64,768]{1,0:T(8,128)S(1)} %get-tuple-element.38, u32[64,768]{1,0:T(8,128)S(1)} %get-tuple-element.37, f32[32,768]{1,0:T(8,128)S(1)} %add_multiply_fusion), kind=kOutput, calls=%fused_computation.10 | convolution fusion | flops 9677832192 | bytes 22511616 | tf_op jit(solution)/shard_map/dot_general | solution.py:110
  127.9 9.7 %copy.26 = f32[3072,768]{1,0:T(8,128)} copy(f32[3072,768]{0,1:T(8,128)} %convolution_bitcast_fusion) | data formatting | bytes 18874368
  139.8 32.1 %all-reduce = (f32[384]{0:T(512)}, f32[768,2]{0,1:T(2,128)}, f32[1]{0:T(128)}) all-reduce(f32[384]{0:T(512)S(1)} %convolution_reduce_fusion, f32[768,2]{0,1:T(2,128)S(1)} %fusion.71, f32[1]{0:T(128)} %bitcast.16), channel_id=1, replica_groups=mesh['groups'=2,'dp'=16] {'dp'}, use_global_device_ids=true, to_apply=%region_19.20 | all-reduce | flops 1921 | bytes 15368 | tf_op jit(solution)/shard_map/psum | solution.py:116
  172.0 43.9 %reduce-scatter.6.cloned.1.call-done = f32[48,384]{1,0:T(8,128)} async-done(((f32[768,384]{1,0:T(8,128)}), f32[48,384]{1,0:T(8,128)}) %reduce-scatter.6.cloned.1.call-update) | async-done | bytes 73744 | tf_op jit(solution)/shard_map/reduce_scatter | solution.py:113
  215.9 114.9 %reduce-scatter.10.cloned.1.call-done = f32[192,768]{1,0:T(8,128)} async-done(((f32[3072,768]{1,0:T(8,128)}), f32[192,768]{1,0:T(8,128)}) %reduce-scatter.10.cloned.1.call-update) | async-done | bytes 589840
  (63 shorter events, 9.4 us)
Async XLA Ops:
  7.2 87.9 %copy-start = (bf16[768,384]{1,0:T(8,128)(2,1)S(1)}, bf16[768,384]{1,0:T(8,128)(2,1)}, u32[]{:S(2)}) copy-start(bf16[768,384]{1,0:T(8,128)(2,1)} %param.14) | copy-start | bytes 1769476
  7.2 59.2 %all-gather.2.cloned.1.call-start = ((), (), s32[]{:S(2)}) async-start(), calls=%async_computation.6 | async-start | bytes 5013504 | tf_op jit(solution)/shard_map/all_gather | solution.py:71
  10.6 73.3 %all-to-all-start = ((s32[16,1,4]{2,1,0:T(1,128)}), s32[16,1,4]{2,1,0:T(1,128)S(1)}, u32[]{:S(2)}, u32[]{:S(2)}) async-start(s32[16,1,4]{2,1,0:T(1,128)} %bitcast.2), calls=%async_computation | async-start | bytes 16384 | tf_op jit(solution)/shard_map/all_to_all | solution.py:93
  81.3 6.2 %copy-start.4 = (s32[32]{0:T(128)S(1)}, s32[32]{0:T(128)}, u32[]{:S(2)}) copy-start(s32[32]{0:T(128)} %param.13) | copy-start | bytes 388
  81.3 13.5 %copy-start.1 = (bf16[768,384]{1,0:T(8,128)(2,1)S(1)}, bf16[768,384]{1,0:T(8,128)(2,1)}, u32[]{:S(2)}) copy-start(bf16[768,384]{1,0:T(8,128)(2,1)} %param.15) | copy-start | bytes 1769476
  81.3 14.8 %copy-start.3 = (f32[768,2]{0,1:T(2,128)S(1)}, f32[768,2]{0,1:T(2,128)}, u32[]{:S(2)}) copy-start(f32[768,2]{0,1:T(2,128)} %param.17) | copy-start | bytes 18436
  81.3 16.1 %copy-start.2 = (f32[384]{0:T(512)S(1)}, f32[384]{0:T(512)}, u32[]{:S(2)}) copy-start(f32[384]{0:T(512)} %param.16) | copy-start | bytes 4612
  83.9 10.9 %all-to-all-start.1 = ((bf16[16,4,768]{2,1,0:T(4,128)(2,1)}), bf16[16,4,768]{2,1,0:T(4,128)(2,1)S(1)}, u32[]{:S(2)}, u32[]{:S(2)}) async-start(bf16[16,4,768]{2,1,0:T(4,128)(2,1)} %reshape.102), calls=%async_computation.1 | async-start | bytes 196608 | tf_op jit(solution)/shard_map/all_to_all | solution.py:90
  87.4 84.5 %reduce-scatter.8.cloned.1.call-start = ((), (), s32[]{:S(2)}) async-start(), calls=%async_computation.8 | async-start | bytes 1253376 | tf_op jit(solution)/shard_map/reduce_scatter | solution.py:114
  100.3 10.9 %all-to-all-start.2 = ((bf16[16,4,768]{2,1,0:T(4,128)(2,1)}), bf16[16,4,768]{2,1,0:T(4,128)(2,1)S(1)}, u32[]{:S(2)}, u32[]{:S(2)}) async-start(bf16[16,4,768]{2,1,0:T(4,128)(2,1)} %reshape.104), calls=%async_computation.2 | async-start | bytes 196608 | tf_op jit(solution)/shard_map/all_to_all | solution.py:104
  103.8 112.1 %reduce-scatter.6.cloned.1.call-start = ((), (), s32[]{:S(2)}) async-start(), calls=%async_computation.7 | async-start | bytes 1253376 | tf_op jit(solution)/shard_map/reduce_scatter | solution.py:113
  105.3 225.5 %reduce-scatter.10.cloned.1.call-start = ((), (), s32[]{:S(2)}) async-start(), calls=%async_computation.9 | async-start | bytes 10027008
Sparse Core Ops, SparseCore 0:
  10.3 56.0 all-gather.1
  99.1 55.5 reduce-scatter.7
  158.8 56.9 reduce-scatter.5
  220.4 110.3 reduce-scatter.9
where the time goes:
time: 338 us; the launch traced here: 337 us
  waiting for transfers between devices  216 us (64%)
  matrix products  36.6 us (11%)
  blocking collectives  32.1 us (9%)
  local copies, waits for them, and re-layouts  15.2 us (4%)
  starting transfers between devices  14.7 us (4%)
  between operations  14.7 us (4%)
  other arithmetic  7.56 us (2%)
    unnamed x5, waiting for transfers between devices  116 us
    all_gather x1, waiting for transfers between devices, per_device(): lax.all_gather(conv_weight, 'dp', axis=0, tiled=True)  45.5 us
    reduce_scatter x1, waiting for transfers between devices, per_device(): lax.psum_scatter(v_grad, 'dp', scatter_dimension=0, tiled=True)  43.9 us
    psum x1, blocking collectives, per_device(): lax.psum((w_grad, c_grad, loss_sum.reshape(1)), 'dp')  32.1 us
    dot_general x1, matrix products, per_device(): lax.dot_general(tile_rows, d_pre, contract, preferred_element_type=jnp.fl...  15.5 us
    dot_general x1, matrix products, per_device(): jnp.dot(tile_rows, lax.all_gather(conv_weight, 'dp', axis=0, tiled=True),...  14.9 us
    unnamed x13, local copies, waits for them, and re-layouts  11 us
    all_to_all x1, starting transfers between devices, per_device(): lax.all_to_all(send_ids.reshape(devices, CAP), 'dp', split_axis=0, concat...  7.39 us
  transfers between devices with their start and end apart: 7, of which 5 were waited for; matrix products, arithmetic and copies ran while one was open for 16% of the time, Pallas kernels for 0%

commit v1 on v0

v1 whole, which is shorter than its diff:
```python
import functools

import jax
import jax.numpy as jnp
from jax import lax
from jax.experimental import pallas as pl
from jax.experimental.pallas import tpu as pltpu
from jax.sharding import PartitionSpec as P

norm_eps = 1e-05
F32 = jnp.float32
BF16 = jnp.bfloat16
LANES = 128
VMEM_LIMIT = 48 * 1024 * 1024


def whole(shape):
    return pl.BlockSpec(shape, lambda *_: (0,) * len(shape))


def forward_kernel(pieces, first, last, positions, where, tiles, *refs):
    ws = refs[:pieces]
    rest = refs[pieces:]
    acc = None
    if not first:
        acc, rest = rest[0], rest[1:]
    if last:
        mask_out, pooled_out, weight = rest
    else:
        acc_out, weight = rest
    share = ws[0].shape[0]

    @pl.when(pl.program_id(0) == 0)
    def _():
        for i in range(pieces):
            start = pl.multiple_of(where[1 + i] * share, share)
            weight[pl.ds(start, share), :] = ws[i][...]

    total = jnp.dot(tiles[...], weight[...], preferred_element_type=F32)
    if not first:
        total = total + acc[...]
    if not last:
        acc_out[...] = total
        return
    mask_out[...] = jnp.where(total > 0, 1.0, jnp.where(total == 0, 0.5, 0.0)).astype(BF16)
    rows, channels = total.shape
    count = rows // positions
    active = jnp.maximum(total, 0.0).reshape(count, positions, channels)
    pooled_out[...] = jnp.sum(active, axis=1) * (1.0 / positions)


def forward_chunk(where, tile_rows, ws, acc, last, positions):
    rows, inputs = tile_rows.shape
    share, channels = ws[0].shape
    pieces = len(ws)
    depth = share * pieces
    block = min(rows, 8 * positions)
    first = acc is None
    tiled = pl.BlockSpec((block, channels), lambda i, w: (i, 0))
    in_specs = [pl.BlockSpec((block, depth), lambda i, w: (i, w[0]))]
    in_specs += [whole((share, channels))] * pieces
    operands = [tile_rows, *ws]
    if not first:
        in_specs.append(tiled)
        operands.append(acc)
    if last:
        out_specs = [tiled, pl.BlockSpec((block // positions, channels), lambda i, w: (i, 0))]
        out_shape = [
            jax.ShapeDtypeStruct((rows, channels), BF16),
            jax.ShapeDtypeStruct((rows // positions, channels), F32),
        ]
    else:
        out_specs = [tiled]
        out_shape = [jax.ShapeDtypeStruct((rows, channels), F32)]
    return pl.pallas_call(
        functools.partial(forward_kernel, pieces, first, last, positions),
        grid_spec=pltpu.PrefetchScalarGridSpec(
            num_scalar_prefetch=1,
            grid=(rows // block,),
            in_specs=in_specs,
            out_specs=out_specs,
            scratch_shapes=[pltpu.VMEM((depth, channels), BF16)],
        ),
        out_shape=out_shape,
        compiler_params=pltpu.CompilerParams(vmem_limit_bytes=VMEM_LIMIT),
        cost_estimate=pl.CostEstimate(
            flops=2 * rows * depth * channels,
            bytes_accessed=2 * rows * depth + 8 * rows * channels,
            transcendentals=0,
        ),
        name="section_forward",
    )(where, *operands)


def member_of(tile_slide, lanes):
    slide = lax.broadcasted_iota(jnp.int32, (tile_slide.shape[0], lanes), 1)
    return (tile_slide == slide).astype(F32)


def normal(pooled):
    centred = pooled - jnp.mean(pooled, axis=-1, keepdims=True)
    spread = jnp.mean(centred * centred, axis=-1, keepdims=True)
    scale = lax.rsqrt(spread + norm_eps)
    return centred * scale, scale


def score_kernel(
    pooled, slide, attn_v, attn_u, attn_w, class_t, emb_out, gated_out, ua_out, ug_out, back_out, stat_out, packet_out
):
    unit, _ = normal(pooled[...])
    emb = unit.astype(BF16)
    emb_out[...] = emb
    act_a = jnp.tanh(jnp.dot(emb, attn_v[...], preferred_element_type=F32))
    act_g = jax.nn.sigmoid(jnp.dot(emb, attn_u[...], preferred_element_type=F32))
    gated = act_a * act_g
    gated_out[...] = gated
    exp_score = jnp.exp(jnp.sum(gated * attn_w[...], axis=1, keepdims=True))
    emb32 = emb.astype(F32)
    classes = class_t.shape[0]
    reads = [jnp.sum(emb32 * class_t[k : k + 1, :], axis=1, keepdims=True) for k in range(classes)]
    lanes = packet_out.shape[1]
    member = member_of(slide[...], lanes)
    total = jnp.sum(member * exp_score, axis=0, keepdims=True)
    own_total = jnp.sum(member * total, axis=1, keepdims=True)
    part = jnp.where(own_total > 0, exp_score / own_total, 0.0)
    packet_out[...] = jnp.zeros_like(packet_out)
    packet_out[0:1, :] = total
    for k in range(classes):
        packet_out[k + 1 : k + 2, :] = jnp.sum(member * (part * reads[k]), axis=0, keepdims=True)
    column = lax.broadcasted_iota(jnp.int32, stat_out.shape, 1)
    stats = jnp.where(column == 0, exp_score, 0.0)
    for k in range(classes):
        stats = jnp.where(column == k + 1, reads[k], stats)
    stat_out[...] = stats
    ua = (attn_w[...] * act_g * (1.0 - act_a * act_a)).astype(BF16)
    ug = (attn_w[...] * act_a * act_g * (1.0 - act_g)).astype(BF16)
    ua_out[...] = ua
    ug_out[...] = ug
    contract = (((1,), (1,)), ((), ()))
    back_out[...] = lax.dot_general(ua, attn_v[...], contract, preferred_element_type=F32) + lax.dot_general(
        ug, attn_u[...], contract, preferred_element_type=F32
    )


def score(pooled, slide, attn_v, attn_u, attn_w, class_t, lanes):
    tiles, channels = pooled.shape
    hidden = attn_v.shape[1]
    return pl.pallas_call(
        score_kernel,
        out_shape=[
            jax.ShapeDtypeStruct((tiles, channels), BF16),
            jax.ShapeDtypeStruct((tiles, hidden), F32),
            jax.ShapeDtypeStruct((tiles, hidden), BF16),
            jax.ShapeDtypeStruct((tiles, hidden), BF16),
            jax.ShapeDtypeStruct((tiles, channels), F32),
            jax.ShapeDtypeStruct((tiles, LANES), F32),
            jax.ShapeDtypeStruct((8, lanes), F32),
        ],
        compiler_params=pltpu.CompilerParams(vmem_limit_bytes=VMEM_LIMIT),
        name="tile_scores",
    )(pooled, slide, attn_v, attn_u, attn_w, class_t)


def merge(one, other):
    total = one[0:1] + other[0:1]
    safe = jnp.where(total > 0, total, 1.0)
    mean = one * (one[0:1] / safe) + other * (other[0:1] / safe)
    row = lax.broadcasted_iota(jnp.int32, one.shape, 0)
    return jnp.where(row == 0, total, mean)


def grads_kernel(
    packets,
    slides,
    shards,
    where,
    *refs,
):
    boxes = refs[:packets]
    (pooled, emb, gated, ua, ug, back, stat, slide, owner, label, class_t) = refs[packets : packets + 11]
    (scale_out, small_out, term_keep, term_send, logit_out, loss_out) = refs[packets + 11 :]
    packet = boxes[0][...]
    for box in boxes[1:]:
        packet = merge(packet, box[...])
    classes = class_t.shape[0]
    lanes = packet.shape[1]
    total = packet[0:1]
    live = lax.broadcasted_iota(jnp.int32, (1, lanes), 1) < slides
    logits = [jnp.where(live, packet[k + 1 : k + 2], 0.0) for k in range(classes)]
    exp_logits = [jnp.exp(v) for v in logits]
    class_sum = functools.reduce(jnp.add, exp_logits)
    hot = [jnp.where(label[...] == k, 1.0, 0.0) for k in range(classes)]
    picked = functools.reduce(jnp.add, [v * h for v, h in zip(logits, hot)])
    loss = jnp.where(live, jnp.log(class_sum) - picked, 0.0)
    loss_out[...] = jnp.broadcast_to(jnp.sum(loss, axis=1, keepdims=True) / slides, loss_out.shape)
    d_logits = [jnp.where(live, (e / class_sum - h) / slides, 0.0) for e, h in zip(exp_logits, hot)]
    centre = functools.reduce(jnp.add, [d * v for d, v in zip(d_logits, logits)])

    mine = jnp.where((owner[...] == where[0]) & live, 1.0, 0.0)
    up = lax.broadcasted_iota(jnp.int32, (lanes, lanes), 0)
    across = lax.broadcasted_iota(jnp.int32, (lanes, lanes), 1)
    rank = jnp.dot(
        jnp.broadcast_to(mine, (8, lanes)), jnp.where(up < across, 1.0, 0.0), preferred_element_type=F32
    )
    wanted = lax.broadcasted_iota(jnp.int32, (8, lanes), 0).astype(F32)
    chosen = jnp.where((rank == wanted) & (mine > 0), 1.0, 0.0)
    column = lax.broadcasted_iota(jnp.int32, (8, LANES), 1)
    rows = jnp.zeros((8, LANES), F32)
    for k in range(classes):
        rows = jnp.where(column == k, jnp.sum(chosen * logits[k], axis=1, keepdims=True), rows)
    logit_out[...] = rows

    member = member_of(slide[...], lanes)

    def of_tile(row):
        return jnp.sum(member * row, axis=1, keepdims=True)

    stats = stat[...]
    weight = stats[:, 0:1] / of_tile(total)
    d_tile = [of_tile(d) for d in d_logits]
    d_weight = functools.reduce(jnp.add, [d * stats[:, k + 1 : k + 2] for k, d in enumerate(d_tile)])
    d_score = weight * (d_weight - of_tile(centre))
    kept = weight.astype(BF16).astype(F32)
    d_rows = functools.reduce(jnp.add, [d * class_t[k : k + 1, :] for k, d in enumerate(d_tile)])
    d_emb = (kept * d_rows + d_score * back[...]).astype(BF16).astype(F32)
    unit, inv = normal(pooled[...])
    d_pool = inv * (
        d_emb
        - jnp.mean(d_emb, axis=-1, keepdims=True)
        - unit * jnp.mean(d_emb * unit, axis=-1, keepdims=True)
    )
    scale_out[...] = d_pool

    emb16 = emb[...]
    emb32 = emb16.astype(F32)
    small_out[...] = jnp.zeros_like(small_out)
    channels = emb16.shape[1]
    for k in range(classes):
        small_out[k : k + 1, :channels] = jnp.sum(emb32 * (kept * d_tile[k]), axis=0, keepdims=True)
    hidden = gated.shape[1]
    small_out[classes : classes + 1, :hidden] = jnp.sum(gated[...] * d_score, axis=0, keepdims=True)

    d_pre_a = (d_score * ua[...].astype(F32)).astype(BF16)
    d_pre_g = (d_score * ug[...].astype(F32)).astype(BF16)
    d_pre = jnp.concatenate([d_pre_a, d_pre_g], axis=1)
    term = lax.dot_general(emb16, d_pre, (((0,), (0,)), ((), ())), preferred_element_type=F32)
    if shards is None:
        term_keep[...] = term
        term_send[...] = jnp.zeros_like(term_send)
        return
    zs, ys, cs = shards
    share = channels // (zs * ys * cs)
    y, c = where[1], where[2]
    for iz in range(zs):
        for iy in range(ys):
            for ic in range(cs):
                at = ((iz * ys + iy) * cs + ic) * share
                block = term[at : at + share]

                @pl.when(c == ic)
                def _():
                    term_keep[y ^ iy, iz] = block

                @pl.when(c != ic)
                def _():
                    term_send[y ^ iy, iz] = block.astype(BF16)


def grads(where, boxes, local, slide, owner, label, class_t, slides, shards):
    pooled, emb, gated, ua, ug, back, stat = local
    tiles, channels = pooled.shape
    hidden = gated.shape[1]
    if shards is None:
        keep_shape, send_shape = (channels, 2 * hidden), (16, LANES)
    else:
        zs, ys, cs = shards
        keep_shape = send_shape = (ys, zs, channels // (zs * ys * cs), 2 * hidden)
    vmem = pl.BlockSpec(memory_space=pltpu.VMEM)
    return pl.pallas_call(
        functools.partial(grads_kernel, len(boxes), slides, shards),
        in_specs=[pl.BlockSpec(memory_space=pltpu.SMEM)] + [vmem] * (len(boxes) + 11),
        out_shape=[
            jax.ShapeDtypeStruct((tiles, channels), F32),
            jax.ShapeDtypeStruct((8, max(channels, hidden)), F32),
            jax.ShapeDtypeStruct(keep_shape, F32),
            jax.ShapeDtypeStruct(send_shape, BF16),
            jax.ShapeDtypeStruct((8, LANES), F32),
            jax.ShapeDtypeStruct((8, LANES), F32),
        ],
        compiler_params=pltpu.CompilerParams(vmem_limit_bytes=VMEM_LIMIT),
        name="head_grads",
    )(where, *boxes, pooled, emb, gated, ua, ug, back, stat, slide, owner, label, class_t)


def spread_kernel(positions, mask, scale, out):
    rows, channels = mask.shape
    count = rows // positions
    scaled = (scale[...] * (1.0 / positions)).astype(BF16)
    masks = mask[...].reshape(count, positions, channels)
    out[...] = (masks * scaled[:, None, :]).reshape(rows, channels)


def spread(mask, scale, positions):
    rows, channels = mask.shape
    block = min(rows, 8 * positions)
    tiled = pl.BlockSpec((block, channels), lambda i: (i, 0))
    return pl.pallas_call(
        functools.partial(spread_kernel, positions),
        grid=(rows // block,),
        in_specs=[tiled, pl.BlockSpec((block // positions, channels), lambda i: (i, 0))],
        out_specs=tiled,
        out_shape=jax.ShapeDtypeStruct((rows, channels), BF16),
        compiler_params=pltpu.CompilerParams(vmem_limit_bytes=VMEM_LIMIT),
        name="section_spread",
    )(mask, scale)


def backward_kernel(ys, cs, where, tiles, d_pre, keep, send):
    term = lax.dot_general(tiles[...], d_pre[...], (((0,), (0,)), ((), ())), preferred_element_type=F32)
    share = term.shape[0] // cs
    c = where[2]
    for ic in range(cs):
        block = term[ic * share : (ic + 1) * share]

        @pl.when(c == ic)
        def _():
            keep[0] = block

        @pl.when(c != ic)
        def _():
            send[0] = block.astype(BF16)


def backward_chunk(where, tile_rows, d_pre, ys, cs, share):
    rows, inputs = tile_rows.shape
    channels = d_pre.shape[1]
    width = cs * share
    out = pl.BlockSpec((1, share, channels), lambda i, w: (i ^ w[1], 0, 0))
    return pl.pallas_call(
        functools.partial(backward_kernel, ys, cs),
        grid_spec=pltpu.PrefetchScalarGridSpec(
            num_scalar_prefetch=1,
            grid=(ys,),
            in_specs=[
                pl.BlockSpec((rows, width), lambda i, w: (0, w[0] * ys + i)),
                whole((rows, channels)),
            ],
            out_specs=[out, out],
        ),
        out_shape=[
            jax.ShapeDtypeStruct((ys, share, channels), F32),
            jax.ShapeDtypeStruct((ys, share, channels), BF16),
        ],
        compiler_params=pltpu.CompilerParams(vmem_limit_bytes=VMEM_LIMIT),
        cost_estimate=pl.CostEstimate(
            flops=2 * rows * width * ys * channels,
            bytes_accessed=2 * rows * width * ys + 2 * rows * channels,
            transcendentals=0,
        ),
        name="section_backward",
    )(where, tile_rows, d_pre)


def grid_of(devices):
    return (4, 2, 2) if devices == 16 else None


def moves(shape):
    zs, ys, cs = shape

    def at(z, y, c):
        return (z * ys + y) * cs + c

    every = [(z, y, c) for z in range(zs) for y in range(ys) for c in range(cs)]
    core = [(at(*i), at(i[0], i[1], i[2] ^ 1)) for i in every]
    row = [(at(*i), at(i[0], i[1] ^ 1, i[2])) for i in every]

    def deep(step):
        return [(at(*i), at((i[0] + step) % zs, i[1], i[2])) for i in every]

    return core, row, deep


def send(x, pairs):
    return lax.ppermute(x, "dp", pairs)


def per_device(tiles, conv_weight, tile_slide, slide_owner, labels, attn_v, attn_u, attn_w, class_w):
    tile_count, positions, inputs = tiles.shape
    share, channels = conv_weight.shape
    hidden = attn_v.shape[1]
    classes = class_w.shape[1]
    slides = slide_owner.shape[0]
    devices = lax.axis_size("dp")
    me = lax.axis_index("dp")
    shape = grid_of(devices)
    rows = tile_count * positions
    tile_rows = tiles.reshape(rows, inputs)
    lanes = -(-slides // LANES) * LANES
    pad = lanes - slides
    slide = tile_slide[:, None]
    owner = jnp.pad(slide_owner, (0, pad), constant_values=-1)[None, :]
    label = jnp.pad(labels, (0, pad), constant_values=-1)[None, :]
    class_t = class_w.T
    attn_w_row = attn_w[None, :]

    if shape is None:
        where = jnp.zeros((2,), jnp.int32)
        gathered = lax.all_gather(conv_weight, "dp", axis=0, tiled=True)
        mask, pooled = forward_chunk(where, tile_rows, [gathered], None, True, positions)
    else:
        zs, ys, cs = shape
        core, row, deep = moves(shape)
        z, y, c = me // (ys * cs), me // cs % ys, me % cs
        place = jnp.stack([y * cs + c, y * cs + (c ^ 1), (y ^ 1) * cs + c, (y ^ 1) * cs + (c ^ 1)])
        mine, acc = conv_weight, None
        for step in range(zs):
            across = send(mine, row)
            pieces = [mine, send(mine, core), across, send(across, core)]
            where = jnp.concatenate([((z - step) % zs)[None], place]).astype(jnp.int32)
            last = step == zs - 1
            out = forward_chunk(where, tile_rows, pieces, acc, last, positions)
            if last:
                mask, pooled = out
            else:
                acc = out[0]
                mine = send(mine, deep(1))

    emb, gated, ua, ug, back, stat, packet = score(pooled, slide, attn_v, attn_u, attn_w_row, class_t, lanes)
    local = (pooled, emb, gated, ua, ug, back, stat)
    if shape is None:
        boxes = lax.all_gather(packet, "dp", axis=0)
        boxes = [boxes[i] for i in range(devices)]
        where = me[None].astype(jnp.int32)
    else:
        packet = merge(packet, send(packet, core))
        packet = merge(packet, send(packet, row))
        boxes = [packet] + [send(packet, deep(i)) for i in (2, 1, 3)]
        where = jnp.stack([me, y, c]).astype(jnp.int32)
    scale, small, term_keep, term_send, logit_rows, loss_rows = grads(
        where, boxes, local, slide, owner, label, class_t, slides, shape
    )
    slides_here = slides // devices
    logits = logit_rows[:slides_here, :classes]
    loss = loss_rows[0, :1]
    total = jnp.sum(lax.all_gather(small, "dp", axis=0), axis=0)
    class_grad = total[:classes, :channels].T
    attn_w_grad = total[classes, :hidden]
    d_pre = spread(mask, scale, positions)

    if shape is None:
        contract = (((0,), (0,)), ((), ()))
        term = lax.dot_general(tile_rows, d_pre, contract, preferred_element_type=F32)
        conv_grad = lax.psum_scatter(term, "dp", scatter_dimension=0, tiled=True)
        pair = lax.psum_scatter(term_keep, "dp", scatter_dimension=0, tiled=True)
        return (conv_grad, pair[:, :hidden], pair[:, hidden:], attn_w_grad, class_grad, logits, loss)

    def chip_sum(keep, away):
        got = send(away, core).astype(F32)
        over = send((keep[1] + got[1]).astype(BF16), row)
        return keep[0] + got[0] + over.astype(F32)

    pair_sum = chip_sum(term_keep, term_send)
    got = [
        send(lax.dynamic_index_in_dim(pair_sum, (z + i) % zs, 0, False).astype(BF16), deep(i)).astype(F32)
        for i in (2, 1, 3)
    ]
    pair = lax.dynamic_index_in_dim(pair_sum, z, 0, False) + got[0] + got[1] + got[2]

    arrived = []
    for step in (2, 1, 3, 0):
        where = jnp.stack([(z + step) % zs, y, c]).astype(jnp.int32)
        keep, away = backward_chunk(where, tile_rows, d_pre, ys, cs, share)
        block = chip_sum(keep, away)
        if step:
            arrived.append(send(block.astype(BF16), deep(step)))
        else:
            conv_grad = block
    for block in arrived:
        conv_grad = conv_grad + block.astype(F32)
    return (conv_grad, pair[:, :hidden], pair[:, hidden:], attn_w_grad, class_grad, logits, loss)


def solution(mesh):
    in_specs = (
        P(("groups", "dp"), None, None),
        P("dp", None),
        P(("groups", "dp")),
        P("groups"),
        P("groups"),
        P(),
        P(),
        P(),
        P(),
    )
    out_specs = (
        P(("groups", "dp"), None),
        P(("groups", "dp"), None),
        P(("groups", "dp"), None),
        P("groups"),
        P("groups", None),
        P(("groups", "dp"), None),
        P("groups"),
    )
    return jax.shard_map(per_device, mesh=mesh, in_specs=in_specs, out_specs=out_specs, check_vma=False)
```

time: 338 us -> 194 us (0.57)
  waiting for transfers between devices: 216 us -> 75.7 us
  Pallas kernels: 0 us -> 56.7 us
  matrix products: 36.6 us -> 0 us
  between operations: 14.7 us -> 0.91 us
  starting transfers between devices: 14.7 us -> 25.5 us
  blocking collectives: 32.1 us -> 22.5 us
  local copies, waits for them, and re-layouts: 15.2 us -> 8 us
  other arithmetic: 7.56 us -> 2.65 us
    unnamed x5 -> x0, waiting for transfers between devices: 116 us -> none
    ppermute x0 -> x36, waiting for transfers between devices: none -> 75.7 us  [send(): return lax.ppermute(x, 'dp', pairs)]
    pallas_call x0 -> x11, Pallas kernels: none -> 56.7 us  [the longest x4 31.5 us: forward_chunk(): pl.pallas_call(functools.partial(forward_kernel, pieces, first, last, pos...]
    all_gather x1 -> x0, waiting for transfers between devices: 45.5 us -> none  [per_device(): lax.all_gather(conv_weight, 'dp', axis=0, tiled=True)]
    reduce_scatter x2 -> x0, waiting for transfers between devices: 43.9 us -> none  [the longest x1 43.9 us: per_device(): lax.psum_scatter(v_grad, 'dp', scatter_dimension=0, tiled=True)]
    dot_general x19 -> x0, matrix products: 36.6 us -> none  [the longest x1 15.5 us: per_device(): lax.dot_general(tile_rows, d_pre, contract, preferred_element_type=jnp.fl...]
    psum x1 -> x0, blocking collectives: 32.1 us -> none  [per_device(): lax.psum((w_grad, c_grad, loss_sum.reshape(1)), 'dp')]
    ppermute x0 -> x36, starting transfers between devices: none -> 25.5 us  [send(): return lax.ppermute(x, 'dp', pairs)]
  transfers between devices with their start and end apart: 7 -> 36, of which waited for: 5 -> 15; matrix products, arithmetic and copies ran while one was open for 16% -> 4% of each run, Pallas kernels for 0% -> 25%
where the time goes in v1:
time: 194 us; the launch traced here: 192 us
  waiting for transfers between devices  75.7 us (39%)
  Pallas kernels  56.7 us (29%)
  starting transfers between devices  25.5 us (13%)
  blocking collectives  22.5 us (12%)
  local copies, waits for them, and re-layouts  8 us (4%)
  other arithmetic  2.65 us (1%)
    ppermute x36, waiting for transfers between devices, send(): return lax.ppermute(x, 'dp', pairs)  75.7 us
    pallas_call x4, Pallas kernels, forward_chunk(): pl.pallas_call(functools.partial(forward_kernel, pieces, first, last, pos...  31.5 us
    ppermute x36, starting transfers between devices, send(): return lax.ppermute(x, 'dp', pairs)  25.5 us
    all_gather x1, blocking collectives, per_device(): total = jnp.sum(lax.all_gather(small, 'dp', axis=0), axis=0)  22.5 us
    pallas_call x4, Pallas kernels, backward_chunk(): pl.pallas_call(functools.partial(backward_kernel, ys, cs), grid_spec=pltp...  20.1 us
  transfers between devices with their start and end apart: 36, of which 15 were waited for; matrix products, arithmetic and copies ran while one was open for 4% of the time, Pallas kernels for 25%

profile of v1, /device:TPU:0, one launch (start us, length us, event | category | flops | bytes accessed | tf_op | source)
XLA Modules:
  0.0 192.0 jit_solution(2432193420883194265)
XLA Ops:
  0.6 3.1 %collective-permute-start = (bf16[192,768]{1,0:T(8,128)(2,1)}, bf16[192,768]{1,0:T(8,128)(2,1)S(1)}, u32[]{:S(2)}, u32[]{:S(2)}) collective-permute-start(bf16[192,768]{1,0:T(8,128)(2,1)} %refs_0_.1), channel_id=1, source_target_pairs={{0,4},{1,5},{2,6},{3,7},{4,8},{5,9},{6,10},{7,11},{8,12},{9,13},{1... | collective-permute-start | bytes 884744 | tf_op jit(solution)/shard_map/ppermute | solution.py:385
  3.7 9.2 %collective-permute-done.refs_0_ = bf16[192,768]{1,0:T(8,128)(2,1)S(1)} collective-permute-done((bf16[192,768]{1,0:T(8,128)(2,1)}, bf16[192,768]{1,0:T(8,128)(2,1)S(1)}, u32[]{:S(2)}, u32[]{:S(2)}) %collective-permute-start) | collective-permute-done | bytes 294944 | tf_op jit(solution)/shard_map/ppermute | solution.py:385
  15.0 8.0 %collective-permute-done.1.refs_0_ = bf16[192,768]{1,0:T(8,128)(2,1)S(1)} collective-permute-done((bf16[192,768]{1,0:T(8,128)(2,1)S(1)}, bf16[192,768]{1,0:T(8,128)(2,1)S(1)}, u32[]{:S(2)}, u32[]{:S(2)}) %collective-permute-start.1) | collective-permute-done | bytes 294944 | tf_op jit(solution)/shard_map/ppermute | solution.py:385
  27.7 4.3 %collective-permute-done.2.refs_0_ = bf16[192,768]{1,0:T(8,128)(2,1)S(1)} collective-permute-done((bf16[192,768]{1,0:T(8,128)(2,1)S(1)}, bf16[192,768]{1,0:T(8,128)(2,1)S(1)}, u32[]{:S(2)}, u32[]{:S(2)}) %collective-permute-start.2) | collective-permute-done | bytes 294944 | tf_op jit(solution)/shard_map/ppermute | solution.py:385
  35.5 7.1 %section_forward.4.refs_4_ = f32[2048,768]{1,0:T(8,128)} custom-call(s32[5]{0:T(128)S(1)} %concatenate.19.where, bf16[2048,3072]{1,0:T(8,128)(2,1)} %bitcast.94, bf16[192,768]{1,0:T(8,128)(2,1)S(1)} %copy-done.3, bf16[192,768]{1,0:T(8,128)(2,1)S(1)} %collective-permute-done.12.refs_1_, bf16[192,768]{1,0:T(8,128)(2,1)S(1)} %collective-permute-done.13.refs_2_, ...), custom_call_target="tpu_custom_call" | custom-call | flops 2415919104 | bytes 15728640 | tf_op jit(solution)/shard_map/section_forward/pallas_call | solution.py:75
  43.2 8.7 %section_forward.5.refs_4_ = f32[2048,768]{1,0:T(8,128)} custom-call(s32[5]{0:T(128)S(1)} %concatenate.18.where, bf16[2048,3072]{1,0:T(8,128)(2,1)} %bitcast.95, bf16[192,768]{1,0:T(8,128)(2,1)S(1)} %collective-permute-done.refs_0_, bf16[192,768]{1,0:T(8,128)(2,1)S(1)} %collective-permute-done.9.refs_1_, ...), custom_call_target="tpu_custom_call" | custom-call | flops 2415919104 | bytes 15728640 | tf_op jit(solution)/shard_map/section_forward/pallas_call | solution.py:75
  51.9 8.7 %section_forward.6.refs_4_ = f32[2048,768]{1,0:T(8,128)} custom-call(s32[5]{0:T(128)S(1)} %concatenate.17.where, bf16[2048,3072]{1,0:T(8,128)(2,1)} %bitcast.96, bf16[192,768]{1,0:T(8,128)(2,1)S(1)} %collective-permute-done.1.refs_0_, bf16[192,768]{1,0:T(8,128)(2,1)S(1)} %collective-permute-done.6.refs_1_, ...), custom_call_target="tpu_custom_call" | custom-call | flops 2415919104 | bytes 15728640 | tf_op jit(solution)/shard_map/section_forward/pallas_call | solution.py:75
  60.6 7.0 %section_forward.7 = (bf16[2048,768]{1,0:T(8,128)(2,1)S(1)}, f32[32,768]{1,0:T(8,128)S(1)}) custom-call(s32[5]{0:T(128)S(1)} %concatenate.16.where, bf16[2048,3072]{1,0:T(8,128)(2,1)} %bitcast.97, bf16[192,768]{1,0:T(8,128)(2,1)S(1)} %collective-permute-done.2.refs_0_, bf16[192,768]{1,0:T(8,128)(2,1)S(1)} %collective-permute-done.3.refs_1_, ...), custom_call_target="tpu_custom_call" | custom-call | flops 2415919104 | bytes 15728640 | tf_op jit(solution)/shard_map/section_forward/pallas_call | solution.py:75
  72.8 2.3 %collective-permute-done.16 = f32[8,128]{1,0:T(8,128)S(1)} collective-permute-done((f32[8,128]{1,0:T(8,128)S(1)}, f32[8,128]{1,0:T(8,128)S(1)}, u32[]{:S(2)}, u32[]{:S(2)}) %collective-permute-start.16) | collective-permute-done | bytes 4128 | tf_op jit(solution)/shard_map/ppermute | solution.py:385
  77.2 2.4 %collective-permute-start.18 = (f32[8,128]{1,0:T(8,128)S(1)}, f32[8,128]{1,0:T(8,128)S(1)}, u32[]{:S(2)}, u32[]{:S(2)}) collective-permute-start(f32[8,128]{1,0:T(8,128)S(1)} %add_select_fusion.refs_0_), channel_id=1, source_target_pairs={{0,4},{1,5},{2,6},{3,7},{4,8},{5,9},{6,10},{7,11},{8,12},{9,13},{1... | collective-permute-start | bytes 12296 | tf_op jit(solution)/shard_map/ppermute | solution.py:385
  84.8 2.7 %section_spread.1.d_pre = bf16[2048,768]{1,0:T(8,128)(2,1)S(1)} custom-call(bf16[2048,768]{1,0:T(8,128)(2,1)} %copy-done, f32[32,768]{1,0:T(8,128)S(1)} %get-tuple-element.39.scale), custom_call_target="tpu_custom_call" | custom-call | tf_op jit(solution)/shard_map/section_spread/pallas_call | solution.py:307
  87.6 5.0 %section_backward.4 = (f32[2,192,768]{2,1,0:T(8,128)S(1)}, bf16[2,192,768]{2,1,0:T(8,128)(2,1)S(1)}) custom-call(s32[3]{0:T(128)S(1)} %add_add_fusion.where, bf16[2048,3072]{1,0:T(8,128)(2,1)} %bitcast.98, bf16[2048,768]{1,0:T(8,128)(2,1)S(1)} %section_spread.1.d_pre), custom_call_target="tpu_custom_call" | custom-call | flops 2415919104 | bytes 6291456 | tf_op jit(solution)/shard_map/section_backward/pallas_call | solution.py:339
  93.2 5.0 %section_backward.5 = (f32[2,192,768]{2,1,0:T(8,128)S(1)}, bf16[2,192,768]{2,1,0:T(8,128)(2,1)S(1)}) custom-call(s32[3]{0:T(128)S(1)} %get-tuple-element.64.where, bf16[2048,3072]{1,0:T(8,128)(2,1)} %bitcast.99, bf16[2048,768]{1,0:T(8,128)(2,1)S(1)} %section_spread.1.d_pre), custom_call_target="tpu_custom_call" | custom-call | flops 2415919104 | bytes 6291456 | tf_op jit(solution)/shard_map/section_backward/pallas_call | solution.py:339
  98.3 5.0 %section_backward.6 = (f32[2,192,768]{2,1,0:T(8,128)S(1)}, bf16[2,192,768]{2,1,0:T(8,128)(2,1)S(1)}) custom-call(s32[3]{0:T(128)S(1)} %get-tuple-element.65.where, bf16[2048,3072]{1,0:T(8,128)(2,1)} %bitcast.100, bf16[2048,768]{1,0:T(8,128)(2,1)S(1)} %section_spread.1.d_pre), custom_call_target="tpu_custom_call" | custom-call | flops 2415919104 | bytes 6291456 | tf_op jit(solution)/shard_map/section_backward/pallas_call | solution.py:339
  103.9 5.0 %section_backward.7 = (f32[2,192,768]{2,1,0:T(8,128)S(1)}, bf16[2,192,768]{2,1,0:T(8,128)(2,1)S(1)}) custom-call(s32[3]{0:T(128)S(1)} %add_add_fusion.4.where, bf16[2048,3072]{1,0:T(8,128)(2,1)} %bitcast.101, bf16[2048,768]{1,0:T(8,128)(2,1)S(1)} %section_spread.1.d_pre), custom_call_target="tpu_custom_call" | custom-call | flops 2415919104 | bytes 6291456 | tf_op jit(solution)/shard_map/section_backward/pallas_call | solution.py:339
  110.1 22.5 %all-gather = f32[128,768]{1,0:T(8,128)S(1)} all-gather(f32[8,768]{1,0:T(8,128)S(1)} %get-tuple-element.50), channel_id=2, replica_groups=mesh['groups'=2,'dp'=16] {'dp'}, dimensions={0}, use_global_device_ids=true | all-gather | bytes 417792 | tf_op jit(solution)/shard_map/all_gather | solution.py:446
  134.2 2.1 %collective-permute-start.21 = (bf16[192,768]{1,0:T(8,128)(2,1)S(1)}, bf16[192,768]{1,0:T(8,128)(2,1)S(1)}, u32[]{:S(2)}, u32[]{:S(2)}) collective-permute-start(bf16[192,768]{1,0:T(8,128)(2,1)S(1)} %fusion.21), channel_id=1, source_target_pairs={{0,2},{1,3},{2,0},{3,1},{4,6},{5,7},{6,4},{7,5},{8,10},{9,11},{10,... | collective-permute-start | bytes 884744 | tf_op jit(solution)/shard_map/ppermute | solution.py:385
  136.7 2.1 %collective-permute-start.26 = (bf16[192,768]{1,0:T(8,128)(2,1)S(1)}, bf16[192,768]{1,0:T(8,128)(2,1)S(1)}, u32[]{:S(2)}, u32[]{:S(2)}) collective-permute-start(bf16[192,768]{1,0:T(8,128)(2,1)S(1)} %fusion.23), channel_id=1, source_target_pairs={{0,2},{1,3},{2,0},{3,1},{4,6},{5,7},{6,4},{7,5},{8,10},{9,11},{10,... | collective-permute-start | bytes 884744 | tf_op jit(solution)/shard_map/ppermute | solution.py:385
  139.0 4.9 %collective-permute-done.32 = bf16[4,48,768]{2,1,0:T(8,128)(2,1)S(1)} collective-permute-done((bf16[4,48,768]{2,1,0:T(8,128)(2,1)S(1)}, bf16[4,48,768]{2,1,0:T(8,128)(2,1)S(1)}, u32[]{:S(2)}, u32[]{:S(2)}) %collective-permute-start.32) | collective-permute-done | bytes 294944 | tf_op jit(solution)/shard_map/ppermute | solution.py:385
  144.1 12.4 %collective-permute-done.23 = bf16[192,768]{1,0:T(8,128)(2,1)S(1)} collective-permute-done((bf16[192,768]{1,0:T(8,128)(2,1)S(1)}, bf16[192,768]{1,0:T(8,128)(2,1)S(1)}, u32[]{:S(2)}, u32[]{:S(2)}) %collective-permute-start.23) | collective-permute-done | bytes 294944 | tf_op jit(solution)/shard_map/ppermute | solution.py:385
  156.6 6.2 %collective-permute-done.26 = bf16[192,768]{1,0:T(8,128)(2,1)S(1)} collective-permute-done((bf16[192,768]{1,0:T(8,128)(2,1)S(1)}, bf16[192,768]{1,0:T(8,128)(2,1)S(1)}, u32[]{:S(2)}, u32[]{:S(2)}) %collective-permute-start.26) | collective-permute-done | bytes 294944 | tf_op jit(solution)/shard_map/ppermute | solution.py:385
  162.9 5.6 %collective-permute-done.29 = bf16[192,768]{1,0:T(8,128)(2,1)S(1)} collective-permute-done((bf16[192,768]{1,0:T(8,128)(2,1)S(1)}, bf16[192,768]{1,0:T(8,128)(2,1)S(1)}, u32[]{:S(2)}, u32[]{:S(2)}) %collective-permute-start.29) | collective-permute-done | bytes 294944 | tf_op jit(solution)/shard_map/ppermute | solution.py:385
  168.8 3.8 %collective-permute-start.30 = (bf16[192,768]{1,0:T(8,128)(2,1)S(1)}, bf16[192,768]{1,0:T(8,128)(2,1)S(1)}, u32[]{:S(2)}, u32[]{:S(2)}) collective-permute-start(bf16[192,768]{1,0:T(8,128)(2,1)S(1)} %fusion.6), channel_id=1, source_target_pairs={{0,12},{1,13},{2,14},{3,15},{4,0},{5,1},{6,2},{7,3},{8,4},{9,5},{1... | collective-permute-start | bytes 884744 | tf_op jit(solution)/shard_map/ppermute | solution.py:385
  173.3 15.6 %collective-permute-done.24 = bf16[192,768]{1,0:T(8,128)(2,1)S(1)} collective-permute-done((bf16[192,768]{1,0:T(8,128)(2,1)S(1)}, bf16[192,768]{1,0:T(8,128)(2,1)S(1)}, u32[]{:S(2)}, u32[]{:S(2)}) %collective-permute-start.24) | collective-permute-done | bytes 294944 | tf_op jit(solution)/shard_map/ppermute | solution.py:385
  (109 shorter events, 32.3 us)
Async XLA Ops:
  0.6 12.3 %collective-permute-start = (bf16[192,768]{1,0:T(8,128)(2,1)}, bf16[192,768]{1,0:T(8,128)(2,1)S(1)}, u32[]{:S(2)}, u32[]{:S(2)}) collective-permute-start(bf16[192,768]{1,0:T(8,128)(2,1)} %refs_0_.1), channel_id=1, source_target_pairs={{0,4},{1,5},{2,6},{3,7},{4,8},{5,9},{6,10},{7,11},{8,12},{9,13},{1... | collective-permute-start | bytes 884744 | tf_op jit(solution)/shard_map/ppermute | solution.py:385
  13.0 11.8 %collective-permute-start.13 = (bf16[192,768]{1,0:T(8,128)(2,1)}, bf16[192,768]{1,0:T(8,128)(2,1)S(1)}, u32[]{:S(2)}, u32[]{:S(2)}) collective-permute-start(bf16[192,768]{1,0:T(8,128)(2,1)} %refs_0_.1), channel_id=1, source_target_pairs={{0,2},{1,3},{2,0},{3,1},{4,6},{5,7},{6,4},{7,5},{8,10},{9,11},{10,... | collective-permute-start | bytes 884744 | tf_op jit(solution)/shard_map/ppermute | solution.py:385
  14.5 12.3 %collective-permute-start.12 = (bf16[192,768]{1,0:T(8,128)(2,1)}, bf16[192,768]{1,0:T(8,128)(2,1)S(1)}, u32[]{:S(2)}, u32[]{:S(2)}) collective-permute-start(bf16[192,768]{1,0:T(8,128)(2,1)} %refs_0_.1), channel_id=1, source_target_pairs={{0,1},{1,0},{2,3},{3,2},{4,5},{5,4},{6,7},{7,6},{8,9},{9,8},{10,11... | collective-permute-start | bytes 884744 | tf_op jit(solution)/shard_map/ppermute | solution.py:385
  14.5 13.2 %collective-permute-start.10 = (bf16[192,768]{1,0:T(8,128)(2,1)S(1)}, bf16[192,768]{1,0:T(8,128)(2,1)S(1)}, u32[]{:S(2)}, u32[]{:S(2)}) collective-permute-start(bf16[192,768]{1,0:T(8,128)(2,1)S(1)} %collective-permute-done.refs_0_), channel_id=1, source_target_pairs={{0,2},{1,3},{2,0},{3,1},{4,6},{5,7},{6,4},{7,5},{8,10},{9,11},{10,... | collective-permute-start | bytes 884744 | tf_op jit(solution)/shard_map/ppermute | solution.py:385
  26.7 15.9 %collective-permute-start.9 = (bf16[192,768]{1,0:T(8,128)(2,1)S(1)}, bf16[192,768]{1,0:T(8,128)(2,1)S(1)}, u32[]{:S(2)}, u32[]{:S(2)}) collective-permute-start(bf16[192,768]{1,0:T(8,128)(2,1)S(1)} %collective-permute-done.refs_0_), channel_id=1, source_target_pairs={{0,1},{1,0},{2,3},{3,2},{4,5},{5,4},{6,7},{7,6},{8,9},{9,8},{10,11... | collective-permute-start | bytes 884744 | tf_op jit(solution)/shard_map/ppermute | solution.py:385
  27.7 15.5 %collective-permute-start.11 = (bf16[192,768]{1,0:T(8,128)(2,1)S(1)}, bf16[192,768]{1,0:T(8,128)(2,1)S(1)}, u32[]{:S(2)}, u32[]{:S(2)}) collective-permute-start(bf16[192,768]{1,0:T(8,128)(2,1)S(1)} %collective-permute-done.10.refs_2_), channel_id=1, source_target_pairs={{0,1},{1,0},{2,3},{3,2},{4,5},{5,4},{6,7},{7,6},{8,9},{9,8},{10,11... | collective-permute-start | bytes 884744 | tf_op jit(solution)/shard_map/ppermute | solution.py:385
  33.1 18.8 %collective-permute-start.6 = (bf16[192,768]{1,0:T(8,128)(2,1)S(1)}, bf16[192,768]{1,0:T(8,128)(2,1)S(1)}, u32[]{:S(2)}, u32[]{:S(2)}) collective-permute-start(bf16[192,768]{1,0:T(8,128)(2,1)S(1)} %collective-permute-done.1.refs_0_), channel_id=1, source_target_pairs={{0,1},{1,0},{2,3},{3,2},{4,5},{5,4},{6,7},{7,6},{8,9},{9,8},{10,11... | collective-permute-start | bytes 884744 | tf_op jit(solution)/shard_map/ppermute | solution.py:385
  34.5 17.3 %collective-permute-start.8 = (bf16[192,768]{1,0:T(8,128)(2,1)S(1)}, bf16[192,768]{1,0:T(8,128)(2,1)S(1)}, u32[]{:S(2)}, u32[]{:S(2)}) collective-permute-start(bf16[192,768]{1,0:T(8,128)(2,1)S(1)} %collective-permute-done.7.refs_2_), channel_id=1, source_target_pairs={{0,1},{1,0},{2,3},{3,2},{4,5},{5,4},{6,7},{7,6},{8,9},{9,8},{10,11... | collective-permute-start | bytes 884744 | tf_op jit(solution)/shard_map/ppermute | solution.py:385
  42.6 18.0 %collective-permute-start.3 = (bf16[192,768]{1,0:T(8,128)(2,1)S(1)}, bf16[192,768]{1,0:T(8,128)(2,1)S(1)}, u32[]{:S(2)}, u32[]{:S(2)}) collective-permute-start(bf16[192,768]{1,0:T(8,128)(2,1)S(1)} %collective-permute-done.2.refs_0_), channel_id=1, source_target_pairs={{0,1},{1,0},{2,3},{3,2},{4,5},{5,4},{6,7},{7,6},{8,9},{9,8},{10,11... | collective-permute-start | bytes 884744 | tf_op jit(solution)/shard_map/ppermute | solution.py:385
  43.1 17.5 %collective-permute-start.5 = (bf16[192,768]{1,0:T(8,128)(2,1)S(1)}, bf16[192,768]{1,0:T(8,128)(2,1)S(1)}, u32[]{:S(2)}, u32[]{:S(2)}) collective-permute-start(bf16[192,768]{1,0:T(8,128)(2,1)S(1)} %collective-permute-done.4.refs_2_), channel_id=1, source_target_pairs={{0,1},{1,0},{2,3},{3,2},{4,5},{5,4},{6,7},{7,6},{8,9},{9,8},{10,11... | collective-permute-start | bytes 884744 | tf_op jit(solution)/shard_map/ppermute | solution.py:385
  84.8 49.0 %collective-permute-start.31 = (bf16[2,4,48,768]{3,2,1,0:T(8,128)(2,1)S(1)}, bf16[2,4,48,768]{3,2,1,0:T(8,128)(2,1)S(1)}, u32[]{:S(2)}, u32[]{:S(2)}) collective-permute-start(bf16[2,4,48,768]{3,2,1,0:T(8,128)(2,1)S(1)} %get-tuple-element.49), channel_id=1, source_target_pairs={{0,1},{1,0},{2,3},{3,2},{4,5},{5,4},{6,7},{7,6},{8,9},{9,8},{10,11... | collective-permute-start | bytes 1769480 | tf_op jit(solution)/shard_map/ppermute | solution.py:385
  92.6 41.5 %collective-permute-start.20 = (bf16[2,192,768]{2,1,0:T(8,128)(2,1)S(1)}, bf16[2,192,768]{2,1,0:T(8,128)(2,1)S(1)}, u32[]{:S(2)}, u32[]{:S(2)}) collective-permute-start(bf16[2,192,768]{2,1,0:T(8,128)(2,1)S(1)} %get-tuple-element.41), channel_id=1, source_target_pairs={{0,1},{1,0},{2,3},{3,2},{4,5},{5,4},{6,7},{7,6},{8,9},{9,8},{10,11... | collective-permute-start | bytes 1769480 | tf_op jit(solution)/shard_map/ppermute | solution.py:385
  98.2 38.1 %collective-permute-start.22 = (bf16[2,192,768]{2,1,0:T(8,128)(2,1)S(1)}, bf16[2,192,768]{2,1,0:T(8,128)(2,1)S(1)}, u32[]{:S(2)}, u32[]{:S(2)}) collective-permute-start(bf16[2,192,768]{2,1,0:T(8,128)(2,1)S(1)} %get-tuple-element.43), channel_id=1, source_target_pairs={{0,1},{1,0},{2,3},{3,2},{4,5},{5,4},{6,7},{7,6},{8,9},{9,8},{10,11... | collective-permute-start | bytes 1769480 | tf_op jit(solution)/shard_map/ppermute | solution.py:385
  103.3 33.2 %collective-permute-start.25 = (bf16[2,192,768]{2,1,0:T(8,128)(2,1)S(1)}, bf16[2,192,768]{2,1,0:T(8,128)(2,1)S(1)}, u32[]{:S(2)}, u32[]{:S(2)}) collective-permute-start(bf16[2,192,768]{2,1,0:T(8,128)(2,1)S(1)} %get-tuple-element.45), channel_id=1, source_target_pairs={{0,1},{1,0},{2,3},{3,2},{4,5},{5,4},{6,7},{7,6},{8,9},{9,8},{10,11... | collective-permute-start | bytes 1769480 | tf_op jit(solution)/shard_map/ppermute | solution.py:385
  108.9 29.9 %collective-permute-start.28 = (bf16[2,192,768]{2,1,0:T(8,128)(2,1)S(1)}, bf16[2,192,768]{2,1,0:T(8,128)(2,1)S(1)}, u32[]{:S(2)}, u32[]{:S(2)}) collective-permute-start(bf16[2,192,768]{2,1,0:T(8,128)(2,1)S(1)} %get-tuple-element.47), channel_id=1, source_target_pairs={{0,1},{1,0},{2,3},{3,2},{4,5},{5,4},{6,7},{7,6},{8,9},{9,8},{10,11... | collective-permute-start | bytes 1769480 | tf_op jit(solution)/shard_map/ppermute | solution.py:385
  134.2 39.1 %collective-permute-start.21 = (bf16[192,768]{1,0:T(8,128)(2,1)S(1)}, bf16[192,768]{1,0:T(8,128)(2,1)S(1)}, u32[]{:S(2)}, u32[]{:S(2)}) collective-permute-start(bf16[192,768]{1,0:T(8,128)(2,1)S(1)} %fusion.21), channel_id=1, source_target_pairs={{0,2},{1,3},{2,0},{3,1},{4,6},{5,7},{6,4},{7,5},{8,10},{9,11},{10,... | collective-permute-start | bytes 884744 | tf_op jit(solution)/shard_map/ppermute | solution.py:385
  136.4 20.1 %collective-permute-start.23 = (bf16[192,768]{1,0:T(8,128)(2,1)S(1)}, bf16[192,768]{1,0:T(8,128)(2,1)S(1)}, u32[]{:S(2)}, u32[]{:S(2)}) collective-permute-start(bf16[192,768]{1,0:T(8,128)(2,1)S(1)} %fusion.22), channel_id=1, source_target_pairs={{0,2},{1,3},{2,0},{3,1},{4,6},{5,7},{6,4},{7,5},{8,10},{9,11},{10,... | collective-permute-start | bytes 884744 | tf_op jit(solution)/shard_map/ppermute | solution.py:385
  136.7 26.1 %collective-permute-start.26 = (bf16[192,768]{1,0:T(8,128)(2,1)S(1)}, bf16[192,768]{1,0:T(8,128)(2,1)S(1)}, u32[]{:S(2)}, u32[]{:S(2)}) collective-permute-start(bf16[192,768]{1,0:T(8,128)(2,1)S(1)} %fusion.23), channel_id=1, source_target_pairs={{0,2},{1,3},{2,0},{3,1},{4,6},{5,7},{6,4},{7,5},{8,10},{9,11},{10,... | collective-permute-start | bytes 884744 | tf_op jit(solution)/shard_map/ppermute | solution.py:385
  138.9 29.7 %collective-permute-start.29 = (bf16[192,768]{1,0:T(8,128)(2,1)S(1)}, bf16[192,768]{1,0:T(8,128)(2,1)S(1)}, u32[]{:S(2)}, u32[]{:S(2)}) collective-permute-start(bf16[192,768]{1,0:T(8,128)(2,1)S(1)} %fusion.24), channel_id=1, source_target_pairs={{0,2},{1,3},{2,0},{3,1},{4,6},{5,7},{6,4},{7,5},{8,10},{9,11},{10,... | collective-permute-start | bytes 884744 | tf_op jit(solution)/shard_map/ppermute | solution.py:385
  144.0 24.7 %collective-permute-start.33 = (bf16[48,768]{1,0:T(8,128)(2,1)S(1)}, bf16[48,768]{1,0:T(8,128)(2,1)S(1)}, u32[]{:S(2)}, u32[]{:S(2)}) collective-permute-start(bf16[48,768]{1,0:T(8,128)(2,1)S(1)} %get-tuple-element.53), channel_id=1, source_target_pairs={{0,8},{1,9},{2,10},{3,11},{4,12},{5,13},{6,14},{7,15},{8,0},{9,1},... | collective-permute-start | bytes 221192 | tf_op jit(solution)/shard_map/ppermute | solution.py:385
  156.5 12.3 %collective-permute-start.34 = (bf16[48,768]{1,0:T(8,128)(2,1)S(1)}, bf16[48,768]{1,0:T(8,128)(2,1)S(1)}, u32[]{:S(2)}, u32[]{:S(2)}) collective-permute-start(bf16[48,768]{1,0:T(8,128)(2,1)S(1)} %get-tuple-element.55), channel_id=1, source_target_pairs={{0,4},{1,5},{2,6},{3,7},{4,8},{5,9},{6,10},{7,11},{8,12},{9,13},{1... | collective-permute-start | bytes 221192 | tf_op jit(solution)/shard_map/ppermute | solution.py:385
  168.6 20.3 %collective-permute-start.24 = (bf16[192,768]{1,0:T(8,128)(2,1)S(1)}, bf16[192,768]{1,0:T(8,128)(2,1)S(1)}, u32[]{:S(2)}, u32[]{:S(2)}) collective-permute-start(bf16[192,768]{1,0:T(8,128)(2,1)S(1)} %fusion.14), channel_id=1, source_target_pairs={{0,8},{1,9},{2,10},{3,11},{4,12},{5,13},{6,14},{7,15},{8,0},{9,1},... | collective-permute-start | bytes 884744 | tf_op jit(solution)/shard_map/ppermute | solution.py:385
  168.7 20.2 %collective-permute-start.27 = (bf16[192,768]{1,0:T(8,128)(2,1)S(1)}, bf16[192,768]{1,0:T(8,128)(2,1)S(1)}, u32[]{:S(2)}, u32[]{:S(2)}) collective-permute-start(bf16[192,768]{1,0:T(8,128)(2,1)S(1)} %fusion.10), channel_id=1, source_target_pairs={{0,4},{1,5},{2,6},{3,7},{4,8},{5,9},{6,10},{7,11},{8,12},{9,13},{1... | collective-permute-start | bytes 884744 | tf_op jit(solution)/shard_map/ppermute | solution.py:385
  168.8 22.2 %collective-permute-start.30 = (bf16[192,768]{1,0:T(8,128)(2,1)S(1)}, bf16[192,768]{1,0:T(8,128)(2,1)S(1)}, u32[]{:S(2)}, u32[]{:S(2)}) collective-permute-start(bf16[192,768]{1,0:T(8,128)(2,1)S(1)} %fusion.6), channel_id=1, source_target_pairs={{0,12},{1,13},{2,14},{3,15},{4,0},{5,1},{6,2},{7,3},{8,4},{9,5},{1... | collective-permute-start | bytes 884744 | tf_op jit(solution)/shard_map/ppermute | solution.py:385
  (17 other events, 116.4 us)

commit v2 on v1

v2 whole, which is shorter than its diff:
```python
import functools

import jax
import jax.numpy as jnp
from jax import lax
from jax.experimental import pallas as pl
from jax.experimental.pallas import tpu as pltpu
from jax.sharding import PartitionSpec as P

norm_eps = 1e-05
F32 = jnp.float32
BF16 = jnp.bfloat16
LANES = 128
EXTRA = 16
VMEM_LIMIT = 32 * 1024 * 1024


IN_VMEM = pl.BlockSpec(memory_space=pltpu.VMEM)
IN_SMEM = pl.BlockSpec(memory_space=pltpu.SMEM)
IN_HBM = pl.BlockSpec(memory_space=pltpu.HBM)
ANYWHERE = pl.BlockSpec(memory_space=pl.ANY)


def in_hbm(x):
    return pltpu.with_memory_space_constraint(x, pltpu.HBM)


def split_kernel(cs, share, where, tiles, own, away):
    inputs = tiles.shape[1]
    c = where[0]
    for ic in range(cs):
        starts = range(ic * share, inputs, cs * share)
        part = jnp.concatenate([tiles[:, at : at + share] for at in starts], axis=1)

        @pl.when(c == ic)
        def _():
            own[...] = part

        @pl.when(c != ic)
        def _():
            away[...] = part


def split_inputs(c, tile_rows, cs, share, part, parts):
    rows, inputs = tile_rows.shape
    rows = rows // parts
    block = min(rows, 256)
    skip = part * (rows // block)
    half = pl.BlockSpec((block, inputs // cs), lambda i: (i, 0))
    return pl.pallas_call(
        functools.partial(split_kernel, cs, share),
        grid=(rows // block,),
        in_specs=[IN_SMEM, pl.BlockSpec((block, inputs), lambda i: (skip + i, 0))],
        out_specs=[half, half],
        out_shape=[pltpu.HBM((rows, inputs // cs), BF16)] * 2,
        compiler_params=pltpu.CompilerParams(vmem_limit_bytes=VMEM_LIMIT),
        name="split_inputs",
    )(c[None].astype(jnp.int32), tile_rows)


def forward_kernel(groups, pieces, first, last, positions, where, token, tiles, *refs):
    ws = refs[:pieces]
    rest = refs[pieces:]
    if not first:
        acc_in, rest = rest[0], rest[1:]
    if last:
        mask_out, pooled_out, _, weight, rows_in, totals, sems, masks = rest
    else:
        acc_out, _, weight, rows_in, totals, sems = rest
    blocks, block, depth = rows_in.shape
    share = ws[0].shape[0]
    wide = depth // groups

    def here(i):
        return pl.ds(pl.multiple_of(i * block, block), block)

    def fetch(i, g):
        across = pl.ds(pl.multiple_of(where[g] * wide, wide), wide)
        to = rows_in.at[i, :, pl.ds(g * wide, wide)]
        return pltpu.make_async_copy(tiles.at[here(i), across], to, sems.at[3 + g, i])

    def resume(i):
        return pltpu.make_async_copy(acc_in.at[here(i)], totals.at[i], sems.at[1, i])

    def store(i):
        if last:
            return pltpu.make_async_copy(masks.at[i], mask_out.at[here(i)], sems.at[2, i])
        return pltpu.make_async_copy(totals.at[i], acc_out.at[here(i)], sems.at[2, i])

    for i in range(blocks):
        for g in range(groups):
            fetch(i, g).start()
        if not first:
            resume(i).start()
    for i in range(pieces):
        start = pl.multiple_of(where[groups + i] * share, share)
        weight[pl.ds(start, share), :] = ws[i][...]
    count = block // positions

    @pl.loop(0, blocks)
    def _(i):
        for g in range(groups):
            fetch(i, g).wait()
        total = jnp.dot(rows_in[i], weight[...], preferred_element_type=F32)
        if not first:
            resume(i).wait()
            total = total + totals[i]
        if last:
            masks[i] = jnp.where(total > 0, 1.0, jnp.where(total == 0, 0.5, 0.0)).astype(BF16)
            active = jnp.maximum(total, 0.0).reshape(count, positions, total.shape[1])
            pooled_out[pl.ds(pl.multiple_of(i * count, count), count), :] = jnp.sum(active, axis=1) * (1.0 / positions)
        else:
            totals[i] = total
        store(i).start()

    for i in range(blocks):
        store(i).wait()


def forward_chunk(where, token, tile_rows, ws, acc, last, positions, groups=1):
    rows, inputs = tile_rows.shape
    share, channels = ws[0].shape
    pieces = len(ws)
    depth = share * pieces
    block = 8 * positions if rows % (8 * positions) == 0 else rows
    first = acc is None
    in_specs = [IN_SMEM, ANYWHERE, IN_HBM] + [IN_VMEM] * pieces
    operands = [where, token, tile_rows, *ws]
    alias = {}
    if not first:
        in_specs.append(IN_HBM)
        operands.append(in_hbm(acc))
    if last:
        out_shape = [
            pltpu.HBM((rows, channels), BF16),
            jax.ShapeDtypeStruct((rows // positions, channels), F32),
        ]
        out_specs = [IN_HBM, IN_VMEM]
    else:
        out_shape = [pltpu.HBM((rows, channels), F32)]
        out_specs = [IN_HBM]
        if not first:
            alias = {len(operands) - 1: 0}
    alias[1] = len(out_shape)
    out_specs.append(ANYWHERE)
    out_shape.append(jax.ShapeDtypeStruct(token.shape, token.dtype))
    blocks = rows // block
    scratch = [
        pltpu.VMEM((depth, channels), BF16),
        pltpu.VMEM((blocks, block, depth), BF16),
        pltpu.VMEM((blocks, block, channels) if not (first and last) else (1, 8, LANES), F32),
        pltpu.SemaphoreType.DMA((3 + groups, blocks)),
    ]
    if last:
        scratch.append(pltpu.VMEM((blocks, block, channels), BF16))
    return pl.pallas_call(
        functools.partial(forward_kernel, groups, pieces, first, last, positions),
        in_specs=in_specs,
        out_specs=out_specs,
        scratch_shapes=scratch,
        out_shape=out_shape,
        input_output_aliases=alias,
        compiler_params=pltpu.CompilerParams(vmem_limit_bytes=VMEM_LIMIT if depth < inputs else 2 * VMEM_LIMIT - 2**22),
        cost_estimate=pl.CostEstimate(
            flops=2 * rows * depth * channels,
            bytes_accessed=2 * rows * depth,
            transcendentals=0,
        ),
        name="section_forward",
    )(*operands)


def member_of(tile_slide, lanes):
    slide = lax.broadcasted_iota(jnp.int32, (tile_slide.shape[0], lanes), 1)
    return (tile_slide == slide).astype(F32)


def normal(pooled):
    centred = pooled - jnp.mean(pooled, axis=-1, keepdims=True)
    spread = jnp.mean(centred * centred, axis=-1, keepdims=True)
    scale = lax.rsqrt(spread + norm_eps)
    return centred * scale, scale


def score_kernel(pooled, slide, attn_v, attn_u, attn_w, class_t, narrow_out, wide_out, packet_out):
    channels, hidden = attn_v.shape
    unit, _ = normal(pooled[...])
    emb = unit.astype(BF16)
    narrow_out[:, :channels] = emb
    act_a = jnp.tanh(jnp.dot(emb, attn_v[...], preferred_element_type=F32))
    act_g = jax.nn.sigmoid(jnp.dot(emb, attn_u[...], preferred_element_type=F32))
    gated = act_a * act_g
    wide_out[:, :hidden] = gated
    exp_score = jnp.exp(jnp.sum(gated * attn_w[...], axis=1, keepdims=True))
    emb32 = emb.astype(F32)
    classes = class_t.shape[0]
    reads = [jnp.sum(emb32 * class_t[k : k + 1, :], axis=1, keepdims=True) for k in range(classes)]
    lanes = packet_out.shape[1]
    member = member_of(slide[...], lanes)
    total = jnp.sum(member * exp_score, axis=0, keepdims=True)
    own_total = jnp.sum(member * total, axis=1, keepdims=True)
    part = jnp.where(own_total > 0, exp_score / own_total, 0.0)
    packet_out[...] = jnp.zeros_like(packet_out)
    packet_out[0:1, :] = total
    for k in range(classes):
        packet_out[k + 1 : k + 2, :] = jnp.sum(member * (part * reads[k]), axis=0, keepdims=True)
    column = lax.broadcasted_iota(jnp.int32, (emb.shape[0], LANES), 1)
    stats = jnp.where(column == 0, exp_score, 0.0)
    for k in range(classes):
        stats = jnp.where(column == k + 1, reads[k], stats)
    wide_out[:, hidden : hidden + LANES] = jnp.where(column == classes + 1, slide[...].astype(F32), stats)
    ua = (attn_w[...] * act_g * (1.0 - act_a * act_a)).astype(BF16)
    ug = (attn_w[...] * act_a * act_g * (1.0 - act_g)).astype(BF16)
    narrow_out[:, channels : channels + hidden] = ua
    narrow_out[:, channels + hidden :] = ug
    contract = (((1,), (1,)), ((), ()))
    wide_out[:, hidden + LANES : hidden + LANES + channels] = pooled[...]
    wide_out[:, hidden + LANES + channels :] = lax.dot_general(ua, attn_v[...], contract, preferred_element_type=F32) + lax.dot_general(
        ug, attn_u[...], contract, preferred_element_type=F32
    )


def score(pooled, slide, attn_v, attn_u, attn_w, class_t, lanes):
    tiles, channels = pooled.shape
    hidden = attn_v.shape[1]
    return pl.pallas_call(
        score_kernel,
        out_shape=[
            jax.ShapeDtypeStruct((tiles, channels + 2 * hidden), BF16),
            jax.ShapeDtypeStruct((tiles, hidden + LANES + 2 * channels), F32),
            jax.ShapeDtypeStruct((8, lanes), F32),
        ],
        compiler_params=pltpu.CompilerParams(vmem_limit_bytes=VMEM_LIMIT),
        name="tile_scores",
    )(pooled, slide, attn_v, attn_u, attn_w, class_t)


def merge(one, other):
    total = one[0:1] + other[0:1]
    safe = jnp.where(total > 0, total, 1.0)
    mean = one * (one[0:1] / safe) + other * (other[0:1] / safe)
    row = lax.broadcasted_iota(jnp.int32, one.shape, 0)
    return jnp.where(row == 0, total, mean)


def grads_kernel(
    packets,
    slides,
    shards,
    sides,
    positions,
    where,
    *refs,
):
    inputs, refs = refs[:sides], refs[sides:]
    boxes = refs[:packets]
    refs = refs[packets:]
    narrows, wides, refs = refs[:sides], refs[sides : 2 * sides], refs[2 * sides :]
    (owner, label, class_t, d_pre_out, term_keep, term_send, logit_out, loss_out, masks, sems) = refs
    blocks, block, channels = masks.shape
    per_side = blocks // sides
    fetches = [
        pltpu.make_async_copy(
            inputs[i // per_side].at[pl.ds(i % per_side * block, block)], masks.at[i], sems.at[i]
        )
        for i in range(blocks)
    ]
    for fetch in fetches:
        fetch.start()
    packet = boxes[0][...]
    for box in boxes[1:]:
        packet = merge(packet, box[...])
    classes = class_t.shape[0]
    lanes = packet.shape[1]
    total = packet[0:1]
    live = lax.broadcasted_iota(jnp.int32, (1, lanes), 1) < slides
    logits = [jnp.where(live, packet[k + 1 : k + 2], 0.0) for k in range(classes)]
    exp_logits = [jnp.exp(v) for v in logits]
    class_sum = functools.reduce(jnp.add, exp_logits)
    hot = [jnp.where(label[...] == k, 1.0, 0.0) for k in range(classes)]
    picked = functools.reduce(jnp.add, [v * h for v, h in zip(logits, hot)])
    loss = jnp.where(live, jnp.log(class_sum) - picked, 0.0)
    loss_out[...] = jnp.broadcast_to(jnp.sum(loss, axis=1, keepdims=True) / slides, loss_out.shape)
    d_logits = [jnp.where(live, (e / class_sum - h) / slides, 0.0) for e, h in zip(exp_logits, hot)]
    centre = functools.reduce(jnp.add, [d * v for d, v in zip(d_logits, logits)])

    mine = jnp.where((owner[...] == where[0]) & live, 1.0, 0.0)
    up = lax.broadcasted_iota(jnp.int32, (lanes, lanes), 0)
    across = lax.broadcasted_iota(jnp.int32, (lanes, lanes), 1)
    rank = jnp.dot(
        jnp.broadcast_to(mine, (8, lanes)), jnp.where(up < across, 1.0, 0.0), preferred_element_type=F32
    )
    wanted = lax.broadcasted_iota(jnp.int32, (8, lanes), 0).astype(F32)
    chosen = jnp.where((rank == wanted) & (mine > 0), 1.0, 0.0)
    column = lax.broadcasted_iota(jnp.int32, (8, LANES), 1)
    rows = jnp.zeros((8, LANES), F32)
    for k in range(classes):
        rows = jnp.where(column == k, jnp.sum(chosen * logits[k], axis=1, keepdims=True), rows)
    logit_out[...] = rows

    hidden = wides[0].shape[1] - LANES - 2 * channels

    def tile_terms(wide):
        stats = wide[:, hidden : hidden + LANES]
        member = member_of(stats[:, classes + 1 : classes + 2].astype(jnp.int32), lanes)

        def of_tile(row):
            return jnp.sum(member * row, axis=1, keepdims=True)

        weight = stats[:, 0:1] / of_tile(total)
        d_tile = [of_tile(d) for d in d_logits]
        d_weight = functools.reduce(jnp.add, [d * stats[:, k + 1 : k + 2] for k, d in enumerate(d_tile)])
        return weight.astype(BF16).astype(F32), d_tile, weight * (d_weight - of_tile(centre))

    terms = [tile_terms(wide) for wide in wides]
    count = block // positions
    for side in range(sides):
        kept, d_tile, d_score = terms[side]
        d_rows = functools.reduce(jnp.add, [d * class_t[k : k + 1, :] for k, d in enumerate(d_tile)])
        back = wides[side][:, hidden + LANES + channels :]
        d_emb = (kept * d_rows + d_score * back).astype(BF16).astype(F32)
        unit, inv = normal(wides[side][:, hidden + LANES : hidden + LANES + channels])
        d_pool = inv * (
            d_emb
            - jnp.mean(d_emb, axis=-1, keepdims=True)
            - unit * jnp.mean(d_emb * unit, axis=-1, keepdims=True)
        )
        scaled = (d_pool * (1.0 / positions)).astype(BF16)
        for j in range(per_side):
            i = side * per_side + j
            fetches[i].wait()
            here = masks[i].reshape(count, positions, channels)
            mine = scaled[j * count : (j + 1) * count]
            d_pre_out[i * block : (i + 1) * block] = (here * mine[:, None, :]).reshape(block, channels)

    smalls = [0.0] * classes
    wide_sum = 0.0
    embs, d_pres = [], []
    for (kept, d_tile, d_score), narrow, wide in zip(terms, narrows, wides):
        emb = narrow[:, :channels]
        emb32 = emb.astype(F32)
        for k in range(classes):
            smalls[k] = smalls[k] + jnp.sum(emb32 * (kept * d_tile[k]), axis=0, keepdims=True)
        wide_sum = wide_sum + jnp.sum(wide[:, :hidden] * d_score, axis=0, keepdims=True)
        embs.append(emb)
        d_pres.append((d_score * narrow[:, channels:].astype(F32)).astype(BF16))
    smalls.append(jnp.concatenate([wide_sum, jnp.zeros((1, hidden), F32)], axis=1))
    emb16 = jnp.concatenate(embs, axis=0)
    d_pre = jnp.concatenate(d_pres, axis=0)
    term = lax.dot_general(emb16, d_pre, (((0,), (0,)), ((), ())), preferred_element_type=F32)
    zs, ys, cs = shards
    share = channels // (zs * ys * cs)
    y, c = where[1], where[2]
    small = jnp.concatenate(smalls + [jnp.zeros((EXTRA - len(smalls), 2 * hidden), F32)], axis=0)
    if sides == 1:
        term_keep[:channels] = term
        term_keep[channels:] = small
        term_send[...] = jnp.zeros_like(term_send)
        return
    base = zs * share
    term_keep[base:] = small
    term_send[base:] = halves(small, len(smalls))
    for iy in range(ys):
        for ic in range(cs):
            starts = [((iz * ys + iy) * cs + ic) * share for iz in range(zs)]
            rows = jnp.concatenate([term[at : at + share] for at in starts], axis=0)

            @pl.when((c == ic) & (y == iy))
            def _():
                term_keep[:base] = rows

            @pl.when((c == ic) & (y != iy))
            def _():
                term_send[:base] = rows.astype(BF16)


def halves(small, count):
    high = small.astype(BF16).astype(F32)
    low = small - high
    return jnp.concatenate([high[:count], low[:count], jnp.zeros_like(small[2 * count :])], axis=0).astype(BF16)


def joined(rows, count):
    wide = rows.astype(F32)
    return jnp.concatenate([wide[:count] + wide[count : 2 * count], jnp.zeros_like(wide[count:])], axis=0)


def deep_kernel(count, steps, where, keep, got, own, *away):
    share = own.shape[0] - EXTRA
    zs = len(steps) + 1
    small = keep[zs * share :] + joined(got[zs * share :], count)
    split = halves(small, count)
    for step, out in zip((0, *steps), (own, *away)):
        at = pl.ds(pl.multiple_of((where[0] + step) % zs * share, share), share)
        block = keep[at, :] + got[at, :].astype(F32)
        out[:share] = block.astype(out.dtype)
        out[share:] = small if step == 0 else split


def deep_fold(where, keep, got, steps, count):
    zs = len(steps) + 1
    shape = ((keep.shape[0] - EXTRA) // zs + EXTRA, keep.shape[1])
    return pl.pallas_call(
        functools.partial(deep_kernel, count, steps),
        in_specs=[pl.BlockSpec(memory_space=pltpu.SMEM)] + [pl.BlockSpec(memory_space=pltpu.VMEM)] * 2,
        out_shape=[jax.ShapeDtypeStruct(shape, F32)] + [jax.ShapeDtypeStruct(shape, BF16)] * len(steps),
        compiler_params=pltpu.CompilerParams(vmem_limit_bytes=VMEM_LIMIT),
        name="attention_deep",
    )(where, keep, got)


def last_kernel(count, own, *rest):
    got, (v_out, u_out, small_out) = rest[:-3], rest[-3:]
    share, hidden = v_out.shape
    block = own[:share]
    small = own[share:]
    for one in got:
        block = block + one[:share].astype(F32)
        small = small + joined(one[share:], count)
    v_out[...] = block[:, :hidden]
    u_out[...] = block[:, hidden:]
    small_out[...] = small


def last_fold(own, got, count):
    share, hidden = own.shape[0] - EXTRA, own.shape[1] // 2
    return pl.pallas_call(
        functools.partial(last_kernel, count),
        out_shape=[
            jax.ShapeDtypeStruct((share, hidden), F32),
            jax.ShapeDtypeStruct((share, hidden), F32),
            jax.ShapeDtypeStruct((EXTRA, own.shape[1]), F32),
        ],
        compiler_params=pltpu.CompilerParams(vmem_limit_bytes=VMEM_LIMIT),
        name="attention_last",
    )(own, *got)


def grads(where, masks, boxes, narrows, wides, owner, label, class_t, slides, shards, positions):
    rows, channels = masks[0].shape
    hidden = wides[0].shape[1] - LANES - 2 * channels
    zs, ys, cs = shards
    sides = len(narrows)
    keep_shape = (channels // (ys * cs) + EXTRA, 2 * hidden)
    send_shape = keep_shape if sides > 1 else (16, LANES)
    block = 8 * positions if rows % (8 * positions) == 0 else rows
    operands = [where, *map(in_hbm, masks), *boxes, *narrows, *wides, owner, label, class_t]
    return pl.pallas_call(
        functools.partial(grads_kernel, len(boxes), slides, shards, sides, positions),
        in_specs=[IN_SMEM] + [IN_HBM] * sides + [IN_VMEM] * (len(operands) - 1 - sides),
        out_shape=[
            pltpu.VMEM((sides * rows, channels), BF16) if sides > 1 else jax.ShapeDtypeStruct((rows, channels), BF16),
            jax.ShapeDtypeStruct(keep_shape, F32),
            jax.ShapeDtypeStruct(send_shape, BF16),
            jax.ShapeDtypeStruct((8, LANES), F32),
            jax.ShapeDtypeStruct((8, LANES), F32),
        ],
        scratch_shapes=[
            pltpu.VMEM((sides * rows // block, block, channels), BF16),
            pltpu.SemaphoreType.DMA((sides * rows // block,)),
        ],
        compiler_params=pltpu.CompilerParams(vmem_limit_bytes=VMEM_LIMIT),
        name="head_grads",
    )(*operands)


def backward_kernel(ys, parts, where, token, d_pre, *refs):
    tiles, refs = refs[:parts], refs[parts:]
    near, over, _, refs = refs[0], refs[1], refs[2], refs[3:]
    _, columns, sems = refs
    sides, rows, width = columns.shape
    share = width // ys
    y = where[1]
    across = pl.ds(pl.multiple_of(where[0] * width, width), width)
    fetches = [pltpu.make_async_copy(tiles[i].at[:, across], columns.at[i], sems.at[i]) for i in range(sides)]
    for fetch in fetches:
        fetch.start()
    contract = (((0,), (0,)), ((), ()))
    term = 0.0
    for i in range(0, sides, 2):
        fetches[i].wait()
        fetches[i + 1].wait()
        both = columns[i : i + 2].reshape(2 * rows, width)
        term = term + lax.dot_general(
            both, d_pre[i * rows : (i + 2) * rows], contract, preferred_element_type=F32
        )
    for iy in range(ys):
        block = term[iy * share : (iy + 1) * share]

        @pl.when(y == iy)
        def _():
            near[...] = block

        @pl.when(y != iy)
        def _():
            over[...] = block.astype(BF16)


def backward_chunk(where, token, tiles, d_pre, ys, share):
    rows = tiles[0].shape[0]
    channels = d_pre.shape[1]
    width = ys * share
    operands = [where, token, pltpu.with_memory_space_constraint(d_pre, pltpu.VMEM), *map(in_hbm, tiles)]
    return pl.pallas_call(
        functools.partial(backward_kernel, ys, len(tiles)),
        in_specs=[IN_SMEM, ANYWHERE, IN_VMEM] + [IN_HBM] * len(tiles),
        out_specs=[IN_VMEM, IN_VMEM, IN_VMEM, ANYWHERE],
        scratch_shapes=[
            pltpu.VMEM((len(tiles), rows, width), BF16),
            pltpu.SemaphoreType.DMA((len(tiles),)),
        ],
        out_shape=[
            jax.ShapeDtypeStruct((share, channels), F32),
            jax.ShapeDtypeStruct((share, channels), BF16),
            pltpu.VMEM(d_pre.shape, d_pre.dtype),
            jax.ShapeDtypeStruct(token.shape, token.dtype),
        ],
        input_output_aliases={1: 3, 2: 2},
        compiler_params=pltpu.CompilerParams(vmem_limit_bytes=VMEM_LIMIT),
        cost_estimate=pl.CostEstimate(
            flops=2 * len(tiles) * rows * width * channels,
            bytes_accessed=2 * len(tiles) * rows * width,
            transcendentals=0,
        ),
        name="section_backward",
    )(*operands)


def sum_fold(near, got, dtype):
    total = near
    for one in got:
        total = total + one.astype(F32)
    return total.astype(dtype)


def grid_of(devices):
    return (4, 2, 2) if devices == 16 else None


def moves(shape):
    zs, ys, cs = shape

    def at(z, y, c):
        return (z * ys + y) * cs + c

    every = [(z, y, c) for z in range(zs) for y in range(ys) for c in range(cs)]
    core = [(at(*i), at(i[0], i[1], i[2] ^ 1)) for i in every]
    row = [(at(*i), at(i[0], i[1] ^ 1, i[2])) for i in every]

    def deep(step):
        return [(at(*i), at((i[0] + step) % zs, i[1], i[2])) for i in every]

    return core, row, deep


def together(*values):
    return lax.optimization_barrier(values)


def send(x, pairs):
    return lax.ppermute(x, "dp", pairs)


def per_device(tiles, conv_weight, tile_slide, slide_owner, labels, attn_v, attn_u, attn_w, class_w):
    tile_count, positions, inputs = tiles.shape
    share, channels = conv_weight.shape
    hidden = attn_v.shape[1]
    classes = class_w.shape[1]
    slides = slide_owner.shape[0]
    devices = lax.axis_size("dp")
    me = lax.axis_index("dp")
    shape = grid_of(devices)
    rows = tile_count * positions
    plain_rows = tiles.reshape(rows, inputs)
    tile_rows = in_hbm(plain_rows)
    lanes = -(-slides // LANES) * LANES
    pad = lanes - slides
    slide = tile_slide[:, None]
    owner = jnp.pad(slide_owner, (0, pad), constant_values=-1)[None, :]
    label = jnp.pad(labels, (0, pad), constant_values=-1)[None, :]
    class_t = class_w.T
    attn_w_row = attn_w[None, :]

    token = jnp.zeros((8, LANES), F32)
    if shape is None:
        where = jnp.zeros((2,), jnp.int32)
        gathered = lax.all_gather(conv_weight, "dp", axis=0, tiled=True)
        mask, pooled, token = forward_chunk(where, token, tile_rows, [gathered], None, True, positions)
    else:
        zs, ys, cs = shape
        core, row, deep = moves(shape)
        z, y, c = me // (ys * cs), me // cs % ys, me % cs
        place = [y * cs + c, y * cs + (c ^ 1), (y ^ 1) * cs + c, (y ^ 1) * cs + (c ^ 1)]
        own_parts, away_parts = [], []
        acc, mine = None, conv_weight
        across = send(mine, row)
        waiting, groups, last = [], [], zs - 1
        for step in range(zs):
            if step < last:
                ahead = send(mine, deep(1))
                if step < 2:
                    own_part, away_part = split_inputs(c, tile_rows, cs, share, step, 2)
                    across, ahead, token, own_part, away_part = together(across, ahead, token, own_part, away_part)
                    own_parts.append(own_part)
                    away_parts.append(send(away_part, core))
                else:
                    across, ahead, token, away_parts[0] = together(across, ahead, token, away_parts[0])
                ahead_across = send(ahead, row)
            waiting += [mine, send(mine, core), across, send(across, core)]
            groups.append((z - step) % zs)
            if step > 0:
                spots = [i * ys * cs + at for i in range(len(groups)) for at in place]
                where = jnp.stack([*groups, *spots]).astype(jnp.int32)
                *out, token = forward_chunk(
                    where, token, tile_rows, waiting, acc, step == last, positions, len(groups)
                )
                acc = out[0]
                waiting, groups = [], []
            if step < last:
                mine, across = ahead, ahead_across
            if step == last - 1:
                across, token, away_parts[1] = together(across, token, away_parts[1])
        mask, pooled = out

    narrow, wide, packet = score(pooled, slide, attn_v, attn_u, attn_w_row, class_t, lanes)
    narrows, wides, masks = [narrow], [wide], [mask]
    if shape is None:
        boxes = lax.all_gather(packet, "dp", axis=0)
        boxes = [boxes[i] for i in range(devices)]
        where = jnp.stack([me, me, me]).astype(jnp.int32)
    else:
        packet = merge(packet, send(packet, core))
        packet = merge(packet, send(packet, row))
        packet, *ours = together(packet, narrow, wide, mask)
        for group, one in zip((narrows, wides, masks), ours):
            group[0] = one
            group.append(send(one, core))
        boxes = [packet] + [send(packet, deep(i)) for i in (2, 1, 3)]
        where = jnp.stack([me, y, c]).astype(jnp.int32)
    d_pre, term_keep, term_send, logit_rows, loss_rows = grads(
        where, masks, boxes, narrows, wides, owner, label, class_t, slides, shape or (1, 1, 1), positions
    )
    slides_here = slides // devices
    logits = logit_rows[:slides_here, :classes]
    loss = loss_rows[0, :1]

    if shape is None:
        contract = (((0,), (0,)), ((), ()))
        term = lax.dot_general(plain_rows, d_pre, contract, preferred_element_type=F32)
        conv_grad = lax.psum_scatter(term, "dp", scatter_dimension=0, tiled=True)
        pair = lax.psum_scatter(term_keep[:channels], "dp", scatter_dimension=0, tiled=True)
        small = jnp.sum(lax.all_gather(term_keep[channels:], "dp", axis=0), axis=0)
        return (conv_grad, pair[:, :hidden], pair[:, hidden:], small[classes, :hidden], small[:classes].T, logits, loss)

    extra = classes + 1
    steps = (2, 1, 3)
    term_send, token = together(term_send, token)
    attn_got = send(term_send, row)

    where = {step: jnp.stack([(z + step) % zs, y, c]).astype(jnp.int32) for step in (0, *steps)}
    first, second, third = steps

    parts = own_parts + away_parts

    def chunk(step, d_pre, token):
        return backward_chunk(where[step], token, parts, d_pre, ys, share)

    near_first, over_first, d_pre, token = chunk(first, d_pre, token)
    over_first, attn_got, token = together(over_first, attn_got, token)
    y_first = send(over_first, row)
    own, *away = deep_fold(z[None], term_keep, attn_got, steps, extra)
    *away, token = together(*away, token)
    attn = [send(block, deep(i)) for i, block in zip(steps, away)]
    near_second, over_second, d_pre, token = chunk(second, d_pre, token)
    over_second, y_first, token, *attn = together(over_second, y_first, token, *attn)
    y_second = send(over_second, row)
    out_first, token = together(sum_fold(near_first, [y_first], BF16), token)
    z_first = send(out_first, deep(first))
    near_third, over_third, d_pre, token = chunk(third, d_pre, token)
    over_third, y_second, token = together(over_third, y_second, token)
    y_third = send(over_third, row)
    out_second, token = together(sum_fold(near_second, [y_second], BF16), token)
    z_second = send(out_second, deep(second))
    near_own, over_own, d_pre, token = chunk(0, d_pre, token)
    over_own, y_third, z_first, token = together(over_own, y_third, z_first, token)
    y_own = send(over_own, row)
    out_third, z_second = together(sum_fold(near_third, [y_third], BF16), z_second)
    z_third = send(out_third, deep(third))
    v_grad, u_grad, small = last_fold(own, attn, extra)
    conv_grad = sum_fold(near_own, [y_own, z_first, z_second, z_third], F32)
    return (conv_grad, v_grad, u_grad, small[classes, :hidden], small[:classes].T, logits, loss)


def solution(mesh):
    in_specs = (
        P(("groups", "dp"), None, None),
        P("dp", None),
        P(("groups", "dp")),
        P("groups"),
        P("groups"),
        P(),
        P(),
        P(),
        P(),
    )
    out_specs = (
        P(("groups", "dp"), None),
        P(("groups", "dp"), None),
        P(("groups", "dp"), None),
        P("groups"),
        P("groups", None),
        P(("groups", "dp"), None),
        P("groups"),
    )
    return jax.shard_map(per_device, mesh=mesh, in_specs=in_specs, out_specs=out_specs, check_vma=False)
```

time: 194 us -> 135 us (0.70)
  waiting for transfers between devices: 75.7 us -> 34.9 us
  blocking collectives: 22.5 us -> 0 us
  Pallas kernels: 56.7 us -> 63.4 us
  starting transfers between devices: 25.5 us -> 29.5 us
  local copies, waits for them, and re-layouts: 8 us -> 4.32 us
    ppermute x36, waiting for transfers between devices: 75.7 us -> 34.9 us  [send(): return lax.ppermute(x, 'dp', pairs)]
    all_gather x1 -> x0, blocking collectives: 22.5 us -> none  [per_device(): total = jnp.sum(lax.all_gather(small, 'dp', axis=0), axis=0)]
    pallas_call x9 -> x11, Pallas kernels: 54.3 us -> 58.4 us  [the longest x3 23.4 us: forward_chunk(): pl.pallas_call(functools.partial(forward_kernel, groups, pieces, first, l...]
    ppermute x36, starting transfers between devices: 25.5 us -> 29.5 us  [send(): return lax.ppermute(x, 'dp', pairs)]
    pallas_call x1, Pallas kernels: 1.58 us -> 4.19 us  [grads(): pl.pallas_call(functools.partial(grads_kernel, len(boxes), slides, shards...]
  transfers between devices with their start and end apart: 36 -> 36, of which waited for: 15 -> 16; matrix products, arithmetic and copies ran while one was open for 4% -> 2% of each run, Pallas kernels for 25% -> 38%
where the time goes in v2:
time: 135 us
  Pallas kernels  63.4 us (47%)
  waiting for transfers between devices  34.9 us (26%)
  starting transfers between devices  29.5 us (22%)
  local copies, waits for them, and re-layouts  4.32 us (3%)
  other arithmetic  1.52 us (1%)
    ppermute x36, waiting for transfers between devices, send(): return lax.ppermute(x, 'dp', pairs)  34.9 us
    ppermute x36, starting transfers between devices, send(): return lax.ppermute(x, 'dp', pairs)  29.5 us
    pallas_call x3, Pallas kernels, forward_chunk(): pl.pallas_call(functools.partial(forward_kernel, groups, pieces, first, l...  23.4 us
    pallas_call x4, Pallas kernels, backward_chunk(): pl.pallas_call(functools.partial(backward_kernel, ys, len(tiles)), in_spe...  20.7 us
    pallas_call x2, Pallas kernels, split_inputs(): pl.pallas_call(functools.partial(split_kernel, cs, share), grid=(rows //...  13.6 us
    pallas_call x1, Pallas kernels, grads(): pl.pallas_call(functools.partial(grads_kernel, len(boxes), slides, shards...  4.19 us
  transfers between devices with their start and end apart: 36, of which 16 were waited for; matrix products, arithmetic and copies ran while one was open for 2% of the time, Pallas kernels for 38%

profile of v2, /device:TPU:0, one launch (start us, length us, event | category | flops | bytes accessed | tf_op | source)
XLA Modules:
  0.0 134.6 jit_solution(11949667432050238110)
XLA Ops:
  0.6 3.1 %collective-permute-start.1 = (bf16[192,768]{1,0:T(8,128)(2,1)}, bf16[192,768]{1,0:T(8,128)(2,1)S(1)}, u32[]{:S(2)}, u32[]{:S(2)}) collective-permute-start(bf16[192,768]{1,0:T(8,128)(2,1)} %refs_0_.1), channel_id=1, source_target_pairs={{0,4},{1,5},{2,6},{3,7},{4,8},{5,9},{6,10},{7,11},{8,12},{9,13},{1... | collective-permute-start | bytes 884744 | tf_op jit(solution)/shard_map/ppermute | solution.py:561
  5.2 6.8 %split_inputs.2 = (bf16[1024,1536]{1,0:T(8,128)(2,1)}, bf16[1024,1536]{1,0:T(8,128)(2,1)}) custom-call(s32[1]{0:T(128)} %bitcast.2.where, bf16[2048,3072]{1,0:T(8,128)(2,1)} %bitcast.43), custom_call_target="tpu_custom_call" | custom-call | tf_op jit(solution)/shard_map/split_inputs/pallas_call | solution.py:50
  15.5 6.8 %split_inputs.3 = (bf16[1024,1536]{1,0:T(8,128)(2,1)}, bf16[1024,1536]{1,0:T(8,128)(2,1)}) custom-call(s32[1]{0:T(128)} %bitcast.2.where, bf16[2048,3072]{1,0:T(8,128)(2,1)} %bitcast.44), custom_call_target="tpu_custom_call" | custom-call | tf_op jit(solution)/shard_map/split_inputs/pallas_call | solution.py:50
  22.3 1.9 %collective-permute-done.3.refs_0_ = bf16[192,768]{1,0:T(8,128)(2,1)S(1)} collective-permute-done((bf16[192,768]{1,0:T(8,128)(2,1)S(1)}, bf16[192,768]{1,0:T(8,128)(2,1)S(1)}, u32[]{:S(2)}, u32[]{:S(2)}) %collective-permute-start.3) | collective-permute-done | bytes 294944 | tf_op jit(solution)/shard_map/ppermute | solution.py:561
  25.2 4.7 %collective-permute-done.6.refs_1_ = bf16[192,768]{1,0:T(8,128)(2,1)S(1)} collective-permute-done((bf16[192,768]{1,0:T(8,128)(2,1)S(1)}, bf16[192,768]{1,0:T(8,128)(2,1)S(1)}, u32[]{:S(2)}, u32[]{:S(2)}) %collective-permute-start.6) | collective-permute-done | bytes 294944 | tf_op jit(solution)/shard_map/ppermute | solution.py:561
  34.7 8.8 %section_forward.3 = (f32[2048,768]{1,0:T(8,128)}, f32[8,128]{1,0:T(8,128)S(1)}) custom-call(s32[10]{0:T(128)S(1)} %stack.114.where, f32[8,128]{1,0:T(8,128)S(1)} %broadcast_in_dim.43.token, bf16[2048,3072]{1,0:T(8,128)(2,1)} %bitcast.45, bf16[192,768]{1,0:T(8,128)(2,1)S(1)} %copy-done.3, ...), custom_call_target="tpu_custom_call", output_to_operand_aliasing={{1}: (1, {})} | custom-call | flops 4831838208 | bytes 6291456 | tf_op jit(solution)/shard_map/section_forward/pallas_call | solution.py:156
  45.3 7.0 %section_forward.4 = (f32[2048,768]{1,0:T(8,128)}, f32[8,128]{1,0:T(8,128)S(1)}) custom-call(s32[5]{0:T(128)S(1)} %stack.116.where, f32[8,128]{1,0:T(8,128)S(1)} %get-tuple-element.108.token, bf16[2048,3072]{1,0:T(8,128)(2,1)} %bitcast.46, bf16[192,768]{1,0:T(8,128)(2,1)S(1)} %collective-permute-done.3.refs_0_, ...), custom_call_target="tpu_custom_call", output_to_operand_aliasing={{0}: (7, {}), {1}: (1, {})} | custom-call | flops 2415919104 | bytes 3145728 | tf_op jit(solution)/shard_map/section_forward/pallas_call | solution.py:156
  54.7 7.5 %section_forward.5 = (bf16[2048,768]{1,0:T(8,128)(2,1)}, f32[32,768]{1,0:T(8,128)S(1)}, f32[8,128]{1,0:T(8,128)S(1)}) custom-call(s32[5]{0:T(128)S(1)} %stack.108.where, f32[8,128]{1,0:T(8,128)S(1)} %get-tuple-element.113.token, bf16[2048,3072]{1,0:T(8,128)(2,1)} %bitcast.47, ...), custom_call_target="tpu_custom_call", output_to_operand_aliasing={{2}: (1, {})} | custom-call | flops 2415919104 | bytes 3145728 | tf_op jit(solution)/shard_map/section_forward/pallas_call | solution.py:156
  64.9 3.1 %collective-permute-done.18 = f32[8,128]{1,0:T(8,128)S(1)} collective-permute-done((f32[8,128]{1,0:T(8,128)S(1)}, f32[8,128]{1,0:T(8,128)S(1)}, u32[]{:S(2)}, u32[]{:S(2)}) %collective-permute-start.18) | collective-permute-done | bytes 4128 | tf_op jit(solution)/shard_map/ppermute | solution.py:561
  68.6 3.1 %collective-permute-start.22 = (f32[8,128]{1,0:T(8,128)S(1)}, f32[8,128]{1,0:T(8,128)S(1)}, u32[]{:S(2)}, u32[]{:S(2)}) collective-permute-start(f32[8,128]{1,0:T(8,128)S(1)} %add_select_fusion.refs_2_), channel_id=1, source_target_pairs={{0,12},{1,13},{2,14},{3,15},{4,0},{5,1},{6,2},{7,3},{8,4},{9,5},{1... | collective-permute-start | bytes 12296 | tf_op jit(solution)/shard_map/ppermute | solution.py:561
  73.1 4.1 %collective-permute-done.21.refs_4_ = f32[8,128]{1,0:T(8,128)S(1)} collective-permute-done((f32[8,128]{1,0:T(8,128)S(1)}, f32[8,128]{1,0:T(8,128)S(1)}, u32[]{:S(2)}, u32[]{:S(2)}) %collective-permute-start.21) | collective-permute-done | bytes 4128 | tf_op jit(solution)/shard_map/ppermute | solution.py:561
  77.2 4.2 %head_grads.1 = (bf16[4096,768]{1,0:T(8,128)(2,1)S(1)}, f32[208,768]{1,0:T(8,128)S(1)}, bf16[208,768]{1,0:T(8,128)(2,1)S(1)}, f32[8,128]{1,0:T(8,128)S(1)}, f32[8,128]{1,0:T(8,128)S(1)}) custom-call(s32[3]{0:T(128)S(1)} %get-tuple-element.191.where, bf16[2048,768]{1,0:T(8,128)(2,1)} %get-tuple-element.121.refs_0_, ...), custom_call_target="tpu_custom_call" | custom-call | tf_op jit(solution)/shard_map/head_grads/pallas_call | solution.py:448
  82.0 5.2 %section_backward.4 = (f32[192,768]{1,0:T(8,128)S(1)}, bf16[192,768]{1,0:T(8,128)(2,1)S(1)}, bf16[4096,768]{1,0:T(8,128)(2,1)S(1)}, f32[8,128]{1,0:T(8,128)S(1)}) custom-call(s32[3]{0:T(128)S(1)} %get-tuple-element.192.where, f32[8,128]{1,0:T(8,128)S(1)} %get-tuple-element.128.token, ...), custom_call_target="tpu_custom_call", output_to_operand_aliasing={{3}: (1, {}), {2}: (2, {})} | custom-call | flops 2415919104 | bytes 3145728 | tf_op jit(solution)/shard_map/section_backward/pallas_call | solution.py:504
  87.2 2.3 %collective-permute-done.25.got = bf16[208,768]{1,0:T(8,128)(2,1)S(1)} collective-permute-done((bf16[208,768]{1,0:T(8,128)(2,1)S(1)}, bf16[208,768]{1,0:T(8,128)(2,1)S(1)}, u32[]{:S(2)}, u32[]{:S(2)}) %collective-permute-start.25) | collective-permute-done | bytes 319520 | tf_op jit(solution)/shard_map/ppermute | solution.py:561
  91.7 2.9 %collective-permute-start.28 = (bf16[64,768]{1,0:T(8,128)(2,1)S(1)}, bf16[64,768]{1,0:T(8,128)(2,1)S(1)}, u32[]{:S(2)}, u32[]{:S(2)}) collective-permute-start(bf16[64,768]{1,0:T(8,128)(2,1)S(1)} %get-tuple-element.150), channel_id=1, source_target_pairs={{0,4},{1,5},{2,6},{3,7},{4,8},{5,9},{6,10},{7,11},{8,12},{9,13},{1... | collective-permute-start | bytes 294920 | tf_op jit(solution)/shard_map/ppermute | solution.py:561
  95.6 5.2 %section_backward.5 = (f32[192,768]{1,0:T(8,128)S(1)}, bf16[192,768]{1,0:T(8,128)(2,1)S(1)}, bf16[4096,768]{1,0:T(8,128)(2,1)S(1)}, f32[8,128]{1,0:T(8,128)S(1)}) custom-call(s32[3]{0:T(128)S(1)} %get-tuple-element.190.where, f32[8,128]{1,0:T(8,128)S(1)} %get-tuple-element.142.token, ...), custom_call_target="tpu_custom_call", output_to_operand_aliasing={{3}: (1, {}), {2}: (2, {})} | custom-call | flops 2415919104 | bytes 3145728 | tf_op jit(solution)/shard_map/section_backward/pallas_call | solution.py:504
  101.1 1.6 %collective-permute-start.30 = (bf16[192,768]{1,0:T(8,128)(2,1)S(1)}, bf16[192,768]{1,0:T(8,128)(2,1)S(1)}, u32[]{:S(2)}, u32[]{:S(2)}) collective-permute-start(bf16[192,768]{1,0:T(8,128)(2,1)S(1)} %get-tuple-element.157), channel_id=1, source_target_pairs={{0,2},{1,3},{2,0},{3,1},{4,6},{5,7},{6,4},{7,5},{8,10},{9,11},{10,... | collective-permute-start | bytes 884744 | tf_op jit(solution)/shard_map/ppermute | solution.py:561
  104.2 5.2 %section_backward.6 = (f32[192,768]{1,0:T(8,128)S(1)}, bf16[192,768]{1,0:T(8,128)(2,1)S(1)}, bf16[4096,768]{1,0:T(8,128)(2,1)S(1)}, f32[8,128]{1,0:T(8,128)S(1)}) custom-call(s32[3]{0:T(128)S(1)} %add_add_fusion.4.where, f32[8,128]{1,0:T(8,128)S(1)} %get-tuple-element.154.token, ...), custom_call_target="tpu_custom_call", output_to_operand_aliasing={{3}: (1, {}), {2}: (2, {})} | custom-call | flops 2415919104 | bytes 3145728 | tf_op jit(solution)/shard_map/section_backward/pallas_call | solution.py:504
  109.9 2.0 %collective-permute-start.34 = (bf16[192,768]{1,0:T(8,128)(2,1)S(1)}, bf16[192,768]{1,0:T(8,128)(2,1)S(1)}, u32[]{:S(2)}, u32[]{:S(2)}) collective-permute-start(bf16[192,768]{1,0:T(8,128)(2,1)S(1)} %add_convert_fusion.1), channel_id=1, source_target_pairs={{0,4},{1,5},{2,6},{3,7},{4,8},{5,9},{6,10},{7,11},{8,12},{9,13},{1... | collective-permute-start | bytes 884744 | tf_op jit(solution)/shard_map/ppermute | solution.py:561
  112.0 5.2 %section_backward.7 = (f32[192,768]{1,0:T(8,128)S(1)}, bf16[192,768]{1,0:T(8,128)(2,1)S(1)}, bf16[4096,768]{1,0:T(8,128)(2,1)S(1)}, f32[8,128]{1,0:T(8,128)S(1)}) custom-call(s32[3]{0:T(128)S(1)} %get-tuple-element.189.where, f32[8,128]{1,0:T(8,128)S(1)} %get-tuple-element.161.token, ...), custom_call_target="tpu_custom_call", output_to_operand_aliasing={{3}: (1, {}), {2}: (2, {})} | custom-call | flops 2415919104 | bytes 3145728 | tf_op jit(solution)/shard_map/section_backward/pallas_call | solution.py:504
  117.1 5.6 %collective-permute-done.32 = bf16[192,768]{1,0:T(8,128)(2,1)S(1)} collective-permute-done((bf16[192,768]{1,0:T(8,128)(2,1)S(1)}, bf16[192,768]{1,0:T(8,128)(2,1)S(1)}, u32[]{:S(2)}, u32[]{:S(2)}) %collective-permute-start.32) | collective-permute-done | bytes 294944 | tf_op jit(solution)/shard_map/ppermute | solution.py:561
  122.8 2.2 %collective-permute-start.35 = (bf16[192,768]{1,0:T(8,128)(2,1)S(1)}, bf16[192,768]{1,0:T(8,128)(2,1)S(1)}, u32[]{:S(2)}, u32[]{:S(2)}) collective-permute-start(bf16[192,768]{1,0:T(8,128)(2,1)S(1)} %add_convert_fusion), channel_id=1, source_target_pairs={{0,12},{1,13},{2,14},{3,15},{4,0},{5,1},{6,2},{7,3},{8,4},{9,5},{1... | collective-permute-start | bytes 884744 | tf_op jit(solution)/shard_map/ppermute | solution.py:561
  126.6 4.8 %collective-permute-done.35 = bf16[192,768]{1,0:T(8,128)(2,1)S(1)} collective-permute-done((bf16[192,768]{1,0:T(8,128)(2,1)S(1)}, bf16[192,768]{1,0:T(8,128)(2,1)S(1)}, u32[]{:S(2)}, u32[]{:S(2)}) %collective-permute-start.35) | collective-permute-done | bytes 294944 | tf_op jit(solution)/shard_map/ppermute | solution.py:561
  131.4 2.2 %collective-permute-done.33 = bf16[192,768]{1,0:T(8,128)(2,1)S(1)} collective-permute-done((bf16[192,768]{1,0:T(8,128)(2,1)S(1)}, bf16[192,768]{1,0:T(8,128)(2,1)S(1)}, u32[]{:S(2)}, u32[]{:S(2)}) %collective-permute-start.33) | collective-permute-done | bytes 294944 | tf_op jit(solution)/shard_map/ppermute | solution.py:561
  (104 shorter events, 28.4 us)
Async XLA Ops:
  0.6 12.3 %collective-permute-start.1 = (bf16[192,768]{1,0:T(8,128)(2,1)}, bf16[192,768]{1,0:T(8,128)(2,1)S(1)}, u32[]{:S(2)}, u32[]{:S(2)}) collective-permute-start(bf16[192,768]{1,0:T(8,128)(2,1)} %refs_0_.1), channel_id=1, source_target_pairs={{0,4},{1,5},{2,6},{3,7},{4,8},{5,9},{6,10},{7,11},{8,12},{9,13},{1... | collective-permute-start | bytes 884744 | tf_op jit(solution)/shard_map/ppermute | solution.py:561
  3.7 9.2 %collective-permute-start = (bf16[192,768]{1,0:T(8,128)(2,1)}, bf16[192,768]{1,0:T(8,128)(2,1)S(1)}, u32[]{:S(2)}, u32[]{:S(2)}) collective-permute-start(bf16[192,768]{1,0:T(8,128)(2,1)} %refs_0_.1), channel_id=1, source_target_pairs={{0,2},{1,3},{2,0},{3,1},{4,6},{5,7},{6,4},{7,5},{8,10},{9,11},{10,... | collective-permute-start | bytes 884744 | tf_op jit(solution)/shard_map/ppermute | solution.py:561
  13.0 30.6 %collective-permute-start.10 = (bf16[1024,1536]{1,0:T(8,128)(2,1)}, bf16[1024,1536]{1,0:T(8,128)(2,1)}, u32[]{:S(2)}, u32[]{:S(2)}) collective-permute-start(bf16[1024,1536]{1,0:T(8,128)(2,1)} %get-tuple-element.106), channel_id=1, source_target_pairs={{0,1},{1,0},{2,3},{3,2},{4,5},{5,4},{6,7},{7,6},{8,9},{9,8},{10,11... | collective-permute-start | bytes 9437192 | tf_op jit(solution)/shard_map/ppermute | solution.py:561
  13.0 11.2 %collective-permute-start.3 = (bf16[192,768]{1,0:T(8,128)(2,1)S(1)}, bf16[192,768]{1,0:T(8,128)(2,1)S(1)}, u32[]{:S(2)}, u32[]{:S(2)}) collective-permute-start(bf16[192,768]{1,0:T(8,128)(2,1)S(1)} %collective-permute-done.1.refs_4_), channel_id=1, source_target_pairs={{0,4},{1,5},{2,6},{3,7},{4,8},{5,9},{6,10},{7,11},{8,12},{9,13},{1... | collective-permute-start | bytes 884744 | tf_op jit(solution)/shard_map/ppermute | solution.py:561
  14.0 10.2 %collective-permute-start.2 = (bf16[192,768]{1,0:T(8,128)(2,1)S(1)}, bf16[192,768]{1,0:T(8,128)(2,1)S(1)}, u32[]{:S(2)}, u32[]{:S(2)}) collective-permute-start(bf16[192,768]{1,0:T(8,128)(2,1)S(1)} %collective-permute-done.1.refs_4_), channel_id=1, source_target_pairs={{0,2},{1,3},{2,0},{3,1},{4,6},{5,7},{6,4},{7,5},{8,10},{9,11},{10,... | collective-permute-start | bytes 884744 | tf_op jit(solution)/shard_map/ppermute | solution.py:561
  24.2 28.1 %collective-permute-start.14 = (bf16[1024,1536]{1,0:T(8,128)(2,1)}, bf16[1024,1536]{1,0:T(8,128)(2,1)}, u32[]{:S(2)}, u32[]{:S(2)}) collective-permute-start(bf16[1024,1536]{1,0:T(8,128)(2,1)} %get-tuple-element.112), channel_id=1, source_target_pairs={{0,1},{1,0},{2,3},{3,2},{4,5},{5,4},{6,7},{7,6},{8,9},{9,8},{10,11... | collective-permute-start | bytes 9437192 | tf_op jit(solution)/shard_map/ppermute | solution.py:561
  30.4 14.2 %collective-permute-start.12 = (bf16[192,768]{1,0:T(8,128)(2,1)S(1)}, bf16[192,768]{1,0:T(8,128)(2,1)S(1)}, u32[]{:S(2)}, u32[]{:S(2)}) collective-permute-start(bf16[192,768]{1,0:T(8,128)(2,1)S(1)} %collective-permute-done.3.refs_0_), channel_id=1, source_target_pairs={{0,1},{1,0},{2,3},{3,2},{4,5},{5,4},{6,7},{7,6},{8,9},{9,8},{10,11... | collective-permute-start | bytes 884744 | tf_op jit(solution)/shard_map/ppermute | solution.py:561
  30.7 12.8 %collective-permute-start.5 = (bf16[192,768]{1,0:T(8,128)(2,1)S(1)}, bf16[192,768]{1,0:T(8,128)(2,1)S(1)}, u32[]{:S(2)}, u32[]{:S(2)}) collective-permute-start(bf16[192,768]{1,0:T(8,128)(2,1)S(1)} %collective-permute-done.3.refs_0_), channel_id=1, source_target_pairs={{0,4},{1,5},{2,6},{3,7},{4,8},{5,9},{6,10},{7,11},{8,12},{9,13},{1... | collective-permute-start | bytes 884744 | tf_op jit(solution)/shard_map/ppermute | solution.py:561
  32.2 11.3 %collective-permute-start.4 = (bf16[192,768]{1,0:T(8,128)(2,1)S(1)}, bf16[192,768]{1,0:T(8,128)(2,1)S(1)}, u32[]{:S(2)}, u32[]{:S(2)}) collective-permute-start(bf16[192,768]{1,0:T(8,128)(2,1)S(1)} %collective-permute-done.3.refs_0_), channel_id=1, source_target_pairs={{0,2},{1,3},{2,0},{3,1},{4,6},{5,7},{6,4},{7,5},{8,10},{9,11},{10,... | collective-permute-start | bytes 884744 | tf_op jit(solution)/shard_map/ppermute | solution.py:561
  43.7 9.4 %collective-permute-start.11 = (bf16[192,768]{1,0:T(8,128)(2,1)S(1)}, bf16[192,768]{1,0:T(8,128)(2,1)S(1)}, u32[]{:S(2)}, u32[]{:S(2)}) collective-permute-start(bf16[192,768]{1,0:T(8,128)(2,1)S(1)} %collective-permute-done.5.refs_0_), channel_id=1, source_target_pairs={{0,2},{1,3},{2,0},{3,1},{4,6},{5,7},{6,4},{7,5},{8,10},{9,11},{10,... | collective-permute-start | bytes 884744 | tf_op jit(solution)/shard_map/ppermute | solution.py:561
  44.3 9.0 %collective-permute-start.15 = (bf16[192,768]{1,0:T(8,128)(2,1)S(1)}, bf16[192,768]{1,0:T(8,128)(2,1)S(1)}, u32[]{:S(2)}, u32[]{:S(2)}) collective-permute-start(bf16[192,768]{1,0:T(8,128)(2,1)S(1)} %collective-permute-done.5.refs_0_), channel_id=1, source_target_pairs={{0,1},{1,0},{2,3},{3,2},{4,5},{5,4},{6,7},{7,6},{8,9},{9,8},{10,11... | collective-permute-start | bytes 884744 | tf_op jit(solution)/shard_map/ppermute | solution.py:561
  68.1 9.1 %collective-permute-start.19 = (bf16[2048,768]{1,0:T(8,128)(2,1)}, bf16[2048,768]{1,0:T(8,128)(2,1)}, u32[]{:S(2)}, u32[]{:S(2)}) collective-permute-start(bf16[2048,768]{1,0:T(8,128)(2,1)} %get-tuple-element.121.refs_0_), channel_id=1, source_target_pairs={{0,1},{1,0},{2,3},{3,2},{4,5},{5,4},{6,7},{7,6},{8,9},{9,8},{10,11... | collective-permute-start | bytes 9437192 | tf_op jit(solution)/shard_map/ppermute | solution.py:561
  68.1 9.1 %collective-permute-start.24 = (f32[32,2048]{1,0:T(8,128)S(1)}, f32[32,2048]{1,0:T(8,128)S(1)}, u32[]{:S(2)}, u32[]{:S(2)}) collective-permute-start(f32[32,2048]{1,0:T(8,128)S(1)} %get-tuple-element.124.refs_8_), channel_id=1, source_target_pairs={{0,1},{1,0},{2,3},{3,2},{4,5},{5,4},{6,7},{7,6},{8,9},{9,8},{10,11... | collective-permute-start | bytes 786440 | tf_op jit(solution)/shard_map/ppermute | solution.py:561
  81.4 8.2 %collective-permute-start.25 = (bf16[208,768]{1,0:T(8,128)(2,1)S(1)}, bf16[208,768]{1,0:T(8,128)(2,1)S(1)}, u32[]{:S(2)}, u32[]{:S(2)}) collective-permute-start(bf16[208,768]{1,0:T(8,128)(2,1)S(1)} %get-tuple-element.135), channel_id=1, source_target_pairs={{0,2},{1,3},{2,0},{3,1},{4,6},{5,7},{6,4},{7,5},{8,10},{9,11},{10,... | collective-permute-start | bytes 958472 | tf_op jit(solution)/shard_map/ppermute | solution.py:561
  89.6 11.5 %collective-permute-start.26 = (bf16[192,768]{1,0:T(8,128)(2,1)S(1)}, bf16[192,768]{1,0:T(8,128)(2,1)S(1)}, u32[]{:S(2)}, u32[]{:S(2)}) collective-permute-start(bf16[192,768]{1,0:T(8,128)(2,1)S(1)} %get-tuple-element.147), channel_id=1, source_target_pairs={{0,2},{1,3},{2,0},{3,1},{4,6},{5,7},{6,4},{7,5},{8,10},{9,11},{10,... | collective-permute-start | bytes 884744 | tf_op jit(solution)/shard_map/ppermute | solution.py:561
  91.3 9.8 %collective-permute-start.27 = (bf16[64,768]{1,0:T(8,128)(2,1)S(1)}, bf16[64,768]{1,0:T(8,128)(2,1)S(1)}, u32[]{:S(2)}, u32[]{:S(2)}) collective-permute-start(bf16[64,768]{1,0:T(8,128)(2,1)S(1)} %get-tuple-element.149), channel_id=1, source_target_pairs={{0,8},{1,9},{2,10},{3,11},{4,12},{5,13},{6,14},{7,15},{8,0},{9,1},... | collective-permute-start | bytes 294920 | tf_op jit(solution)/shard_map/ppermute | solution.py:561
  91.7 9.3 %collective-permute-start.28 = (bf16[64,768]{1,0:T(8,128)(2,1)S(1)}, bf16[64,768]{1,0:T(8,128)(2,1)S(1)}, u32[]{:S(2)}, u32[]{:S(2)}) collective-permute-start(bf16[64,768]{1,0:T(8,128)(2,1)S(1)} %get-tuple-element.150), channel_id=1, source_target_pairs={{0,4},{1,5},{2,6},{3,7},{4,8},{5,9},{6,10},{7,11},{8,12},{9,13},{1... | collective-permute-start | bytes 294920 | tf_op jit(solution)/shard_map/ppermute | solution.py:561
  94.6 6.5 %collective-permute-start.29 = (bf16[64,768]{1,0:T(8,128)(2,1)S(1)}, bf16[64,768]{1,0:T(8,128)(2,1)S(1)}, u32[]{:S(2)}, u32[]{:S(2)}) collective-permute-start(bf16[64,768]{1,0:T(8,128)(2,1)S(1)} %get-tuple-element.151), channel_id=1, source_target_pairs={{0,12},{1,13},{2,14},{3,15},{4,0},{5,1},{6,2},{7,3},{8,4},{9,5},{1... | collective-permute-start | bytes 294920 | tf_op jit(solution)/shard_map/ppermute | solution.py:561
  101.1 8.3 %collective-permute-start.30 = (bf16[192,768]{1,0:T(8,128)(2,1)S(1)}, bf16[192,768]{1,0:T(8,128)(2,1)S(1)}, u32[]{:S(2)}, u32[]{:S(2)}) collective-permute-start(bf16[192,768]{1,0:T(8,128)(2,1)S(1)} %get-tuple-element.157), channel_id=1, source_target_pairs={{0,2},{1,3},{2,0},{3,1},{4,6},{5,7},{6,4},{7,5},{8,10},{9,11},{10,... | collective-permute-start | bytes 884744 | tf_op jit(solution)/shard_map/ppermute | solution.py:561
  102.8 20.0 %collective-permute-start.32 = (bf16[192,768]{1,0:T(8,128)(2,1)S(1)}, bf16[192,768]{1,0:T(8,128)(2,1)S(1)}, u32[]{:S(2)}, u32[]{:S(2)}) collective-permute-start(bf16[192,768]{1,0:T(8,128)(2,1)S(1)} %add_convert_fusion.2), channel_id=1, source_target_pairs={{0,8},{1,9},{2,10},{3,11},{4,12},{5,13},{6,14},{7,15},{8,0},{9,1},... | collective-permute-start | bytes 884744 | tf_op jit(solution)/shard_map/ppermute | solution.py:561
  109.4 13.4 %collective-permute-start.31 = (bf16[192,768]{1,0:T(8,128)(2,1)S(1)}, bf16[192,768]{1,0:T(8,128)(2,1)S(1)}, u32[]{:S(2)}, u32[]{:S(2)}) collective-permute-start(bf16[192,768]{1,0:T(8,128)(2,1)S(1)} %get-tuple-element.165), channel_id=1, source_target_pairs={{0,2},{1,3},{2,0},{3,1},{4,6},{5,7},{6,4},{7,5},{8,10},{9,11},{10,... | collective-permute-start | bytes 884744 | tf_op jit(solution)/shard_map/ppermute | solution.py:561
  109.9 12.8 %collective-permute-start.34 = (bf16[192,768]{1,0:T(8,128)(2,1)S(1)}, bf16[192,768]{1,0:T(8,128)(2,1)S(1)}, u32[]{:S(2)}, u32[]{:S(2)}) collective-permute-start(bf16[192,768]{1,0:T(8,128)(2,1)S(1)} %add_convert_fusion.1), channel_id=1, source_target_pairs={{0,4},{1,5},{2,6},{3,7},{4,8},{5,9},{6,10},{7,11},{8,12},{9,13},{1... | collective-permute-start | bytes 884744 | tf_op jit(solution)/shard_map/ppermute | solution.py:561
  122.8 8.6 %collective-permute-start.35 = (bf16[192,768]{1,0:T(8,128)(2,1)S(1)}, bf16[192,768]{1,0:T(8,128)(2,1)S(1)}, u32[]{:S(2)}, u32[]{:S(2)}) collective-permute-start(bf16[192,768]{1,0:T(8,128)(2,1)S(1)} %add_convert_fusion), channel_id=1, source_target_pairs={{0,12},{1,13},{2,14},{3,15},{4,0},{5,1},{6,2},{7,3},{8,4},{9,5},{1... | collective-permute-start | bytes 884744 | tf_op jit(solution)/shard_map/ppermute | solution.py:561
  125.0 8.6 %collective-permute-start.33 = (bf16[192,768]{1,0:T(8,128)(2,1)S(1)}, bf16[192,768]{1,0:T(8,128)(2,1)S(1)}, u32[]{:S(2)}, u32[]{:S(2)}) collective-permute-start(bf16[192,768]{1,0:T(8,128)(2,1)S(1)} %get-tuple-element.167), channel_id=1, source_target_pairs={{0,2},{1,3},{2,0},{3,1},{4,6},{5,7},{6,4},{7,5},{8,10},{9,11},{10,... | collective-permute-start | bytes 884744 | tf_op jit(solution)/shard_map/ppermute | solution.py:561
  (22 other events, 132.0 us)

commit v3 on v2

--- a/solution.py
+++ b/solution.py
@@ -64,9 +64,9 @@
     if not first:
         acc_in, rest = rest[0], rest[1:]
     if last:
-        mask_out, pooled_out, _, weight, rows_in, totals, sems, masks = rest
+        mask_out, pooled_out, _, weight, rows_in, totals, sems, loads, masks = rest
     else:
-        acc_out, _, weight, rows_in, totals, sems = rest
+        acc_out, _, weight, rows_in, totals, sems, loads = rest
     blocks, block, depth = rows_in.shape
     share = ws[0].shape[0]
     wide = depth // groups
@@ -78,6 +78,10 @@
         across = pl.ds(pl.multiple_of(where[g] * wide, wide), wide)
         to = rows_in.at[i, :, pl.ds(g * wide, wide)]
         return pltpu.make_async_copy(tiles.at[here(i), across], to, sems.at[3 + g, i])
+
+    def load(i):
+        start = pl.multiple_of(where[groups + i] * share, share)
+        return pltpu.make_async_copy(ws[i], weight.at[pl.ds(start, share)], loads.at[i])
 
     def resume(i):
         return pltpu.make_async_copy(acc_in.at[here(i)], totals.at[i], sems.at[1, i])
@@ -93,8 +97,9 @@
         if not first:
             resume(i).start()
     for i in range(pieces):
-        start = pl.multiple_of(where[groups + i] * share, share)
-        weight[pl.ds(start, share), :] = ws[i][...]
+        load(i).start()
+    for i in range(pieces):
+        load(i).wait()
     count = block // positions
 
     @pl.loop(0, blocks)
@@ -124,7 +129,7 @@
     depth = share * pieces
     block = 8 * positions if rows % (8 * positions) == 0 else rows
     first = acc is None
-    in_specs = [IN_SMEM, ANYWHERE, IN_HBM] + [IN_VMEM] * pieces
+    in_specs = [IN_SMEM, ANYWHERE, IN_HBM] + [ANYWHERE] * pieces
     operands = [where, token, tile_rows, *ws]
     alias = {}
     if not first:
@@ -150,6 +155,7 @@
         pltpu.VMEM((blocks, block, depth), BF16),
         pltpu.VMEM((blocks, block, channels) if not (first and last) else (1, 8, LANES), F32),
         pltpu.SemaphoreType.DMA((3 + groups, blocks)),
+        pltpu.SemaphoreType.DMA((pieces,)),
     ]
     if last:
         scratch.append(pltpu.VMEM((blocks, block, channels), BF16))
@@ -449,7 +455,7 @@
         functools.partial(grads_kernel, len(boxes), slides, shards, sides, positions),
         in_specs=[IN_SMEM] + [IN_HBM] * sides + [IN_VMEM] * (len(operands) - 1 - sides),
         out_shape=[
-            pltpu.VMEM((sides * rows, channels), BF16) if sides > 1 else jax.ShapeDtypeStruct((rows, channels), BF16),
+            jax.ShapeDtypeStruct((sides * rows, channels), BF16),
             jax.ShapeDtypeStruct(keep_shape, F32),
             jax.ShapeDtypeStruct(send_shape, BF16),
             jax.ShapeDtypeStruct((8, LANES), F32),
@@ -466,7 +472,7 @@
 
 def backward_kernel(ys, parts, where, token, d_pre, *refs):
     tiles, refs = refs[:parts], refs[parts:]
-    near, over, _, refs = refs[0], refs[1], refs[2], refs[3:]
+    near, over, refs = refs[0], refs[1], refs[2:]
     _, columns, sems = refs
     sides, rows, width = columns.shape
     share = width // ys
@@ -500,11 +506,11 @@
     rows = tiles[0].shape[0]
     channels = d_pre.shape[1]
     width = ys * share
-    operands = [where, token, pltpu.with_memory_space_constraint(d_pre, pltpu.VMEM), *map(in_hbm, tiles)]
+    operands = [where, token, d_pre, *map(in_hbm, tiles)]
     return pl.pallas_call(
         functools.partial(backward_kernel, ys, len(tiles)),
         in_specs=[IN_SMEM, ANYWHERE, IN_VMEM] + [IN_HBM] * len(tiles),
-        out_specs=[IN_VMEM, IN_VMEM, IN_VMEM, ANYWHERE],
+        out_specs=[IN_VMEM, IN_VMEM, ANYWHERE],
         scratch_shapes=[
             pltpu.VMEM((len(tiles), rows, width), BF16),
             pltpu.SemaphoreType.DMA((len(tiles),)),
@@ -512,10 +518,9 @@
         out_shape=[
             jax.ShapeDtypeStruct((share, channels), F32),
             jax.ShapeDtypeStruct((share, channels), BF16),
-            pltpu.VMEM(d_pre.shape, d_pre.dtype),
             jax.ShapeDtypeStruct(token.shape, token.dtype),
         ],
-        input_output_aliases={1: 3, 2: 2},
+        input_output_aliases={1: 2},
         compiler_params=pltpu.CompilerParams(vmem_limit_bytes=VMEM_LIMIT),
         cost_estimate=pl.CostEstimate(
             flops=2 * len(tiles) * rows * width * channels,
@@ -544,13 +549,16 @@
         return (z * ys + y) * cs + c
 
     every = [(z, y, c) for z in range(zs) for y in range(ys) for c in range(cs)]
+    def pair(bits):
+        return [(at(*i), at(i[0] ^ bits, i[1], i[2])) for i in every]
+
     core = [(at(*i), at(i[0], i[1], i[2] ^ 1)) for i in every]
     row = [(at(*i), at(i[0], i[1] ^ 1, i[2])) for i in every]
 
     def deep(step):
         return [(at(*i), at((i[0] + step) % zs, i[1], i[2])) for i in every]
 
-    return core, row, deep
+    return core, row, deep, pair
 
 
 def together(*values):
@@ -588,38 +596,56 @@
         mask, pooled, token = forward_chunk(where, token, tile_rows, [gathered], None, True, positions)
     else:
         zs, ys, cs = shape
-        core, row, deep = moves(shape)
+        core, row, deep, pair = moves(shape)
         z, y, c = me // (ys * cs), me // cs % ys, me % cs
-        place = [y * cs + c, y * cs + (c ^ 1), (y ^ 1) * cs + c, (y ^ 1) * cs + (c ^ 1)]
         own_parts, away_parts = [], []
-        acc, mine = None, conv_weight
-        across = send(mine, row)
-        waiting, groups, last = [], [], zs - 1
+
+        def block(step, near, pieces):
+            spot = (z - step) % zs * ys + (y if near else y ^ 1)
+            return spot, pieces
+
+        mine, across, mine_core = conv_weight, send(conv_weight, row), send(conv_weight, core)
+        acc, waiting, last = None, [], zs - 1
         for step in range(zs):
             if step < last:
                 ahead = send(mine, deep(1))
+                extra = []
                 if step < 2:
-                    own_part, away_part = split_inputs(c, tile_rows, cs, share, step, 2)
-                    across, ahead, token, own_part, away_part = together(across, ahead, token, own_part, away_part)
-                    own_parts.append(own_part)
-                    away_parts.append(send(away_part, core))
-                else:
-                    across, ahead, token, away_parts[0] = together(across, ahead, token, away_parts[0])
-                ahead_across = send(ahead, row)
-            waiting += [mine, send(mine, core), across, send(across, core)]
-            groups.append((z - step) % zs)
+                    extra += split_inputs(c, tile_rows, cs, share, step, 2)
+                if step > 0:
+                    extra.append(away_parts[step - 1])
+                    extra.append(across_core)
+                across, ahead, mine_core, token, *extra = together(across, ahead, mine_core, token, *extra)
+                if step > 0:
+                    landed = extra.pop()
+                    if waiting:
+                        waiting[-1][1][1] = landed
+                    away_parts[step - 1] = in_hbm(extra.pop())
+                ahead_across, ahead_core = send(ahead, row), send(ahead, core)
+                across_core = send(across, core)
+                waiting.append(block(step, True, [mine, mine_core]))
+                waiting.append(block(step, False, [across, across_core]))
+                if step < 2:
+                    own_parts.append(extra[0])
+                    if step == 1:
+                        across_core, extra[1] = together(across_core, extra[1])
+                        waiting[-1] = block(step, False, [across, across_core])
+                    away_parts.append(send(extra[1], core))
+                if step == last - 1:
+                    waiting.append(block(last, True, [ahead, ahead_core]))
+                mine, across, mine_core = ahead, ahead_across, ahead_core
+            else:
+                across, token = together(across, token)
+                waiting.append(block(last, False, [across, send(across, core)]))
             if step > 0:
-                spots = [i * ys * cs + at for i in range(len(groups)) for at in place]
-                where = jnp.stack([*groups, *spots]).astype(jnp.int32)
+                groups = [spot for spot, _ in waiting]
+                order = [i * cs + (c ^ k) for i in range(len(groups)) for k in range(cs)]
+                where = jnp.stack([*groups, *order]).astype(jnp.int32)
+                pieces = [piece for _, pair in waiting for piece in pair]
                 *out, token = forward_chunk(
-                    where, token, tile_rows, waiting, acc, step == last, positions, len(groups)
+                    where, token, tile_rows, pieces, acc, step == last, positions, len(groups)
                 )
-                acc = out[0]
-                waiting, groups = [], []
-            if step < last:
-                mine, across = ahead, ahead_across
-            if step == last - 1:
-                across, token, away_parts[1] = together(across, token, away_parts[1])
+                acc, waiting = out[0], []
         mask, pooled = out
 
     narrow, wide, packet = score(pooled, slide, attn_v, attn_u, attn_w_row, class_t, lanes)
@@ -657,37 +683,38 @@
     term_send, token = together(term_send, token)
     attn_got = send(term_send, row)
 
-    where = {step: jnp.stack([(z + step) % zs, y, c]).astype(jnp.int32) for step in (0, *steps)}
-    first, second, third = steps
+    where = [jnp.stack([z ^ bits, y, c]).astype(jnp.int32) for bits in range(zs)]
 
     parts = own_parts + away_parts
 
-    def chunk(step, d_pre, token):
-        return backward_chunk(where[step], token, parts, d_pre, ys, share)
-
-    near_first, over_first, d_pre, token = chunk(first, d_pre, token)
-    over_first, attn_got, token = together(over_first, attn_got, token)
-    y_first = send(over_first, row)
+    def chunk(bits, d_pre, token):
+        near, over, token = backward_chunk(where[bits], token, parts, d_pre, ys, share)
+        return near, over, d_pre, token
+
+    near_both, over_both, d_pre, token = chunk(3, d_pre, token)
+    over_both, attn_got, token = together(over_both, attn_got, token)
+    y_both = send(over_both, row)
+    near_far, over_far, d_pre, token = chunk(2, d_pre, token)
+    over_far, attn_got, token = together(over_far, attn_got, token)
+    y_far = send(over_far, row)
     own, *away = deep_fold(z[None], term_keep, attn_got, steps, extra)
-    *away, token = together(*away, token)
     attn = [send(block, deep(i)) for i, block in zip(steps, away)]
-    near_second, over_second, d_pre, token = chunk(second, d_pre, token)
-    over_second, y_first, token, *attn = together(over_second, y_first, token, *attn)
-    y_second = send(over_second, row)
-    out_first, token = together(sum_fold(near_first, [y_first], BF16), token)
-    z_first = send(out_first, deep(first))
-    near_third, over_third, d_pre, token = chunk(third, d_pre, token)
-    over_third, y_second, token = together(over_third, y_second, token)
-    y_third = send(over_third, row)
-    out_second, token = together(sum_fold(near_second, [y_second], BF16), token)
-    z_second = send(out_second, deep(second))
+    out_both, token, *_ = together(sum_fold(near_both, [y_both], BF16), token)
+    z_both = send(out_both, pair(1))
+    near_next, over_next, d_pre, token = chunk(1, d_pre, token)
+    over_next, y_far, token, *attn = together(over_next, y_far, token, *attn)
+    y_next = send(over_next, row)
+    half = share // 2
+    outs = [sum_fold(near_far[at], [y_far[at], z_both[at]], BF16) for at in (slice(half), slice(half, None))]
+    *outs, token = together(*outs, token)
+    z_far = [send(out, pair(2)) for out in outs]
     near_own, over_own, d_pre, token = chunk(0, d_pre, token)
-    over_own, y_third, z_first, token = together(over_own, y_third, z_first, token)
+    over_own, y_next, z_far[0], token = together(over_own, y_next, z_far[0], token)
     y_own = send(over_own, row)
-    out_third, z_second = together(sum_fold(near_third, [y_third], BF16), z_second)
-    z_third = send(out_third, deep(third))
+    z_next = send(sum_fold(near_next, [y_next], BF16), pair(1))
+    own, near_own = together(own, near_own)
     v_grad, u_grad, small = last_fold(own, attn, extra)
-    conv_grad = sum_fold(near_own, [y_own, z_first, z_second, z_third], F32)
+    conv_grad = sum_fold(near_own, [y_own, z_next, jnp.concatenate(z_far, axis=0)], F32)
     return (conv_grad, v_grad, u_grad, small[classes, :hidden], small[:classes].T, logits, loss)
 
 

time: 135 us -> 127 us (0.941)
  waiting for transfers between devices: 34.9 us -> 24.2 us
  starting transfers between devices: 29.5 us -> 31.1 us
    ppermute x36 -> x37, waiting for transfers between devices: 34.9 us -> 24.2 us  [send(): return lax.ppermute(x, 'dp', pairs)]
    ppermute x36 -> x37, starting transfers between devices: 29.5 us -> 31.1 us  [send(): return lax.ppermute(x, 'dp', pairs)]
  transfers between devices with their start and end apart: 36 -> 37, of which waited for: 16 -> 19; matrix products, arithmetic and copies ran while one was open for 2% -> 2% of each run, Pallas kernels for 38% -> 42%
where the time goes in v3:
time: 127 us
  Pallas kernels  64.6 us (51%)
  starting transfers between devices  31.1 us (24%)
  waiting for transfers between devices  24.2 us (19%)
  local copies, waits for them, and re-layouts  4.24 us (3%)
  other arithmetic  1.67 us (1%)
    ppermute x37, starting transfers between devices, send(): return lax.ppermute(x, 'dp', pairs)  31.1 us
    pallas_call x3, Pallas kernels, forward_chunk(): pl.pallas_call(functools.partial(forward_kernel, groups, pieces, first, l...  24.5 us
    ppermute x37, waiting for transfers between devices, send(): return lax.ppermute(x, 'dp', pairs)  24.2 us
    pallas_call x4, Pallas kernels, backward_chunk(): pl.pallas_call(functools.partial(backward_kernel, ys, len(tiles)), in_spe...  20.9 us
    pallas_call x2, Pallas kernels, split_inputs(): pl.pallas_call(functools.partial(split_kernel, cs, share), grid=(rows //...  13.5 us
    pallas_call x1, Pallas kernels, grads(): pl.pallas_call(functools.partial(grads_kernel, len(boxes), slides, shards...  4.19 us
  transfers between devices with their start and end apart: 37, of which 19 were waited for; matrix products, arithmetic and copies ran while one was open for 2% of the time, Pallas kernels for 42%

profile of v3, /device:TPU:0, one launch (start us, length us, event | category | flops | bytes accessed | tf_op | source)
XLA Modules:
  0.0 126.6 jit_solution(7116420947372505007)
XLA Ops:
  0.6 3.0 %collective-permute-start = (bf16[192,768]{1,0:T(8,128)(2,1)}, bf16[192,768]{1,0:T(8,128)(2,1)S(1)}, u32[]{:S(2)}, u32[]{:S(2)}) collective-permute-start(bf16[192,768]{1,0:T(8,128)(2,1)} %refs_0_.1), channel_id=1, source_target_pairs={{0,2},{1,3},{2,0},{3,1},{4,6},{5,7},{6,4},{7,5},{8,10},{9,11},{10,... | collective-permute-start | bytes 884744 | tf_op jit(solution)/shard_map/ppermute | solution.py:569
  3.7 1.6 %collective-permute-start.1 = (bf16[192,768]{1,0:T(8,128)(2,1)}, bf16[192,768]{1,0:T(8,128)(2,1)S(1)}, u32[]{:S(2)}, u32[]{:S(2)}) collective-permute-start(bf16[192,768]{1,0:T(8,128)(2,1)} %refs_0_.1), channel_id=1, source_target_pairs={{0,4},{1,5},{2,6},{3,7},{4,8},{5,9},{6,10},{7,11},{8,12},{9,13},{1... | collective-permute-start | bytes 884744 | tf_op jit(solution)/shard_map/ppermute | solution.py:569
  5.2 6.7 %split_inputs.2 = (bf16[1024,1536]{1,0:T(8,128)(2,1)}, bf16[1024,1536]{1,0:T(8,128)(2,1)}) custom-call(s32[1]{0:T(128)} %bitcast.3.where, bf16[2048,3072]{1,0:T(8,128)(2,1)} %bitcast.46), custom_call_target="tpu_custom_call" | custom-call | tf_op jit(solution)/shard_map/split_inputs/pallas_call | solution.py:50
  11.9 2.3 %collective-permute-done.1.refs_4_ = bf16[192,768]{1,0:T(8,128)(2,1)S(1)} collective-permute-done((bf16[192,768]{1,0:T(8,128)(2,1)}, bf16[192,768]{1,0:T(8,128)(2,1)S(1)}, u32[]{:S(2)}, u32[]{:S(2)}) %collective-permute-start.1) | collective-permute-done | bytes 294944 | tf_op jit(solution)/shard_map/ppermute | solution.py:569
  15.3 6.8 %split_inputs.3 = (bf16[1024,1536]{1,0:T(8,128)(2,1)}, bf16[1024,1536]{1,0:T(8,128)(2,1)}) custom-call(s32[1]{0:T(128)} %bitcast.3.where, bf16[2048,3072]{1,0:T(8,128)(2,1)} %bitcast.47), custom_call_target="tpu_custom_call" | custom-call | tf_op jit(solution)/shard_map/split_inputs/pallas_call | solution.py:50
  23.7 2.0 %collective-permute-done.4.refs_0_ = bf16[192,768]{1,0:T(8,128)(2,1)S(1)} collective-permute-done((bf16[192,768]{1,0:T(8,128)(2,1)S(1)}, bf16[192,768]{1,0:T(8,128)(2,1)S(1)}, u32[]{:S(2)}, u32[]{:S(2)}) %collective-permute-start.4) | collective-permute-done | bytes 294944 | tf_op jit(solution)/shard_map/ppermute | solution.py:569
  31.2 9.0 %section_forward.3 = (f32[2048,768]{1,0:T(8,128)}, f32[8,128]{1,0:T(8,128)S(1)}) custom-call(s32[12]{0:T(128)S(1)} %stack.122.where, f32[8,128]{1,0:T(8,128)S(1)} %broadcast_in_dim.43.token, bf16[2048,3072]{1,0:T(8,128)(2,1)} %bitcast.48, bf16[192,768]{1,0:T(8,128)(2,1)S(1)} %copy-done.3, ...), custom_call_target="tpu_custom_call", output_to_operand_aliasing={{1}: (1, {})} | custom-call | flops 4831838208 | bytes 6291456 | tf_op jit(solution)/shard_map/section_forward/pallas_call | solution.py:162
  42.8 9.2 %section_forward.4 = (f32[2048,768]{1,0:T(8,128)}, f32[8,128]{1,0:T(8,128)S(1)}) custom-call(s32[9]{0:T(128)S(1)} %stack.126.where, f32[8,128]{1,0:T(8,128)S(1)} %get-tuple-element.114.token, bf16[2048,3072]{1,0:T(8,128)(2,1)} %bitcast.49, bf16[192,768]{1,0:T(8,128)(2,1)S(1)} %collective-permute-done.4.refs_0_, ...), custom_call_target="tpu_custom_call", output_to_operand_aliasing={{0}: (9, {}), {1}: (1, {})} | custom-call | flops 3623878656 | bytes 4718592 | tf_op jit(solution)/shard_map/section_forward/pallas_call | solution.py:162
  53.7 6.3 %section_forward.5 = (bf16[2048,768]{1,0:T(8,128)(2,1)}, f32[32,768]{1,0:T(8,128)S(1)}, f32[8,128]{1,0:T(8,128)S(1)}) custom-call(s32[3]{0:T(128)S(1)} %pad_add_fusion.where, f32[8,128]{1,0:T(8,128)S(1)} %get-tuple-element.119.token, bf16[2048,3072]{1,0:T(8,128)(2,1)} %bitcast.50, ...), custom_call_target="tpu_custom_call", output_to_operand_aliasing={{2}: (1, {})} | custom-call | flops 1207959552 | bytes 1572864 | tf_op jit(solution)/shard_map/section_forward/pallas_call | solution.py:162
  62.8 3.0 %collective-permute-done.18 = f32[8,128]{1,0:T(8,128)S(1)} collective-permute-done((f32[8,128]{1,0:T(8,128)S(1)}, f32[8,128]{1,0:T(8,128)S(1)}, u32[]{:S(2)}, u32[]{:S(2)}) %collective-permute-start.18) | collective-permute-done | bytes 4128 | tf_op jit(solution)/shard_map/ppermute | solution.py:569
  66.7 3.6 %collective-permute-start.21 = (f32[8,128]{1,0:T(8,128)S(1)}, f32[8,128]{1,0:T(8,128)S(1)}, u32[]{:S(2)}, u32[]{:S(2)}) collective-permute-start(f32[8,128]{1,0:T(8,128)S(1)} %add_select_fusion.refs_2_), channel_id=1, source_target_pairs={{0,4},{1,5},{2,6},{3,7},{4,8},{5,9},{6,10},{7,11},{8,12},{9,13},{1... | collective-permute-start | bytes 12296 | tf_op jit(solution)/shard_map/ppermute | solution.py:569
  72.2 1.7 %collective-permute-done.22.refs_5_ = f32[8,128]{1,0:T(8,128)S(1)} collective-permute-done((f32[8,128]{1,0:T(8,128)S(1)}, f32[8,128]{1,0:T(8,128)S(1)}, u32[]{:S(2)}, u32[]{:S(2)}) %collective-permute-start.22) | collective-permute-done | bytes 4128 | tf_op jit(solution)/shard_map/ppermute | solution.py:569
  74.0 4.2 %head_grads.1 = (bf16[4096,768]{1,0:T(8,128)(2,1)S(1)}, f32[208,768]{1,0:T(8,128)S(1)}, bf16[208,768]{1,0:T(8,128)(2,1)S(1)}, f32[8,128]{1,0:T(8,128)S(1)}, f32[8,128]{1,0:T(8,128)S(1)}) custom-call(s32[3]{0:T(128)S(1)} %get-tuple-element.191.where, bf16[2048,768]{1,0:T(8,128)(2,1)} %get-tuple-element.127.refs_0_, ...), custom_call_target="tpu_custom_call" | custom-call | tf_op jit(solution)/shard_map/head_grads/pallas_call | solution.py:454
  79.0 5.3 %section_backward.4 = (f32[192,768]{1,0:T(8,128)S(1)}, bf16[192,768]{1,0:T(8,128)(2,1)S(1)}, f32[8,128]{1,0:T(8,128)S(1)}) custom-call(s32[3]{0:T(128)S(1)} %get-tuple-element.193.where, f32[8,128]{1,0:T(8,128)S(1)} %get-tuple-element.134.token, bf16[4096,768]{1,0:T(8,128)(2,1)S(1)} %get-tuple-element.135.d_pre, ...), custom_call_target="tpu_custom_call", output_to_operand_aliasing={{2}: (1, {})} | custom-call | flops 2415919104 | bytes 3145728 | tf_op jit(solution)/shard_map/section_backward/pallas_call | solution.py:510
  84.3 1.8 %collective-permute-done.25.got = bf16[208,768]{1,0:T(8,128)(2,1)S(1)} collective-permute-done((bf16[208,768]{1,0:T(8,128)(2,1)S(1)}, bf16[208,768]{1,0:T(8,128)(2,1)S(1)}, u32[]{:S(2)}, u32[]{:S(2)}) %collective-permute-start.25) | collective-permute-done | bytes 319520 | tf_op jit(solution)/shard_map/ppermute | solution.py:569
  86.7 5.2 %section_backward.5 = (f32[192,768]{1,0:T(8,128)S(1)}, bf16[192,768]{1,0:T(8,128)(2,1)S(1)}, f32[8,128]{1,0:T(8,128)S(1)}) custom-call(s32[3]{0:T(128)S(1)} %get-tuple-element.192.where, f32[8,128]{1,0:T(8,128)S(1)} %get-tuple-element.143.token, bf16[4096,768]{1,0:T(8,128)(2,1)S(1)} %get-tuple-element.135.d_pre, ...), custom_call_target="tpu_custom_call", output_to_operand_aliasing={{2}: (1, {})} | custom-call | flops 2415919104 | bytes 3145728 | tf_op jit(solution)/shard_map/section_backward/pallas_call | solution.py:510
  93.8 2.3 %collective-permute-start.31 = (bf16[192,768]{1,0:T(8,128)(2,1)S(1)}, bf16[192,768]{1,0:T(8,128)(2,1)S(1)}, u32[]{:S(2)}, u32[]{:S(2)}) collective-permute-start(bf16[192,768]{1,0:T(8,128)(2,1)S(1)} %add_convert_fusion.1), channel_id=1, source_target_pairs={{0,4},{1,5},{2,6},{3,7},{4,0},{5,1},{6,2},{7,3},{8,12},{9,13},{10,... | collective-permute-start | bytes 884744 | tf_op jit(solution)/shard_map/ppermute | solution.py:569
  97.4 2.4 %collective-permute-start.28 = (bf16[64,768]{1,0:T(8,128)(2,1)S(1)}, bf16[64,768]{1,0:T(8,128)(2,1)S(1)}, u32[]{:S(2)}, u32[]{:S(2)}) collective-permute-start(bf16[64,768]{1,0:T(8,128)(2,1)S(1)} %get-tuple-element.157), channel_id=1, source_target_pairs={{0,8},{1,9},{2,10},{3,11},{4,12},{5,13},{6,14},{7,15},{8,0},{9,1},... | collective-permute-start | bytes 294920 | tf_op jit(solution)/shard_map/ppermute | solution.py:569
  99.8 3.8 %collective-permute-start.30 = (bf16[64,768]{1,0:T(8,128)(2,1)S(1)}, bf16[64,768]{1,0:T(8,128)(2,1)S(1)}, u32[]{:S(2)}, u32[]{:S(2)}) collective-permute-start(bf16[64,768]{1,0:T(8,128)(2,1)S(1)} %get-tuple-element.159), channel_id=1, source_target_pairs={{0,12},{1,13},{2,14},{3,15},{4,0},{5,1},{6,2},{7,3},{8,4},{9,5},{1... | collective-permute-start | bytes 294920 | tf_op jit(solution)/shard_map/ppermute | solution.py:569
  103.6 5.2 %section_backward.6 = (f32[192,768]{1,0:T(8,128)S(1)}, bf16[192,768]{1,0:T(8,128)(2,1)S(1)}, f32[8,128]{1,0:T(8,128)S(1)}) custom-call(s32[3]{0:T(128)S(1)} %get-tuple-element.194.where, f32[8,128]{1,0:T(8,128)S(1)} %get-tuple-element.153.token, bf16[4096,768]{1,0:T(8,128)(2,1)S(1)} %get-tuple-element.135.d_pre, ...), custom_call_target="tpu_custom_call", output_to_operand_aliasing={{2}: (1, {})} | custom-call | flops 2415919104 | bytes 3145728 | tf_op jit(solution)/shard_map/section_backward/pallas_call | solution.py:510
  109.9 5.2 %section_backward.7 = (f32[192,768]{1,0:T(8,128)S(1)}, bf16[192,768]{1,0:T(8,128)(2,1)S(1)}, f32[8,128]{1,0:T(8,128)S(1)}) custom-call(s32[3]{0:T(128)S(1)} %add_add_fusion.3.where, f32[8,128]{1,0:T(8,128)S(1)} %get-tuple-element.163.token, bf16[4096,768]{1,0:T(8,128)(2,1)S(1)} %get-tuple-element.135.d_pre, ...), custom_call_target="tpu_custom_call", output_to_operand_aliasing={{2}: (1, {})} | custom-call | flops 2415919104 | bytes 3145728 | tf_op jit(solution)/shard_map/section_backward/pallas_call | solution.py:510
  115.1 2.2 %collective-permute-start.36 = (bf16[96,768]{1,0:T(8,128)(2,1)S(1)}, bf16[96,768]{1,0:T(8,128)(2,1)S(1)}, u32[]{:S(2)}, u32[]{:S(2)}) collective-permute-start(bf16[96,768]{1,0:T(8,128)(2,1)S(1)} %get-tuple-element.173), channel_id=1, source_target_pairs={{0,8},{1,9},{2,10},{3,11},{4,12},{5,13},{6,14},{7,15},{8,0},{9,1},... | collective-permute-start | bytes 442376 | tf_op jit(solution)/shard_map/ppermute | solution.py:569
  118.9 1.8 %collective-permute-start.34 = (bf16[192,768]{1,0:T(8,128)(2,1)S(1)}, bf16[192,768]{1,0:T(8,128)(2,1)S(1)}, u32[]{:S(2)}, u32[]{:S(2)}) collective-permute-start(bf16[192,768]{1,0:T(8,128)(2,1)S(1)} %get-tuple-element.169), channel_id=1, source_target_pairs={{0,2},{1,3},{2,0},{3,1},{4,6},{5,7},{6,4},{7,5},{8,10},{9,11},{10,... | collective-permute-start | bytes 884744 | tf_op jit(solution)/shard_map/ppermute | solution.py:569
  122.8 2.8 %collective-permute-done.35 = bf16[192,768]{1,0:T(8,128)(2,1)S(1)} collective-permute-done((bf16[192,768]{1,0:T(8,128)(2,1)S(1)}, bf16[192,768]{1,0:T(8,128)(2,1)S(1)}, u32[]{:S(2)}, u32[]{:S(2)}) %collective-permute-start.35) | collective-permute-done | bytes 294944 | tf_op jit(solution)/shard_map/ppermute | solution.py:569
  (108 shorter events, 28.3 us)
Async XLA Ops:
  0.6 11.3 %collective-permute-start = (bf16[192,768]{1,0:T(8,128)(2,1)}, bf16[192,768]{1,0:T(8,128)(2,1)S(1)}, u32[]{:S(2)}, u32[]{:S(2)}) collective-permute-start(bf16[192,768]{1,0:T(8,128)(2,1)} %refs_0_.1), channel_id=1, source_target_pairs={{0,2},{1,3},{2,0},{3,1},{4,6},{5,7},{6,4},{7,5},{8,10},{9,11},{10,... | collective-permute-start | bytes 884744 | tf_op jit(solution)/shard_map/ppermute | solution.py:569
  3.7 10.6 %collective-permute-start.1 = (bf16[192,768]{1,0:T(8,128)(2,1)}, bf16[192,768]{1,0:T(8,128)(2,1)S(1)}, u32[]{:S(2)}, u32[]{:S(2)}) collective-permute-start(bf16[192,768]{1,0:T(8,128)(2,1)} %refs_0_.1), channel_id=1, source_target_pairs={{0,4},{1,5},{2,6},{3,7},{4,8},{5,9},{6,10},{7,11},{8,12},{9,13},{1... | collective-permute-start | bytes 884744 | tf_op jit(solution)/shard_map/ppermute | solution.py:569
  5.2 9.0 %collective-permute-start.2 = (bf16[192,768]{1,0:T(8,128)(2,1)}, bf16[192,768]{1,0:T(8,128)(2,1)S(1)}, u32[]{:S(2)}, u32[]{:S(2)}) collective-permute-start(bf16[192,768]{1,0:T(8,128)(2,1)} %refs_0_.1), channel_id=1, source_target_pairs={{0,1},{1,0},{2,3},{3,2},{4,5},{5,4},{6,7},{7,6},{8,9},{9,8},{10,11... | collective-permute-start | bytes 884744 | tf_op jit(solution)/shard_map/ppermute | solution.py:569
  14.2 11.5 %collective-permute-start.6 = (bf16[1024,1536]{1,0:T(8,128)(2,1)}, bf16[1024,1536]{1,0:T(8,128)(2,1)S(1)}, u32[]{:S(2)}, u32[]{:S(2)}) collective-permute-start(bf16[1024,1536]{1,0:T(8,128)(2,1)} %get-tuple-element.101), channel_id=1, source_target_pairs={{0,1},{1,0},{2,3},{3,2},{4,5},{5,4},{6,7},{7,6},{8,9},{9,8},{10,11... | collective-permute-start | bytes 9437192 | tf_op jit(solution)/shard_map/ppermute | solution.py:569
  14.2 9.4 %collective-permute-start.3 = (bf16[192,768]{1,0:T(8,128)(2,1)S(1)}, bf16[192,768]{1,0:T(8,128)(2,1)S(1)}, u32[]{:S(2)}, u32[]{:S(2)}) collective-permute-start(bf16[192,768]{1,0:T(8,128)(2,1)S(1)} %collective-permute-done.1.refs_4_), channel_id=1, source_target_pairs={{0,2},{1,3},{2,0},{3,1},{4,6},{5,7},{6,4},{7,5},{8,10},{9,11},{10,... | collective-permute-start | bytes 884744 | tf_op jit(solution)/shard_map/ppermute | solution.py:569
  14.8 10.9 %collective-permute-start.4 = (bf16[192,768]{1,0:T(8,128)(2,1)S(1)}, bf16[192,768]{1,0:T(8,128)(2,1)S(1)}, u32[]{:S(2)}, u32[]{:S(2)}) collective-permute-start(bf16[192,768]{1,0:T(8,128)(2,1)S(1)} %collective-permute-done.1.refs_4_), channel_id=1, source_target_pairs={{0,4},{1,5},{2,6},{3,7},{4,8},{5,9},{6,10},{7,11},{8,12},{9,13},{1... | collective-permute-start | bytes 884744 | tf_op jit(solution)/shard_map/ppermute | solution.py:569
  14.8 10.9 %collective-permute-start.5 = (bf16[192,768]{1,0:T(8,128)(2,1)S(1)}, bf16[192,768]{1,0:T(8,128)(2,1)S(1)}, u32[]{:S(2)}, u32[]{:S(2)}) collective-permute-start(bf16[192,768]{1,0:T(8,128)(2,1)S(1)} %collective-permute-done.1.refs_4_), channel_id=1, source_target_pairs={{0,1},{1,0},{2,3},{3,2},{4,5},{5,4},{6,7},{7,6},{8,9},{9,8},{10,11... | collective-permute-start | bytes 884744 | tf_op jit(solution)/shard_map/ppermute | solution.py:569
  15.0 10.7 %collective-permute-start.7 = (bf16[192,768]{1,0:T(8,128)(2,1)S(1)}, bf16[192,768]{1,0:T(8,128)(2,1)S(1)}, u32[]{:S(2)}, u32[]{:S(2)}) collective-permute-start(bf16[192,768]{1,0:T(8,128)(2,1)S(1)} %collective-permute-done.refs_2_), channel_id=1, source_target_pairs={{0,1},{1,0},{2,3},{3,2},{4,5},{5,4},{6,7},{7,6},{8,9},{9,8},{10,11... | collective-permute-start | bytes 884744 | tf_op jit(solution)/shard_map/ppermute | solution.py:569
  28.1 12.8 %collective-permute-start.12 = (bf16[1024,1536]{1,0:T(8,128)(2,1)}, bf16[1024,1536]{1,0:T(8,128)(2,1)}, u32[]{:S(2)}, u32[]{:S(2)}) collective-permute-start(bf16[1024,1536]{1,0:T(8,128)(2,1)} %get-tuple-element.112), channel_id=1, source_target_pairs={{0,1},{1,0},{2,3},{3,2},{4,5},{5,4},{6,7},{7,6},{8,9},{9,8},{10,11... | collective-permute-start | bytes 9437192 | tf_op jit(solution)/shard_map/ppermute | solution.py:569
  28.3 11.9 %collective-permute-start.10 = (bf16[192,768]{1,0:T(8,128)(2,1)S(1)}, bf16[192,768]{1,0:T(8,128)(2,1)S(1)}, u32[]{:S(2)}, u32[]{:S(2)}) collective-permute-start(bf16[192,768]{1,0:T(8,128)(2,1)S(1)} %collective-permute-done.4.refs_0_), channel_id=1, source_target_pairs={{0,1},{1,0},{2,3},{3,2},{4,5},{5,4},{6,7},{7,6},{8,9},{9,8},{10,11... | collective-permute-start | bytes 884744 | tf_op jit(solution)/shard_map/ppermute | solution.py:569
  28.7 11.5 %collective-permute-start.8 = (bf16[192,768]{1,0:T(8,128)(2,1)S(1)}, bf16[192,768]{1,0:T(8,128)(2,1)S(1)}, u32[]{:S(2)}, u32[]{:S(2)}) collective-permute-start(bf16[192,768]{1,0:T(8,128)(2,1)S(1)} %collective-permute-done.4.refs_0_), channel_id=1, source_target_pairs={{0,2},{1,3},{2,0},{3,1},{4,6},{5,7},{6,4},{7,5},{8,10},{9,11},{10,... | collective-permute-start | bytes 884744 | tf_op jit(solution)/shard_map/ppermute | solution.py:569
  30.3 10.6 %collective-permute-start.9 = (bf16[192,768]{1,0:T(8,128)(2,1)S(1)}, bf16[192,768]{1,0:T(8,128)(2,1)S(1)}, u32[]{:S(2)}, u32[]{:S(2)}) collective-permute-start(bf16[192,768]{1,0:T(8,128)(2,1)S(1)} %collective-permute-done.4.refs_0_), channel_id=1, source_target_pairs={{0,4},{1,5},{2,6},{3,7},{4,8},{5,9},{6,10},{7,11},{8,12},{9,13},{1... | collective-permute-start | bytes 884744 | tf_op jit(solution)/shard_map/ppermute | solution.py:569
  41.4 10.6 %collective-permute-start.13 = (bf16[192,768]{1,0:T(8,128)(2,1)S(1)}, bf16[192,768]{1,0:T(8,128)(2,1)S(1)}, u32[]{:S(2)}, u32[]{:S(2)}) collective-permute-start(bf16[192,768]{1,0:T(8,128)(2,1)S(1)} %collective-permute-done.9.refs_4_), channel_id=1, source_target_pairs={{0,2},{1,3},{2,0},{3,1},{4,6},{5,7},{6,4},{7,5},{8,10},{9,11},{10,... | collective-permute-start | bytes 884744 | tf_op jit(solution)/shard_map/ppermute | solution.py:569
  65.9 8.1 %collective-permute-start.19 = (bf16[2048,768]{1,0:T(8,128)(2,1)}, bf16[2048,768]{1,0:T(8,128)(2,1)}, u32[]{:S(2)}, u32[]{:S(2)}) collective-permute-start(bf16[2048,768]{1,0:T(8,128)(2,1)} %get-tuple-element.127.refs_0_), channel_id=1, source_target_pairs={{0,1},{1,0},{2,3},{3,2},{4,5},{5,4},{6,7},{7,6},{8,9},{9,8},{10,11... | collective-permute-start | bytes 9437192 | tf_op jit(solution)/shard_map/ppermute | solution.py:569
  65.9 8.1 %collective-permute-start.24 = (f32[32,2048]{1,0:T(8,128)S(1)}, f32[32,2048]{1,0:T(8,128)S(1)}, u32[]{:S(2)}, u32[]{:S(2)}) collective-permute-start(f32[32,2048]{1,0:T(8,128)S(1)} %get-tuple-element.130.refs_8_), channel_id=1, source_target_pairs={{0,1},{1,0},{2,3},{3,2},{4,5},{5,4},{6,7},{7,6},{8,9},{9,8},{10,11... | collective-permute-start | bytes 786440 | tf_op jit(solution)/shard_map/ppermute | solution.py:569
  78.2 7.9 %collective-permute-start.25 = (bf16[208,768]{1,0:T(8,128)(2,1)S(1)}, bf16[208,768]{1,0:T(8,128)(2,1)S(1)}, u32[]{:S(2)}, u32[]{:S(2)}) collective-permute-start(bf16[208,768]{1,0:T(8,128)(2,1)S(1)} %get-tuple-element.141), channel_id=1, source_target_pairs={{0,2},{1,3},{2,0},{3,1},{4,6},{5,7},{6,4},{7,5},{8,10},{9,11},{10,... | collective-permute-start | bytes 958472 | tf_op jit(solution)/shard_map/ppermute | solution.py:569
  92.0 16.8 %collective-permute-start.27 = (bf16[192,768]{1,0:T(8,128)(2,1)S(1)}, bf16[192,768]{1,0:T(8,128)(2,1)S(1)}, u32[]{:S(2)}, u32[]{:S(2)}) collective-permute-start(bf16[192,768]{1,0:T(8,128)(2,1)S(1)} %get-tuple-element.155), channel_id=1, source_target_pairs={{0,2},{1,3},{2,0},{3,1},{4,6},{5,7},{6,4},{7,5},{8,10},{9,11},{10,... | collective-permute-start | bytes 884744 | tf_op jit(solution)/shard_map/ppermute | solution.py:569
  93.8 15.1 %collective-permute-start.31 = (bf16[192,768]{1,0:T(8,128)(2,1)S(1)}, bf16[192,768]{1,0:T(8,128)(2,1)S(1)}, u32[]{:S(2)}, u32[]{:S(2)}) collective-permute-start(bf16[192,768]{1,0:T(8,128)(2,1)S(1)} %add_convert_fusion.1), channel_id=1, source_target_pairs={{0,4},{1,5},{2,6},{3,7},{4,0},{5,1},{6,2},{7,3},{8,12},{9,13},{10,... | collective-permute-start | bytes 884744 | tf_op jit(solution)/shard_map/ppermute | solution.py:569
  97.4 11.4 %collective-permute-start.28 = (bf16[64,768]{1,0:T(8,128)(2,1)S(1)}, bf16[64,768]{1,0:T(8,128)(2,1)S(1)}, u32[]{:S(2)}, u32[]{:S(2)}) collective-permute-start(bf16[64,768]{1,0:T(8,128)(2,1)S(1)} %get-tuple-element.157), channel_id=1, source_target_pairs={{0,8},{1,9},{2,10},{3,11},{4,12},{5,13},{6,14},{7,15},{8,0},{9,1},... | collective-permute-start | bytes 294920 | tf_op jit(solution)/shard_map/ppermute | solution.py:569
  99.8 9.0 %collective-permute-start.29 = (bf16[64,768]{1,0:T(8,128)(2,1)S(1)}, bf16[64,768]{1,0:T(8,128)(2,1)S(1)}, u32[]{:S(2)}, u32[]{:S(2)}) collective-permute-start(bf16[64,768]{1,0:T(8,128)(2,1)S(1)} %get-tuple-element.158), channel_id=1, source_target_pairs={{0,4},{1,5},{2,6},{3,7},{4,8},{5,9},{6,10},{7,11},{8,12},{9,13},{1... | collective-permute-start | bytes 294920 | tf_op jit(solution)/shard_map/ppermute | solution.py:569
  99.8 9.0 %collective-permute-start.30 = (bf16[64,768]{1,0:T(8,128)(2,1)S(1)}, bf16[64,768]{1,0:T(8,128)(2,1)S(1)}, u32[]{:S(2)}, u32[]{:S(2)}) collective-permute-start(bf16[64,768]{1,0:T(8,128)(2,1)S(1)} %get-tuple-element.159), channel_id=1, source_target_pairs={{0,12},{1,13},{2,14},{3,15},{4,0},{5,1},{6,2},{7,3},{8,4},{9,5},{1... | collective-permute-start | bytes 294920 | tf_op jit(solution)/shard_map/ppermute | solution.py:569
  108.8 9.1 %collective-permute-start.32 = (bf16[192,768]{1,0:T(8,128)(2,1)S(1)}, bf16[192,768]{1,0:T(8,128)(2,1)S(1)}, u32[]{:S(2)}, u32[]{:S(2)}) collective-permute-start(bf16[192,768]{1,0:T(8,128)(2,1)S(1)} %get-tuple-element.167), channel_id=1, source_target_pairs={{0,2},{1,3},{2,0},{3,1},{4,6},{5,7},{6,4},{7,5},{8,10},{9,11},{10,... | collective-permute-start | bytes 884744 | tf_op jit(solution)/shard_map/ppermute | solution.py:569
  109.0 9.7 %collective-permute-start.33 = (bf16[96,768]{1,0:T(8,128)(2,1)S(1)}, bf16[96,768]{1,0:T(8,128)(2,1)S(1)}, u32[]{:S(2)}, u32[]{:S(2)}) collective-permute-start(bf16[96,768]{1,0:T(8,128)(2,1)S(1)} %get-tuple-element.168), channel_id=1, source_target_pairs={{0,8},{1,9},{2,10},{3,11},{4,12},{5,13},{6,14},{7,15},{8,0},{9,1},... | collective-permute-start | bytes 442376 | tf_op jit(solution)/shard_map/ppermute | solution.py:569
  115.1 7.7 %collective-permute-start.36 = (bf16[96,768]{1,0:T(8,128)(2,1)S(1)}, bf16[96,768]{1,0:T(8,128)(2,1)S(1)}, u32[]{:S(2)}, u32[]{:S(2)}) collective-permute-start(bf16[96,768]{1,0:T(8,128)(2,1)S(1)} %get-tuple-element.173), channel_id=1, source_target_pairs={{0,8},{1,9},{2,10},{3,11},{4,12},{5,13},{6,14},{7,15},{8,0},{9,1},... | collective-permute-start | bytes 442376 | tf_op jit(solution)/shard_map/ppermute | solution.py:569
  (24 other events, 133.0 us)

commit v4 on v3

--- a/solution.py
+++ b/solution.py
@@ -704,7 +704,7 @@
     near_next, over_next, d_pre, token = chunk(1, d_pre, token)
     over_next, y_far, token, *attn = together(over_next, y_far, token, *attn)
     y_next = send(over_next, row)
-    half = share // 2
+    half = share // 48 * 16
     outs = [sum_fold(near_far[at], [y_far[at], z_both[at]], BF16) for at in (slice(half), slice(half, None))]
     *outs, token = together(*outs, token)
     z_far = [send(out, pair(2)) for out in outs]
@@ -712,7 +712,7 @@
     over_own, y_next, z_far[0], token = together(over_own, y_next, z_far[0], token)
     y_own = send(over_own, row)
     z_next = send(sum_fold(near_next, [y_next], BF16), pair(1))
-    own, near_own = together(own, near_own)
+    own, z_far[1] = together(own, z_far[1])
     v_grad, u_grad, small = last_fold(own, attn, extra)
     conv_grad = sum_fold(near_own, [y_own, z_next, jnp.concatenate(z_far, axis=0)], F32)
     return (conv_grad, v_grad, u_grad, small[classes, :hidden], small[:classes].T, logits, loss)

time: 127 us -> 131 us (1.031)
  waiting for transfers between devices: 24.2 us -> 28.8 us
    ppermute x37, waiting for transfers between devices: 24.2 us -> 28.8 us  [send(): return lax.ppermute(x, 'dp', pairs)]
  transfers between devices with their start and end apart: 37 -> 37, of which waited for: 19 -> 18; matrix products, arithmetic and copies ran while one was open for 2% -> 2% of each run, Pallas kernels for 42% -> 41%
where the time goes in v4:
time: 131 us; the launch traced here: 130 us
  Pallas kernels  64.6 us (49%)
  starting transfers between devices  30.2 us (23%)
  waiting for transfers between devices  28.8 us (22%)
  local copies, waits for them, and re-layouts  4.24 us (3%)
  other arithmetic  1.65 us (1%)
    ppermute x37, starting transfers between devices, send(): return lax.ppermute(x, 'dp', pairs)  30.2 us
    ppermute x37, waiting for transfers between devices, send(): return lax.ppermute(x, 'dp', pairs)  28.8 us
    pallas_call x3, Pallas kernels, forward_chunk(): pl.pallas_call(functools.partial(forward_kernel, groups, pieces, first, l...  24.5 us
    pallas_call x4, Pallas kernels, backward_chunk(): pl.pallas_call(functools.partial(backward_kernel, ys, len(tiles)), in_spe...  20.9 us
    pallas_call x2, Pallas kernels, split_inputs(): pl.pallas_call(functools.partial(split_kernel, cs, share), grid=(rows //...  13.4 us
    pallas_call x1, Pallas kernels, grads(): pl.pallas_call(functools.partial(grads_kernel, len(boxes), slides, shards...  4.19 us
  transfers between devices with their start and end apart: 37, of which 18 were waited for; matrix products, arithmetic and copies ran while one was open for 2% of the time, Pallas kernels for 41%

profile of v4, /device:TPU:0, one launch (start us, length us, event | category | flops | bytes accessed | tf_op | source)
XLA Modules:
  0.0 130.4 jit_solution(1544194711454511532)
XLA Ops:
  0.6 3.0 %collective-permute-start = (bf16[192,768]{1,0:T(8,128)(2,1)}, bf16[192,768]{1,0:T(8,128)(2,1)S(1)}, u32[]{:S(2)}, u32[]{:S(2)}) collective-permute-start(bf16[192,768]{1,0:T(8,128)(2,1)} %refs_0_.1), channel_id=1, source_target_pairs={{0,2},{1,3},{2,0},{3,1},{4,6},{5,7},{6,4},{7,5},{8,10},{9,11},{10,... | collective-permute-start | bytes 884744 | tf_op jit(solution)/shard_map/ppermute | solution.py:569
  3.7 1.6 %collective-permute-start.1 = (bf16[192,768]{1,0:T(8,128)(2,1)}, bf16[192,768]{1,0:T(8,128)(2,1)S(1)}, u32[]{:S(2)}, u32[]{:S(2)}) collective-permute-start(bf16[192,768]{1,0:T(8,128)(2,1)} %refs_0_.1), channel_id=1, source_target_pairs={{0,4},{1,5},{2,6},{3,7},{4,8},{5,9},{6,10},{7,11},{8,12},{9,13},{1... | collective-permute-start | bytes 884744 | tf_op jit(solution)/shard_map/ppermute | solution.py:569
  5.2 6.7 %split_inputs.2 = (bf16[1024,1536]{1,0:T(8,128)(2,1)}, bf16[1024,1536]{1,0:T(8,128)(2,1)}) custom-call(s32[1]{0:T(128)} %bitcast.2.where, bf16[2048,3072]{1,0:T(8,128)(2,1)} %bitcast.46), custom_call_target="tpu_custom_call" | custom-call | tf_op jit(solution)/shard_map/split_inputs/pallas_call | solution.py:50
  11.9 2.3 %collective-permute-done.1.refs_4_ = bf16[192,768]{1,0:T(8,128)(2,1)S(1)} collective-permute-done((bf16[192,768]{1,0:T(8,128)(2,1)}, bf16[192,768]{1,0:T(8,128)(2,1)S(1)}, u32[]{:S(2)}, u32[]{:S(2)}) %collective-permute-start.1) | collective-permute-done | bytes 294944 | tf_op jit(solution)/shard_map/ppermute | solution.py:569
  15.3 6.8 %split_inputs.3 = (bf16[1024,1536]{1,0:T(8,128)(2,1)}, bf16[1024,1536]{1,0:T(8,128)(2,1)}) custom-call(s32[1]{0:T(128)} %bitcast.2.where, bf16[2048,3072]{1,0:T(8,128)(2,1)} %bitcast.47), custom_call_target="tpu_custom_call" | custom-call | tf_op jit(solution)/shard_map/split_inputs/pallas_call | solution.py:50
  23.7 2.0 %collective-permute-done.4.refs_0_ = bf16[192,768]{1,0:T(8,128)(2,1)S(1)} collective-permute-done((bf16[192,768]{1,0:T(8,128)(2,1)S(1)}, bf16[192,768]{1,0:T(8,128)(2,1)S(1)}, u32[]{:S(2)}, u32[]{:S(2)}) %collective-permute-start.4) | collective-permute-done | bytes 294944 | tf_op jit(solution)/shard_map/ppermute | solution.py:569
  31.2 9.0 %section_forward.3 = (f32[2048,768]{1,0:T(8,128)}, f32[8,128]{1,0:T(8,128)S(1)}) custom-call(s32[12]{0:T(128)S(1)} %stack.130.where, f32[8,128]{1,0:T(8,128)S(1)} %broadcast_in_dim.40.token, bf16[2048,3072]{1,0:T(8,128)(2,1)} %bitcast.48, bf16[192,768]{1,0:T(8,128)(2,1)S(1)} %copy-done.3, ...), custom_call_target="tpu_custom_call", output_to_operand_aliasing={{1}: (1, {})} | custom-call | flops 4831838208 | bytes 6291456 | tf_op jit(solution)/shard_map/section_forward/pallas_call | solution.py:162
  42.8 9.2 %section_forward.4 = (f32[2048,768]{1,0:T(8,128)}, f32[8,128]{1,0:T(8,128)S(1)}) custom-call(s32[9]{0:T(128)S(1)} %stack.134.where, f32[8,128]{1,0:T(8,128)S(1)} %get-tuple-element.114.token, bf16[2048,3072]{1,0:T(8,128)(2,1)} %bitcast.49, bf16[192,768]{1,0:T(8,128)(2,1)S(1)} %collective-permute-done.4.refs_0_, ...), custom_call_target="tpu_custom_call", output_to_operand_aliasing={{0}: (9, {}), {1}: (1, {})} | custom-call | flops 3623878656 | bytes 4718592 | tf_op jit(solution)/shard_map/section_forward/pallas_call | solution.py:162
  53.7 6.3 %section_forward.5 = (bf16[2048,768]{1,0:T(8,128)(2,1)}, f32[32,768]{1,0:T(8,128)S(1)}, f32[8,128]{1,0:T(8,128)S(1)}) custom-call(s32[3]{0:T(128)S(1)} %pad_add_fusion.where, f32[8,128]{1,0:T(8,128)S(1)} %get-tuple-element.119.token, bf16[2048,3072]{1,0:T(8,128)(2,1)} %bitcast.50, ...), custom_call_target="tpu_custom_call", output_to_operand_aliasing={{2}: (1, {})} | custom-call | flops 1207959552 | bytes 1572864 | tf_op jit(solution)/shard_map/section_forward/pallas_call | solution.py:162
  62.8 3.0 %collective-permute-done.18 = f32[8,128]{1,0:T(8,128)S(1)} collective-permute-done((f32[8,128]{1,0:T(8,128)S(1)}, f32[8,128]{1,0:T(8,128)S(1)}, u32[]{:S(2)}, u32[]{:S(2)}) %collective-permute-start.18) | collective-permute-done | bytes 4128 | tf_op jit(solution)/shard_map/ppermute | solution.py:569
  66.7 3.6 %collective-permute-start.21 = (f32[8,128]{1,0:T(8,128)S(1)}, f32[8,128]{1,0:T(8,128)S(1)}, u32[]{:S(2)}, u32[]{:S(2)}) collective-permute-start(f32[8,128]{1,0:T(8,128)S(1)} %add_select_fusion.refs_2_), channel_id=1, source_target_pairs={{0,4},{1,5},{2,6},{3,7},{4,8},{5,9},{6,10},{7,11},{8,12},{9,13},{1... | collective-permute-start | bytes 12296 | tf_op jit(solution)/shard_map/ppermute | solution.py:569
  72.2 1.8 %collective-permute-done.22.refs_5_ = f32[8,128]{1,0:T(8,128)S(1)} collective-permute-done((f32[8,128]{1,0:T(8,128)S(1)}, f32[8,128]{1,0:T(8,128)S(1)}, u32[]{:S(2)}, u32[]{:S(2)}) %collective-permute-start.22) | collective-permute-done | bytes 4128 | tf_op jit(solution)/shard_map/ppermute | solution.py:569
  74.0 4.2 %head_grads.1 = (bf16[4096,768]{1,0:T(8,128)(2,1)S(1)}, f32[208,768]{1,0:T(8,128)S(1)}, bf16[208,768]{1,0:T(8,128)(2,1)S(1)}, f32[8,128]{1,0:T(8,128)S(1)}, f32[8,128]{1,0:T(8,128)S(1)}) custom-call(s32[3]{0:T(128)S(1)} %get-tuple-element.191.where, bf16[2048,768]{1,0:T(8,128)(2,1)} %get-tuple-element.127.refs_0_, ...), custom_call_target="tpu_custom_call" | custom-call | tf_op jit(solution)/shard_map/head_grads/pallas_call | solution.py:454
  79.0 5.3 %section_backward.4 = (f32[192,768]{1,0:T(8,128)S(1)}, bf16[192,768]{1,0:T(8,128)(2,1)S(1)}, f32[8,128]{1,0:T(8,128)S(1)}) custom-call(s32[3]{0:T(128)S(1)} %get-tuple-element.190.where, f32[8,128]{1,0:T(8,128)S(1)} %get-tuple-element.133.token, bf16[4096,768]{1,0:T(8,128)(2,1)S(1)} %get-tuple-element.134.d_pre, ...), custom_call_target="tpu_custom_call", output_to_operand_aliasing={{2}: (1, {})} | custom-call | flops 2415919104 | bytes 3145728 | tf_op jit(solution)/shard_map/section_backward/pallas_call | solution.py:510
  84.3 1.8 %collective-permute-done.25.got = bf16[208,768]{1,0:T(8,128)(2,1)S(1)} collective-permute-done((bf16[208,768]{1,0:T(8,128)(2,1)S(1)}, bf16[208,768]{1,0:T(8,128)(2,1)S(1)}, u32[]{:S(2)}, u32[]{:S(2)}) %collective-permute-start.25) | collective-permute-done | bytes 319520 | tf_op jit(solution)/shard_map/ppermute | solution.py:569
  86.8 5.2 %section_backward.5 = (f32[192,768]{1,0:T(8,128)S(1)}, bf16[192,768]{1,0:T(8,128)(2,1)S(1)}, f32[8,128]{1,0:T(8,128)S(1)}) custom-call(s32[3]{0:T(128)S(1)} %get-tuple-element.189.where, f32[8,128]{1,0:T(8,128)S(1)} %get-tuple-element.142.token, bf16[4096,768]{1,0:T(8,128)(2,1)S(1)} %get-tuple-element.134.d_pre, ...), custom_call_target="tpu_custom_call", output_to_operand_aliasing={{2}: (1, {})} | custom-call | flops 2415919104 | bytes 3145728 | tf_op jit(solution)/shard_map/section_backward/pallas_call | solution.py:510
  93.8 2.4 %collective-permute-start.31 = (bf16[192,768]{1,0:T(8,128)(2,1)S(1)}, bf16[192,768]{1,0:T(8,128)(2,1)S(1)}, u32[]{:S(2)}, u32[]{:S(2)}) collective-permute-start(bf16[192,768]{1,0:T(8,128)(2,1)S(1)} %add_convert_fusion.1), channel_id=1, source_target_pairs={{0,4},{1,5},{2,6},{3,7},{4,0},{5,1},{6,2},{7,3},{8,12},{9,13},{10,... | collective-permute-start | bytes 884744 | tf_op jit(solution)/shard_map/ppermute | solution.py:569
  97.4 2.3 %collective-permute-start.28 = (bf16[64,768]{1,0:T(8,128)(2,1)S(1)}, bf16[64,768]{1,0:T(8,128)(2,1)S(1)}, u32[]{:S(2)}, u32[]{:S(2)}) collective-permute-start(bf16[64,768]{1,0:T(8,128)(2,1)S(1)} %get-tuple-element.156), channel_id=1, source_target_pairs={{0,8},{1,9},{2,10},{3,11},{4,12},{5,13},{6,14},{7,15},{8,0},{9,1},... | collective-permute-start | bytes 294920 | tf_op jit(solution)/shard_map/ppermute | solution.py:569
  99.8 3.8 %collective-permute-start.30 = (bf16[64,768]{1,0:T(8,128)(2,1)S(1)}, bf16[64,768]{1,0:T(8,128)(2,1)S(1)}, u32[]{:S(2)}, u32[]{:S(2)}) collective-permute-start(bf16[64,768]{1,0:T(8,128)(2,1)S(1)} %get-tuple-element.158), channel_id=1, source_target_pairs={{0,12},{1,13},{2,14},{3,15},{4,0},{5,1},{6,2},{7,3},{8,4},{9,5},{1... | collective-permute-start | bytes 294920 | tf_op jit(solution)/shard_map/ppermute | solution.py:569
  103.6 5.2 %section_backward.6 = (f32[192,768]{1,0:T(8,128)S(1)}, bf16[192,768]{1,0:T(8,128)(2,1)S(1)}, f32[8,128]{1,0:T(8,128)S(1)}) custom-call(s32[3]{0:T(128)S(1)} %get-tuple-element.192.where, f32[8,128]{1,0:T(8,128)S(1)} %get-tuple-element.150.token, bf16[4096,768]{1,0:T(8,128)(2,1)S(1)} %get-tuple-element.134.d_pre, ...), custom_call_target="tpu_custom_call", output_to_operand_aliasing={{2}: (1, {})} | custom-call | flops 2415919104 | bytes 3145728 | tf_op jit(solution)/shard_map/section_backward/pallas_call | solution.py:510
  110.0 2.0 %collective-permute-start.33 = (bf16[64,768]{1,0:T(8,128)(2,1)S(1)}, bf16[64,768]{1,0:T(8,128)(2,1)S(1)}, u32[]{:S(2)}, u32[]{:S(2)}) collective-permute-start(bf16[64,768]{1,0:T(8,128)(2,1)S(1)} %add_convert_fusion.3), channel_id=1, source_target_pairs={{0,8},{1,9},{2,10},{3,11},{4,12},{5,13},{6,14},{7,15},{8,0},{9,1},... | collective-permute-start | bytes 294920 | tf_op jit(solution)/shard_map/ppermute | solution.py:569
  112.0 5.2 %section_backward.7 = (f32[192,768]{1,0:T(8,128)S(1)}, bf16[192,768]{1,0:T(8,128)(2,1)S(1)}, f32[8,128]{1,0:T(8,128)S(1)}) custom-call(s32[3]{0:T(128)S(1)} %add_add_fusion.where, f32[8,128]{1,0:T(8,128)S(1)} %get-tuple-element.162.token, bf16[4096,768]{1,0:T(8,128)(2,1)S(1)} %get-tuple-element.134.d_pre, ...), custom_call_target="tpu_custom_call", output_to_operand_aliasing={{2}: (1, {})} | custom-call | flops 2415919104 | bytes 3145728 | tf_op jit(solution)/shard_map/section_backward/pallas_call | solution.py:510
  117.2 4.1 %collective-permute-done.33 = bf16[64,768]{1,0:T(8,128)(2,1)S(1)} collective-permute-done((bf16[64,768]{1,0:T(8,128)(2,1)S(1)}, bf16[64,768]{1,0:T(8,128)(2,1)S(1)}, u32[]{:S(2)}, u32[]{:S(2)}) %collective-permute-start.33) | collective-permute-done | bytes 98336 | tf_op jit(solution)/shard_map/ppermute | solution.py:569
  124.4 4.9 %collective-permute-done.35 = bf16[192,768]{1,0:T(8,128)(2,1)S(1)} collective-permute-done((bf16[192,768]{1,0:T(8,128)(2,1)S(1)}, bf16[192,768]{1,0:T(8,128)(2,1)S(1)}, u32[]{:S(2)}, u32[]{:S(2)}) %collective-permute-start.35) | collective-permute-done | bytes 294944 | tf_op jit(solution)/shard_map/ppermute | solution.py:569
  (109 shorter events, 27.8 us)
Async XLA Ops:
  0.6 11.3 %collective-permute-start = (bf16[192,768]{1,0:T(8,128)(2,1)}, bf16[192,768]{1,0:T(8,128)(2,1)S(1)}, u32[]{:S(2)}, u32[]{:S(2)}) collective-permute-start(bf16[192,768]{1,0:T(8,128)(2,1)} %refs_0_.1), channel_id=1, source_target_pairs={{0,2},{1,3},{2,0},{3,1},{4,6},{5,7},{6,4},{7,5},{8,10},{9,11},{10,... | collective-permute-start | bytes 884744 | tf_op jit(solution)/shard_map/ppermute | solution.py:569
  3.7 10.6 %collective-permute-start.1 = (bf16[192,768]{1,0:T(8,128)(2,1)}, bf16[192,768]{1,0:T(8,128)(2,1)S(1)}, u32[]{:S(2)}, u32[]{:S(2)}) collective-permute-start(bf16[192,768]{1,0:T(8,128)(2,1)} %refs_0_.1), channel_id=1, source_target_pairs={{0,4},{1,5},{2,6},{3,7},{4,8},{5,9},{6,10},{7,11},{8,12},{9,13},{1... | collective-permute-start | bytes 884744 | tf_op jit(solution)/shard_map/ppermute | solution.py:569
  5.2 9.0 %collective-permute-start.2 = (bf16[192,768]{1,0:T(8,128)(2,1)}, bf16[192,768]{1,0:T(8,128)(2,1)S(1)}, u32[]{:S(2)}, u32[]{:S(2)}) collective-permute-start(bf16[192,768]{1,0:T(8,128)(2,1)} %refs_0_.1), channel_id=1, source_target_pairs={{0,1},{1,0},{2,3},{3,2},{4,5},{5,4},{6,7},{7,6},{8,9},{9,8},{10,11... | collective-permute-start | bytes 884744 | tf_op jit(solution)/shard_map/ppermute | solution.py:569
  14.2 11.5 %collective-permute-start.6 = (bf16[1024,1536]{1,0:T(8,128)(2,1)}, bf16[1024,1536]{1,0:T(8,128)(2,1)S(1)}, u32[]{:S(2)}, u32[]{:S(2)}) collective-permute-start(bf16[1024,1536]{1,0:T(8,128)(2,1)} %get-tuple-element.101), channel_id=1, source_target_pairs={{0,1},{1,0},{2,3},{3,2},{4,5},{5,4},{6,7},{7,6},{8,9},{9,8},{10,11... | collective-permute-start | bytes 9437192 | tf_op jit(solution)/shard_map/ppermute | solution.py:569
  14.2 9.4 %collective-permute-start.3 = (bf16[192,768]{1,0:T(8,128)(2,1)S(1)}, bf16[192,768]{1,0:T(8,128)(2,1)S(1)}, u32[]{:S(2)}, u32[]{:S(2)}) collective-permute-start(bf16[192,768]{1,0:T(8,128)(2,1)S(1)} %collective-permute-done.1.refs_4_), channel_id=1, source_target_pairs={{0,2},{1,3},{2,0},{3,1},{4,6},{5,7},{6,4},{7,5},{8,10},{9,11},{10,... | collective-permute-start | bytes 884744 | tf_op jit(solution)/shard_map/ppermute | solution.py:569
  14.8 10.9 %collective-permute-start.4 = (bf16[192,768]{1,0:T(8,128)(2,1)S(1)}, bf16[192,768]{1,0:T(8,128)(2,1)S(1)}, u32[]{:S(2)}, u32[]{:S(2)}) collective-permute-start(bf16[192,768]{1,0:T(8,128)(2,1)S(1)} %collective-permute-done.1.refs_4_), channel_id=1, source_target_pairs={{0,4},{1,5},{2,6},{3,7},{4,8},{5,9},{6,10},{7,11},{8,12},{9,13},{1... | collective-permute-start | bytes 884744 | tf_op jit(solution)/shard_map/ppermute | solution.py:569
  14.8 10.9 %collective-permute-start.5 = (bf16[192,768]{1,0:T(8,128)(2,1)S(1)}, bf16[192,768]{1,0:T(8,128)(2,1)S(1)}, u32[]{:S(2)}, u32[]{:S(2)}) collective-permute-start(bf16[192,768]{1,0:T(8,128)(2,1)S(1)} %collective-permute-done.1.refs_4_), channel_id=1, source_target_pairs={{0,1},{1,0},{2,3},{3,2},{4,5},{5,4},{6,7},{7,6},{8,9},{9,8},{10,11... | collective-permute-start | bytes 884744 | tf_op jit(solution)/shard_map/ppermute | solution.py:569
  15.0 10.7 %collective-permute-start.7 = (bf16[192,768]{1,0:T(8,128)(2,1)S(1)}, bf16[192,768]{1,0:T(8,128)(2,1)S(1)}, u32[]{:S(2)}, u32[]{:S(2)}) collective-permute-start(bf16[192,768]{1,0:T(8,128)(2,1)S(1)} %collective-permute-done.refs_2_), channel_id=1, source_target_pairs={{0,1},{1,0},{2,3},{3,2},{4,5},{5,4},{6,7},{7,6},{8,9},{9,8},{10,11... | collective-permute-start | bytes 884744 | tf_op jit(solution)/shard_map/ppermute | solution.py:569
  28.1 12.8 %collective-permute-start.12 = (bf16[1024,1536]{1,0:T(8,128)(2,1)}, bf16[1024,1536]{1,0:T(8,128)(2,1)}, u32[]{:S(2)}, u32[]{:S(2)}) collective-permute-start(bf16[1024,1536]{1,0:T(8,128)(2,1)} %get-tuple-element.112), channel_id=1, source_target_pairs={{0,1},{1,0},{2,3},{3,2},{4,5},{5,4},{6,7},{7,6},{8,9},{9,8},{10,11... | collective-permute-start | bytes 9437192 | tf_op jit(solution)/shard_map/ppermute | solution.py:569
  28.3 11.9 %collective-permute-start.10 = (bf16[192,768]{1,0:T(8,128)(2,1)S(1)}, bf16[192,768]{1,0:T(8,128)(2,1)S(1)}, u32[]{:S(2)}, u32[]{:S(2)}) collective-permute-start(bf16[192,768]{1,0:T(8,128)(2,1)S(1)} %collective-permute-done.4.refs_0_), channel_id=1, source_target_pairs={{0,1},{1,0},{2,3},{3,2},{4,5},{5,4},{6,7},{7,6},{8,9},{9,8},{10,11... | collective-permute-start | bytes 884744 | tf_op jit(solution)/shard_map/ppermute | solution.py:569
  28.7 11.5 %collective-permute-start.8 = (bf16[192,768]{1,0:T(8,128)(2,1)S(1)}, bf16[192,768]{1,0:T(8,128)(2,1)S(1)}, u32[]{:S(2)}, u32[]{:S(2)}) collective-permute-start(bf16[192,768]{1,0:T(8,128)(2,1)S(1)} %collective-permute-done.4.refs_0_), channel_id=1, source_target_pairs={{0,2},{1,3},{2,0},{3,1},{4,6},{5,7},{6,4},{7,5},{8,10},{9,11},{10,... | collective-permute-start | bytes 884744 | tf_op jit(solution)/shard_map/ppermute | solution.py:569
  30.3 10.6 %collective-permute-start.9 = (bf16[192,768]{1,0:T(8,128)(2,1)S(1)}, bf16[192,768]{1,0:T(8,128)(2,1)S(1)}, u32[]{:S(2)}, u32[]{:S(2)}) collective-permute-start(bf16[192,768]{1,0:T(8,128)(2,1)S(1)} %collective-permute-done.4.refs_0_), channel_id=1, source_target_pairs={{0,4},{1,5},{2,6},{3,7},{4,8},{5,9},{6,10},{7,11},{8,12},{9,13},{1... | collective-permute-start | bytes 884744 | tf_op jit(solution)/shard_map/ppermute | solution.py:569
  41.4 10.6 %collective-permute-start.13 = (bf16[192,768]{1,0:T(8,128)(2,1)S(1)}, bf16[192,768]{1,0:T(8,128)(2,1)S(1)}, u32[]{:S(2)}, u32[]{:S(2)}) collective-permute-start(bf16[192,768]{1,0:T(8,128)(2,1)S(1)} %collective-permute-done.9.refs_4_), channel_id=1, source_target_pairs={{0,2},{1,3},{2,0},{3,1},{4,6},{5,7},{6,4},{7,5},{8,10},{9,11},{10,... | collective-permute-start | bytes 884744 | tf_op jit(solution)/shard_map/ppermute | solution.py:569
  65.9 8.1 %collective-permute-start.19 = (bf16[2048,768]{1,0:T(8,128)(2,1)}, bf16[2048,768]{1,0:T(8,128)(2,1)}, u32[]{:S(2)}, u32[]{:S(2)}) collective-permute-start(bf16[2048,768]{1,0:T(8,128)(2,1)} %get-tuple-element.127.refs_0_), channel_id=1, source_target_pairs={{0,1},{1,0},{2,3},{3,2},{4,5},{5,4},{6,7},{7,6},{8,9},{9,8},{10,11... | collective-permute-start | bytes 9437192 | tf_op jit(solution)/shard_map/ppermute | solution.py:569
  65.9 8.1 %collective-permute-start.24 = (f32[32,2048]{1,0:T(8,128)S(1)}, f32[32,2048]{1,0:T(8,128)S(1)}, u32[]{:S(2)}, u32[]{:S(2)}) collective-permute-start(f32[32,2048]{1,0:T(8,128)S(1)} %get-tuple-element.130.refs_8_), channel_id=1, source_target_pairs={{0,1},{1,0},{2,3},{3,2},{4,5},{5,4},{6,7},{7,6},{8,9},{9,8},{10,11... | collective-permute-start | bytes 786440 | tf_op jit(solution)/shard_map/ppermute | solution.py:569
  78.2 7.9 %collective-permute-start.25 = (bf16[208,768]{1,0:T(8,128)(2,1)S(1)}, bf16[208,768]{1,0:T(8,128)(2,1)S(1)}, u32[]{:S(2)}, u32[]{:S(2)}) collective-permute-start(bf16[208,768]{1,0:T(8,128)(2,1)S(1)} %get-tuple-element.140), channel_id=1, source_target_pairs={{0,2},{1,3},{2,0},{3,1},{4,6},{5,7},{6,4},{7,5},{8,10},{9,11},{10,... | collective-permute-start | bytes 958472 | tf_op jit(solution)/shard_map/ppermute | solution.py:569
  92.0 16.9 %collective-permute-start.27 = (bf16[192,768]{1,0:T(8,128)(2,1)S(1)}, bf16[192,768]{1,0:T(8,128)(2,1)S(1)}, u32[]{:S(2)}, u32[]{:S(2)}) collective-permute-start(bf16[192,768]{1,0:T(8,128)(2,1)S(1)} %get-tuple-element.152), channel_id=1, source_target_pairs={{0,2},{1,3},{2,0},{3,1},{4,6},{5,7},{6,4},{7,5},{8,10},{9,11},{10,... | collective-permute-start | bytes 884744 | tf_op jit(solution)/shard_map/ppermute | solution.py:569
  93.8 15.1 %collective-permute-start.31 = (bf16[192,768]{1,0:T(8,128)(2,1)S(1)}, bf16[192,768]{1,0:T(8,128)(2,1)S(1)}, u32[]{:S(2)}, u32[]{:S(2)}) collective-permute-start(bf16[192,768]{1,0:T(8,128)(2,1)S(1)} %add_convert_fusion.1), channel_id=1, source_target_pairs={{0,4},{1,5},{2,6},{3,7},{4,0},{5,1},{6,2},{7,3},{8,12},{9,13},{10,... | collective-permute-start | bytes 884744 | tf_op jit(solution)/shard_map/ppermute | solution.py:569
  97.4 11.4 %collective-permute-start.28 = (bf16[64,768]{1,0:T(8,128)(2,1)S(1)}, bf16[64,768]{1,0:T(8,128)(2,1)S(1)}, u32[]{:S(2)}, u32[]{:S(2)}) collective-permute-start(bf16[64,768]{1,0:T(8,128)(2,1)S(1)} %get-tuple-element.156), channel_id=1, source_target_pairs={{0,8},{1,9},{2,10},{3,11},{4,12},{5,13},{6,14},{7,15},{8,0},{9,1},... | collective-permute-start | bytes 294920 | tf_op jit(solution)/shard_map/ppermute | solution.py:569
  99.7 9.1 %collective-permute-start.29 = (bf16[64,768]{1,0:T(8,128)(2,1)S(1)}, bf16[64,768]{1,0:T(8,128)(2,1)S(1)}, u32[]{:S(2)}, u32[]{:S(2)}) collective-permute-start(bf16[64,768]{1,0:T(8,128)(2,1)S(1)} %get-tuple-element.157), channel_id=1, source_target_pairs={{0,4},{1,5},{2,6},{3,7},{4,8},{5,9},{6,10},{7,11},{8,12},{9,13},{1... | collective-permute-start | bytes 294920 | tf_op jit(solution)/shard_map/ppermute | solution.py:569
  99.8 9.1 %collective-permute-start.30 = (bf16[64,768]{1,0:T(8,128)(2,1)S(1)}, bf16[64,768]{1,0:T(8,128)(2,1)S(1)}, u32[]{:S(2)}, u32[]{:S(2)}) collective-permute-start(bf16[64,768]{1,0:T(8,128)(2,1)S(1)} %get-tuple-element.158), channel_id=1, source_target_pairs={{0,12},{1,13},{2,14},{3,15},{4,0},{5,1},{6,2},{7,3},{8,4},{9,5},{1... | collective-permute-start | bytes 294920 | tf_op jit(solution)/shard_map/ppermute | solution.py:569
  108.8 8.4 %collective-permute-start.32 = (bf16[192,768]{1,0:T(8,128)(2,1)S(1)}, bf16[192,768]{1,0:T(8,128)(2,1)S(1)}, u32[]{:S(2)}, u32[]{:S(2)}) collective-permute-start(bf16[192,768]{1,0:T(8,128)(2,1)S(1)} %get-tuple-element.165), channel_id=1, source_target_pairs={{0,2},{1,3},{2,0},{3,1},{4,6},{5,7},{6,4},{7,5},{8,10},{9,11},{10,... | collective-permute-start | bytes 884744 | tf_op jit(solution)/shard_map/ppermute | solution.py:569
  109.0 13.5 %collective-permute-start.36 = (bf16[128,768]{1,0:T(8,128)(2,1)S(1)}, bf16[128,768]{1,0:T(8,128)(2,1)S(1)}, u32[]{:S(2)}, u32[]{:S(2)}) collective-permute-start(bf16[128,768]{1,0:T(8,128)(2,1)S(1)} %add_convert_fusion.2), channel_id=1, source_target_pairs={{0,8},{1,9},{2,10},{3,11},{4,12},{5,13},{6,14},{7,15},{8,0},{9,1},... | collective-permute-start | bytes 589832 | tf_op jit(solution)/shard_map/ppermute | solution.py:569
  110.0 11.3 %collective-permute-start.33 = (bf16[64,768]{1,0:T(8,128)(2,1)S(1)}, bf16[64,768]{1,0:T(8,128)(2,1)S(1)}, u32[]{:S(2)}, u32[]{:S(2)}) collective-permute-start(bf16[64,768]{1,0:T(8,128)(2,1)S(1)} %add_convert_fusion.3), channel_id=1, source_target_pairs={{0,8},{1,9},{2,10},{3,11},{4,12},{5,13},{6,14},{7,15},{8,0},{9,1},... | collective-permute-start | bytes 294920 | tf_op jit(solution)/shard_map/ppermute | solution.py:569
  (24 other events, 135.2 us)
